TPU v7x, 32 devices: a whole 2x2x4 slice. The times are simulated.
32 devices in a mesh: blk: 16 (over z, x, core), rel: 2 (over y).
Axes of the slice: x: 2, y: 2, z: 4, core: 2. Of those that a mesh axis runs over, the one named last changes fastest.
Arguments:
- left_slab: float32 [65536, 400], P(('blk', 'rel')), may hold values from -1.3 to 1.3
- left_state: float32 [65536], P(('blk', 'rel')), may hold values from 1e-05 to 0.0001
- right_slab: float32 [65536, 400], P(('blk', 'rel')), may hold values from -1.3 to 1.3
- right_state: float32 [65536], P(('blk', 'rel')), may hold values from 1e-05 to 0.0001
- relations: float32 [32, 400], replicated, may hold values from 0.1 to 1.9
- relation_state: float32 [32], replicated, may hold values from 0.01 to 0.2
- src_index: int32 [2, 8192], P(None, ('blk', 'rel')), may hold values from 0 to 2047
- dst_index: int32 [2, 8192], P(None, ('blk', 'rel')), may hold values from 0 to 2047
- relation_id: int32 [2, 8192], P(None, ('blk', 'rel')), may hold values from 0 to 31
- neg_source: int32 [2, 32000], P(None, ('blk', 'rel')), may hold values from 0 to 2047
- neg_target: int32 [2, 32000], P(None, ('blk', 'rel')), may hold values from 0 to 2047
Outputs:
- left_out: float32 [65536, 400], P(('blk', 'rel'))
- right_out: float32 [65536, 400], P(('blk', 'rel'))
- relations_out: float32 [16, 32, 400], P('blk')
All inputs are finite; a program needn't handle non-finite values.
Results may differ from a plain program's by a relative error of at most 0.00069.
Values sent between devices are 32-bit elements; how exact they have to be, the bound alone decides.
No kernel may reach another device: no remote copies, remote signals or barrier semaphores. Data moves between devices by JAX's collectives and lax.ppermute only.
A program may use at most 64 MiB of HBM per device.

v0:
```python
import functools

import jax
import jax.numpy as jnp
from jax import lax
from jax.experimental import pallas as pl
from jax.experimental.pallas import tpu as pltpu
from jax.sharding import PartitionSpec as P

rate = 0.1
F32 = jnp.float32
BF16 = jnp.bfloat16
LANES = 128
NEAR = (4, 4)
STATE = 0
NEAR_FIRST = (4, 4)
FAR = (5, 2, 1)
VMEM_LIMIT = 30 * 2**20

NN = (((1,), (0,)), ((), ()))
NT = (((1,), (1,)), ((), ()))
TN = (((0,), (0,)), ((), ()))


def mul(a, b, dims):
    return lax.dot_general(a, b, dims, preferred_element_type=F32)


def split(x, parts):
    out = []
    for _ in range(parts):
        part = x.astype(BF16)
        out.append(part)
        x = x - part.astype(F32)
    return out


def mul_parts(parts, table, dims):
    along = dims[0][1][0]
    return mul(jnp.concatenate(parts, axis=1), jnp.concatenate([table] * len(parts), axis=along), dims)


def lanes_at(i, size, start=0):
    if isinstance(i, int):
        return slice(start + i * size, start + (i + 1) * size)
    return pl.ds(pl.multiple_of(start + i * size, LANES), size)


def step_of(rows, most=512):
    return next(size for size in (1024, 512, 256) if size <= most and rows % size == 0)


def each(count, body, fixed=False):
    if fixed:
        for i in range(count):
            body(i)
        return

    def one(i, carry):
        body(i)
        return carry

    lax.fori_loop(0, count, one, 0)


def row_onehot(idx, table):
    count, rows = table.shape
    col = jnp.broadcast_to(idx, (LANES, count)).T
    lane = lax.broadcasted_iota(jnp.int32, (count, LANES), 1)

    def tile(t):
        hit = col == lane + t * LANES
        table[:, lanes_at(t, LANES)] = jnp.where(hit, 1.0, 0.0).astype(BF16)

    each(rows // LANES, tile)


def row_counts(idx, rows):
    count = idx.shape[1]
    high = lax.broadcasted_iota(jnp.int32, (rows // LANES, count), 0)
    low = lax.broadcasted_iota(jnp.int32, (LANES, count), 0)
    high_hit = jnp.where(idx // LANES == high, 1.0, 0.0).astype(BF16)
    low_hit = jnp.where(idx % LANES == low, 1.0, 0.0).astype(BF16)
    return mul(high_hit, low_hit, NT)


def times_at(counts, i, size, start=0):
    first = (start + i * size) // LANES
    return jnp.concatenate([counts[pl.ds(first + t, 1), :] for t in range(size // LANES)], axis=1)


def half_rows(x):
    return (0.5 * x).T.astype(BF16)


def negative_weights(rows16, query_rows, number):
    half = 0.5 / number
    return (jnp.tanh(mul(query_rows, rows16, NN)) * half + half).astype(BF16)


def often(weight, times):
    return (weight.astype(F32) * times).astype(BF16)


def negatives(rows16, query, query_rows, times, number):
    weight = negative_weights(rows16, query_rows, number)
    return mul(query, weight, NN) * times, mul(rows16, often(weight, times), NT)


def prepare(step, left, relations, src, dst, rid, nsrc, ndst,
            weight, source, query, query_rows, left16, oh_src, oh_dst, count_l, count_r, kind):
    rows = left.shape[1]
    here = slice(step, step + 1)
    row_onehot(src[here, :], oh_src)
    row_onehot(dst[here, :], oh_dst)
    count_l[...] = row_counts(nsrc[here, :], rows)
    count_r[...] = row_counts(ndst[here, :], rows)
    kinds = lax.broadcasted_iota(jnp.int32, kind.shape, 0)
    kind[...] = jnp.where(rid[here, :] == kinds, 1.0, 0.0).astype(BF16)
    weight[...] = sum(mul(part, kind[...], TN) for part in split(relations[...], 3))
    source[...] = jnp.zeros_like(source)

    size = step_of(rows)

    def part(i):
        cut = lanes_at(i, size)
        parts = split(left[:, cut], 3)
        left16[:, cut] = parts[0]
        source[...] += mul_parts(parts, oh_src[:, cut], NT)

    each(rows // size, part)
    product = source[...] * weight[...]
    query[...] = product.astype(BF16)
    query_rows[...] = half_rows(product.astype(BF16).astype(F32))


def take_piece(number, start, piece, query, query_rows, oh_dst, count_r, target, gq, rgrad, fixed=False):
    depth = target.shape[0]
    if start == 0:
        target[...] = jnp.zeros_like(target)
        gq[...] = jnp.zeros_like(gq)

    size = step_of(piece.shape[1], 256 if fixed else 512)

    def part(i):
        cut = lanes_at(i, size)
        parts = split(piece[0:depth, cut], 3)
        hits = oh_dst[:, lanes_at(i, size, start)]
        target[...] += mul_parts(parts, hits, NT)
        times = times_at(count_r, i, size, start)
        rgrad[:, cut], more = negatives(parts[0], query[...], query_rows[...], times, number)
        gq[...] += more

    each(piece.shape[1] // size, part, fixed)


def join(number, weight, source, target, gq, left16, count_l, kind, rel_in,
         probe, probe_rows, gp, lgrad, to_src, to_dst, rel_out, fixed=False):
    rows = left16.shape[1]
    product = weight[...] * target[...]
    probe[...] = product.astype(BF16)
    probe_rows[...] = half_rows(product.astype(BF16).astype(F32))
    gp[...] = jnp.zeros_like(gp)

    size = step_of(rows)

    def part(i):
        cut = lanes_at(i, size)
        lgrad[:, cut], more = negatives(left16[:, cut], probe[...], probe_rows[...], times_at(count_l, i, size), number)
        gp[...] += more

    each(rows // size, part, fixed)
    depth = weight.shape[0]
    w, s, t = weight[...], source[...], target[...]
    coef = -jax.nn.sigmoid(-jnp.sum(s * w * t, axis=0, keepdims=True))
    to_src[0:depth, :], to_src[depth:, :] = split(coef * w * t + gq[...] * w, 2)
    to_dst[0:depth, :], to_dst[depth:, :] = split(coef * w * s + gp[...] * w, 2)
    g_weight = coef * s * t + gq[...] * s + gp[...] * t
    rel_out[...] = rel_in[...] + sum(mul(kind[...], p, NT) for p in split(g_weight, 2))


def adagrad(slab, state, grad, edges, table, start, out, new_state, send=None, fixed=False, more=None):
    depth = grad.shape[0]
    size = step_of(grad.shape[1])

    def part(i):
        cut = lanes_at(i, size)
        hits = table[:, lanes_at(i, size, start)]
        g = grad[:, cut] + mul_parts([edges[0:depth, :], edges[depth:, :]], hits, NN)
        if more is not None:
            g = g + more(i, size)
        new = state[:, cut] + jnp.sum(g * g, axis=0, keepdims=True) * (1.0 / depth)
        new_state[:, cut] = new
        out[0:depth, cut] = slab[0:depth, cut] - g * (rate * lax.rsqrt(new))
        if send is not None:
            send(i).start()

    each(grad.shape[1] // size, part, fixed)


def sender(result, to, start, sems):
    size = step_of(result.shape[1])

    def copy(i):
        here = lanes_at(i, size)
        there = lanes_at(i, size, start)
        return pltpu.make_async_copy(result.at[:, here], to.at[:, there], sems.at[i + start // 256])

    return copy


def update_and_send(pieces, state, grads, edges, table, new_state, to, sems, fixed=False, start=0, more=None):
    sent = []
    for piece, grad in zip(pieces, grads):
        rows = grad.shape[1]
        copy = sender(grad, to, start, sems)
        cut = slice(start, start + rows)
        adagrad(piece, state.at[:, cut], grad, edges, table, start, grad, new_state.at[:, cut], copy, fixed, more)
        sent.append((copy, rows // step_of(rows)))
        start += rows

    def wait():
        for copy, count in sent:
            each(count, lambda i, copy=copy: copy(i).wait(), fixed)

    return wait


def pack_state(state, piece, depth):
    size = state.shape[1] // 8
    for k in range(8):
        piece[depth + k : depth + k + 1, 0:size] = state[:, k * size : (k + 1) * size]


def unpack_state(piece, depth, state):
    size = state.shape[1] // 8
    for k in range(8):
        state[:, k * size : (k + 1) * size] = piece[depth + k : depth + k + 1, 0:size]


def on_parity(parity):
    return pl.when(lax.axis_index("blk") % 2 == parity)


def pieces_of(rows, eighths):
    sizes = [rows // 8 * n for n in eighths]
    return [(sum(sizes[:i]), size) for i, size in enumerate(sizes)]


def rows_of(pieces, at, size):
    found = []
    start = 0
    for piece in pieces:
        begin, end = max(at, start), min(at + size, start + piece.shape[1])
        if begin < end:
            found.append((piece.at[:, begin - start : end - start], begin, end - begin))
        start += piece.shape[1]
    return found


def train(parity, number, last, fixed, kept, takes, gives, *refs):
    refs = list(refs)
    (left, lstate, rstate_in, rel_in) = refs[:4]
    (weight, source, query, query_rows, left16, oh_src, oh_dst, count_l, count_r, kind) = refs[4:14]
    right = refs[14 : 14 + takes]
    refs = refs[14 + takes + kept :]
    left_out, lstate_out, rel_out = refs[:3]
    right_out = refs[3 : 3 + len(gives)]
    (target, gq, rgrad, probe, probe_rows, gp, lgrad, to_src, to_dst, rstate, spare, sems) = refs[3 + len(gives) :]
    depth, rows = left.shape
    lstate_out[...] = lstate[...]
    rel_out[...] = rel_in[...]

    @on_parity(parity)
    def _():
        grads = []
        at = 0
        for piece in right:
            grads.append(rgrad.at[:, at : at + piece.shape[1]])
            take_piece(number, at, piece, query, query_rows, oh_dst, count_r, target, gq, grads[-1], fixed)
            at += piece.shape[1]
        join(number, weight, source, target, gq, left16, count_l, kind, rel_in,
             probe, probe_rows, gp, lgrad, to_src, to_dst, rel_out, fixed)
        if last:
            unpack_state(right[STATE], depth, rstate)
            wait_right = update_and_send(right, rstate, grads, to_dst, oh_dst, spare, right_out[0], sems.at[0], fixed)
            wait_left = update_and_send([left], lstate, [lgrad], to_src, oh_src, spare, left_out, sems.at[1], fixed)
            wait_right()
            wait_left()
        else:
            for (at, size), out in zip(pieces_of(rows, gives), right_out):
                for old, begin, length in rows_of(right, at, size):
                    cut = slice(begin, begin + length)
                    here = slice(begin - at, begin - at + length)
                    adagrad(old, rstate_in.at[:, cut], rgrad.at[:, cut], to_dst, oh_dst, begin, out.at[:, here], spare.at[:, cut], None, fixed)
            pack_state(spare, right_out[STATE], depth)
            adagrad(left, lstate, lgrad, to_src, oh_src, 0, left_out, lstate_out, None, fixed)


def shape(*dims, dtype=F32):
    return jax.ShapeDtypeStruct(dims, dtype)


def prepared_shapes(depth, rows, edges, kinds):
    return (
        shape(depth, edges), shape(depth, edges), shape(depth, edges, dtype=BF16), shape(edges, depth, dtype=BF16),
        shape(depth, rows, dtype=BF16), shape(edges, rows, dtype=BF16), shape(edges, rows, dtype=BF16),
        shape(rows // LANES, LANES), shape(rows // LANES, LANES), shape(kinds, edges, dtype=BF16),
    )


def scratch(shapes):
    return [pltpu.VMEM(s.shape, s.dtype) for s in shapes]


def call(kernel, name, operands, shapes, in_large=(), out_large=(), scratch_shapes=(), aliases=None):
    vmem = pl.BlockSpec(memory_space=pltpu.VMEM)
    large = pl.BlockSpec(memory_space=pl.ANY)
    return pl.pallas_call(
        kernel,
        out_shape=tuple(shapes),
        in_specs=[large if i in in_large else vmem for i in range(len(operands))],
        out_specs=tuple(large if i in out_large else vmem for i in range(len(shapes))),
        scratch_shapes=list(scratch_shapes),
        input_output_aliases=aliases or {},
        compiler_params=pltpu.CompilerParams(vmem_limit_bytes=VMEM_LIMIT),
        cost_estimate=pl.CostEstimate(flops=1_000_000, bytes_accessed=100_000, transcendentals=0),
        name=name,
    )(*operands)


def prepared(step, left, relations, index):
    depth, rows = left.shape
    return call(
        functools.partial(prepare, step), "prepare%d" % step, [left, relations, *index],
        prepared_shapes(depth, rows, index[0].shape[1], relations.shape[0]),
    )


def trained(parity, name, number, fixed, gives, left, lstate, right, rstate, rel, ready, keep=()):
    depth, rows = left.shape
    edges = ready[0].shape[1]
    last = not gives
    blocks = [shape(depth, size) for _at, size in pieces_of(rows, gives or (8,))]
    if not last:
        blocks[STATE] = shape(depth + 8, blocks[STATE].shape[1])
    edge = shape(depth, edges)
    edge16 = shape(depth, edges, dtype=BF16)
    pair16 = shape(2 * depth, edges, dtype=BF16)
    slab = shape(depth, rows)
    inner = [edge, edge, slab, edge16, shape(edges, depth, dtype=BF16), edge, slab, pair16, pair16, shape(1, rows), shape(1, rows)]
    left_out, lstate_out, rel_out, *right_out = call(
        functools.partial(train, parity, number, last, fixed, len(keep), len(right), gives or (8,)),
        name,
        [left, lstate, rstate, rel, *ready, *right, *keep],
        [slab, shape(1, rows), shape(*rel.shape), *blocks],
        out_large=(0, 3) if last else (),
        scratch_shapes=[*scratch(inner), pltpu.SemaphoreType.DMA((2, rows // 256))],
        aliases={14 + len(right) + i: 0 for i in range(len(keep))},
    )
    return left_out, lstate_out, right_out, rel_out


def only_on(parity, body):
    def kernel(*refs):
        @on_parity(parity)
        def _():
            body(*refs)

    return kernel


def last_piece(parity, name, number, at, piece, ready, after, held=()):
    (_weight, _source, query, query_rows, _left16, _oh_src, oh_dst, _count_l, count_r, _kind) = ready
    depth, edges = query.shape

    def body(piece, query, query_rows, oh_dst, count_r, *rest):
        take_piece(number, at, piece, query, query_rows, oh_dst, count_r, *rest[len(held) + 1 :], fixed=True)

    operands = [piece, query, query_rows, oh_dst, count_r, *held, after]
    return call(
        only_on(parity, body), name, operands,
        [shape(depth, edges), shape(depth, edges), shape(depth, piece.shape[1])],
        aliases={5: 0, 6: 1} if held else {},
    )


def source_scores(number, probe, probe_rows, left16, count_l, gp, weights=None):
    rows = left16.shape[1]
    size = step_of(rows, 1024)
    gp[...] = jnp.zeros_like(gp)
    for i in range(rows // size):
        cut = lanes_at(i, size)
        rows16 = left16[:, cut]
        part = negative_weights(rows16, probe_rows[...], number)
        if weights is not None:
            weights[:, cut] = part
        gp[...] += mul(rows16, often(part, times_at(count_l, i, size)), NT)


def early_edges(parity, name, number, step, low, high, target, ready, dst):
    (weight, source, _query, _query_rows, left16, _oh_src, _oh_dst, count_l, _count_r, _kind) = ready
    depth = left16.shape[0]
    edges = weight.shape[1]

    def body(weight, source, target, left16, count_l, dst, to_dst, gp, probe, probe_rows):
        w, s, t = weight[...], source[...], target[...]
        product = (w * t).astype(BF16)
        probe[...] = product
        probe_rows[...] = half_rows(product.astype(F32))
        source_scores(number, probe, probe_rows, left16, count_l, gp)
        at = dst[step : step + 1, :]
        here = jnp.logical_and(at >= low, at < high)
        coef = -jax.nn.sigmoid(-jnp.sum(s * w * t, axis=0, keepdims=True))
        to_dst[0:depth, :], to_dst[depth:, :] = split(jnp.where(here, coef * w * s + gp[...] * w, 0.0), 2)

    return call(
        only_on(parity, body), name, [weight, source, target, left16, count_l, dst],
        [shape(2 * depth, edges, dtype=BF16)],
        scratch_shapes=scratch([shape(depth, edges), shape(depth, edges, dtype=BF16), shape(edges, depth, dtype=BF16)]),
    )[0]


def early_right(parity, name, at, piece, state, rgrad, to_dst, oh_dst, keep):
    depth, rows = keep.shape

    def body(piece, rgrad, to_dst, oh_dst, *rest):
        out, new_state, spare, sems = rest[-4:]
        if state is None:
            unpack_state(piece, depth, new_state)
        else:
            new_state[...] = rest[0][...]
        update_and_send([piece], new_state, [rgrad], to_dst, oh_dst, spare, out, sems, fixed=True, start=at)()

    operands = [piece, rgrad, to_dst, oh_dst, *([] if state is None else [state]), keep]
    place = len(operands) - 1
    return call(
        only_on(parity, body), name, operands, [shape(depth, rows), shape(1, rows)],
        in_large=(place,), out_large=(0,),
        scratch_shapes=[*scratch([shape(1, rows)]), pltpu.SemaphoreType.DMA((rows // 256,))],
        aliases={place: 0},
    )


def late_edges(parity, number, step, at, piece, ready, dst, target, gq, rel, after):
    (weight, source, query, query_rows, left16, _oh_src, oh_dst, count_l, count_r, kind) = ready
    depth, rows = left16.shape
    edges = weight.shape[1]
    pair16 = shape(2 * depth, edges, dtype=BF16)

    def body(piece, weight, source, query, query_rows, left16, oh_dst, count_l, count_r, kind, dst, held_t, held_q, rel_in,
             _after, rgrad, to_src, to_dst, rel_out, probe, weights, gp, probe_rows):
        rel_out[...] = rel_in[...]

        @on_parity(parity)
        def _():
            size = piece.shape[1]
            parts = split(piece[...], 3)
            w, s = weight[...], source[...]
            t = held_t[...] + mul_parts(parts, oh_dst[:, at : at + size], NT)
            product = (w * t).astype(BF16)
            probe[...] = product
            probe_rows[...] = half_rows(product.astype(F32))
            source_scores(number, probe, probe_rows, left16, count_l, gp, weights)
            rgrad[...], more = negatives(parts[0], query[...], query_rows[...], times_at(count_r, 0, size, at), number)
            q = held_q[...] + more
            p = gp[...]
            coef = -jax.nn.sigmoid(-jnp.sum(s * w * t, axis=0, keepdims=True))
            g_weight = coef * s * t + q * s + p * t
            rel_out[...] = rel_in[...] + sum(mul(kind[...], part, NT) for part in split(g_weight, 2))
            to_src[0:depth, :], to_src[depth:, :] = split(coef * w * t + q * w, 2)
            here = dst[step : step + 1, :] >= at
            to_dst[0:depth, :], to_dst[depth:, :] = split(jnp.where(here, coef * w * s + p * w, 0.0), 2)

    return call(
        body, "late_edges",
        [piece, weight, source, query, query_rows, left16, oh_dst, count_l, count_r, kind, dst, target, gq, rel, after],
        [shape(depth, piece.shape[1]), pair16, pair16, shape(*rel.shape), shape(depth, edges, dtype=BF16), shape(edges, rows, dtype=BF16)],
        scratch_shapes=scratch([shape(depth, edges), shape(edges, depth, dtype=BF16)]),
    )


def left_rows(cut, left, lstate, to_src, oh_src, probe, weights, count_l):
    depth = left.shape[0]
    size = cut.stop - cut.start
    g = mul(probe[...], weights[:, cut], NN) * times_at(count_l, 0, size, cut.start)
    g = g + mul_parts([to_src[0:depth, :], to_src[depth:, :]], oh_src[:, cut], NN)
    new = lstate[:, cut] + jnp.sum(g * g, axis=0, keepdims=True) * (1.0 / depth)
    return left[:, cut] - g * (rate * lax.rsqrt(new))


def first_along_rel():
    return lax.axis_index("rel") < lax.axis_size("rel") // 2


def ahead_left(parity, left, lstate, to_src, oh_src, probe, weights, count_l, rel):
    depth, rows = left.shape

    def body(left, lstate, to_src, oh_src, probe, weights, count_l, _rel, result, _rel_out):
        @pl.when(first_along_rel())
        def _():
            for i in range(rows // 512):
                cut = slice(i * 256, (i + 1) * 256)
                result[:, cut] = left_rows(cut, left, lstate, to_src, oh_src, probe, weights, count_l)

    return call(
        only_on(parity, body), "ahead_left", [left, lstate, to_src, oh_src, probe, weights, count_l, rel],
        [shape(depth, rows // 2), shape(*rel.shape)], aliases={7: 1},
    )


def late_slabs(parity, at, left, lstate, to_src, oh_src, probe, weights, count_l, ahead,
               piece, state, rgrad, to_dst, oh_dst, keep_left, keep_right):
    depth, rows = left.shape

    def body(left, lstate, to_src, oh_src, probe, weights, count_l, ahead, piece, state, rgrad, to_dst, oh_dst,
             _keep_left, _keep_right, left_out, right_out, result, spare, sems):
        def made_ahead():
            return pltpu.make_async_copy(ahead, left_out.at[:, 0 : rows // 2], sems.at[0, 0])

        def copy(i):
            cut = slice(i * 256, (i + 1) * 256)
            return pltpu.make_async_copy(result.at[:, cut], left_out.at[:, cut], sems.at[0, i])

        def make(i):
            cut = slice(i * 256, (i + 1) * 256)
            result[:, cut] = left_rows(cut, left, lstate, to_src, oh_src, probe, weights, count_l)
            copy(i).start()

        count = rows // 256

        @pl.when(first_along_rel())
        def _():
            made_ahead().start()

        @pl.when(jnp.logical_not(first_along_rel()))
        def _():
            for i in range(count // 2):
                make(i)

        wait = update_and_send([piece], state, [rgrad], to_dst, oh_dst, spare, right_out, sems.at[1], fixed=True, start=at)
        for i in range(count // 2, count):
            make(i)
        wait()

        @pl.when(first_along_rel())
        def _():
            made_ahead().wait()

        @pl.when(jnp.logical_not(first_along_rel()))
        def _():
            for i in range(count // 2):
                copy(i).wait()

        for i in range(count // 2, count):
            copy(i).wait()

    operands = [left, lstate, to_src, oh_src, probe, weights, count_l, ahead, piece, state, rgrad, to_dst, oh_dst, keep_left, keep_right]
    return call(
        only_on(parity, body), "late_slabs", operands, [shape(depth, rows), shape(depth, rows)], in_large=(13, 14), out_large=(0, 1),
        scratch_shapes=[*scratch([shape(depth, rows), shape(1, rows)]), pltpu.SemaphoreType.DMA((2, rows // 256))],
        aliases={13: 0, 14: 1},
    )


def relation_update(relations, relation_state, rels):
    kinds, depth = relations.shape

    def body(relations, relation_state, *rest):
        grad = sum(ref[...] for ref in rest[:-1])
        first = lax.broadcasted_iota(jnp.int32, (kinds, kinds), 0)
        second = lax.broadcasted_iota(jnp.int32, (kinds, kinds), 1)
        old = jnp.sum(jnp.where(first == second, relation_state[...], 0.0), axis=1, keepdims=True)
        new = old + jnp.sum(grad * grad, axis=1, keepdims=True) * (1.0 / depth)
        rest[-1][...] = relations[...] - grad * (rate * lax.rsqrt(new))

    return call(body, "relation_update", [relations, relation_state, *rels], [shape(kinds, depth)])[0]


def local(
    left_slab, left_state, right_slab, right_state, relations, relation_state,
    src_index, dst_index, relation_id, neg_source, neg_target,
):
    peers = lax.axis_size("blk")
    inside = [(i, i + 1) for i in range(0, peers, 2)]
    swap = inside + [(i + 1, i) for i in range(0, peers, 2)]
    across = [(i, (i + 1) % peers) for i in range(1, peers, 2)]
    skip = [(i, (i + 2) % peers) for i in range(0, peers, 2)]
    index = (src_index, dst_index, relation_id, neg_source, neg_target)
    left = left_slab.T
    right = right_slab.T
    rows = left.shape[1]
    lstate = left_state.reshape(1, rows)
    number = float(neg_source.shape[1])
    right_far = lax.ppermute(right, "blk", across)
    right_near = [lax.ppermute(right[:, at : at + size], "blk", inside) for at, size in pieces_of(rows, NEAR_FIRST)]
    state_near = lax.ppermute(right_state, "blk", swap)
    state_far = lax.ppermute(state_near, "blk", skip).reshape(1, rows)
    state_near = state_near.reshape(1, rows)
    rel = jnp.zeros(relations.shape, F32)
    ready = prepared(0, left, relations, index)
    left_a, lstate, far, rel = trained(1, "first_near", number, False, FAR, left, lstate, right_near, state_near, rel, ready)
    far = [lax.ppermute(piece, "blk", across) for piece in far]
    left_a, lstate, near, rel = trained(
        0, "first_far", number, True, NEAR, left, lstate, [right_far], state_far, rel, ready, (left_a,)
    )
    near = [lax.ppermute(piece, "blk", inside) for piece in near]
    ready = prepared(1, left_a, relations, index)
    first_lstate = lstate
    left_b, lstate, right_b, rel = trained(1, "last_near", number, False, (), left_a, lstate, near, state_near, rel, ready)
    cuts = pieces_of(rows, FAR)
    right_b, = right_b
    held = ()
    state = None
    for i, (at, size) in enumerate(cuts[:-1]):
        after = lstate if state is None else state
        target, gq, rgrad = last_piece(0, "last_piece%d" % i, number, at, far[i], ready, after, held)
        held = (target, gq)
        to_dst = early_edges(0, "early_edges%d" % i, number, 1, at, at + size, target, ready, dst_index)
        right_b, state = early_right(0, "early_right%d" % i, at, far[i], state, rgrad, to_dst, ready[6], right_b)
    at = cuts[-1][0]
    rgrad, to_src, to_dst, rel, probe, weights = late_edges(0, number, 1, at, far[-1], ready, dst_index, target, gq, rel, state)
    ahead, rel = ahead_left(0, left_a, first_lstate, to_src, ready[5], probe, weights, ready[7], rel)
    if lax.axis_size("rel") == 2:
        rels = [rel, lax.ppermute(rel, "rel", [(0, 1), (1, 0)])]
    else:
        rels = [lax.psum(rel, "rel")]
    left_b, right_b = late_slabs(
        0, at, left_a, first_lstate, to_src, ready[5], probe, weights, ready[7], ahead,
        far[-1], state, rgrad, to_dst, ready[6], left_b, right_b,
    )
    relations_out = relation_update(relations, relation_state.reshape(1, -1), rels)
    return (left_b.T, right_b.T, relations_out[None])


def solution(mesh):
    in_specs = (
        P(("blk", "rel"), None),
        P(("blk", "rel")),
        P(("blk", "rel"), None),
        P(("blk", "rel")),
        P(),
        P(),
        P(None, ("blk", "rel")),
        P(None, ("blk", "rel")),
        P(None, ("blk", "rel")),
        P(None, ("blk", "rel")),
        P(None, ("blk", "rel")),
    )
    out_specs = (P(("blk", "rel"), None), P(("blk", "rel"), None), P("blk", None, None))
    return jax.shard_map(local, mesh=mesh, in_specs=in_specs, out_specs=out_specs, check_vma=False)
```

profile of v0, /device:TPU:0, one launch (start us, length us, event | category | flops | bytes accessed | tf_op | source)
XLA Modules:
  0.0 88.8 jit_solution(4102255752174621757)
XLA Ops:
  0.6 0.0 copy-start.9
  0.6 0.0 copy-start
  0.7 0.0 copy-start.1
  0.7 0.0 copy-start.2
  0.7 0.0 copy-start.3
  0.7 0.0 copy-start.4
  0.7 0.0 copy-start.6
  0.7 0.0 copy-start.7
  0.7 1.6 %collective-permute-start.4 = (f32[400,2048]{1,0:T(8,128)}, f32[400,2048]{1,0:T(8,128)S(1)}, u32[]{:S(2)}, u32[]{:S(2)}) collective-permute-start(f32[400,2048]{1,0:T(8,128)} %bitcast.18), channel_id=1, source_target_pairs={{2,4},{6,8},{10,12},{14,16},{18,20},{22,24},{26,28},{30,0},{3,5},{... | collective-permute-start | bytes 9830408 | tf_op jit(solution)/shard_map/ppermute | solution.py:595
  2.3 2.3 %fusion = (f32[400,1024]{1,0:T(8,128)S(1)}, f32[400,1024]{1,0:T(8,128)S(1)}) fusion(f32[400,2048]{1,0:T(8,128)} %bitcast.19), kind=kLoop, calls=%fused_computation | loop fusion | bytes 6553600 | tf_op jit(solution)/shard_map/slice | solution.py:596
  4.6 0.0 copy-start.5
  4.6 5.9 %collective-permute-start.2 = (f32[400,1024]{1,0:T(8,128)S(1)}, f32[400,1024]{1,0:T(8,128)S(1)}, u32[]{:S(2)}, u32[]{:S(2)}) collective-permute-start(f32[400,1024]{1,0:T(8,128)S(1)} %get-tuple-element.113), channel_id=1, source_target_pairs={{0,2},{4,6},{8,10},{12,14},{16,18},{20,22},{24,26},{28,30},{1,3},{... | collective-permute-start | bytes 4915208 | tf_op jit(solution)/shard_map/ppermute | solution.py:596
  10.5 1.4 %collective-permute-start.1 = (f32[400,1024]{1,0:T(8,128)S(1)}, f32[400,1024]{1,0:T(8,128)S(1)}, u32[]{:S(2)}, u32[]{:S(2)}) collective-permute-start(f32[400,1024]{1,0:T(8,128)S(1)} %get-tuple-element.114), channel_id=1, source_target_pairs={{0,2},{4,6},{8,10},{12,14},{16,18},{20,22},{24,26},{28,30},{1,3},{... | collective-permute-start | bytes 4915208 | tf_op jit(solution)/shard_map/ppermute | solution.py:596
  11.9 0.0 copy-done.9
  11.9 0.1 collective-permute-start
  12.0 0.0 copy-done
  12.0 0.0 copy-done.1
  12.0 0.0 copy-done.2
  12.0 0.0 copy-done.3
  12.0 0.0 copy-done.4
  12.1 0.0 copy-done.6
  12.1 0.0 copy-done.7
  12.1 3.6 %prepare0.1 = (f32[400,256]{1,0:T(8,128)S(1)}, f32[400,256]{1,0:T(8,128)S(1)}, bf16[400,256]{1,0:T(8,128)(2,1)S(1)}, bf16[256,400]{1,0:T(8,128)(2,1)S(1)}, bf16[...) custom-call(f32[400,2048]{1,0:T(8,128)S(1)} %bitcast.9, ...), custom_call_target="tpu_custom_call" | custom-call | flops 1000000 | bytes 100000 | tf_op jit(solution)/shard_map/prepare0/pallas_call | solution.py:319
  15.7 0.2 collective-permute-done
  15.9 0.0 collective-permute-done.2.refs_15_
  15.9 0.0 collective-permute-done.1.refs_14_
  15.9 0.0 copy-done.5
  15.9 0.2 first_near.1
  16.1 1.3 %collective-permute-start.7 = (f32[408,1280]{1,0:T(8,128)S(1)}, f32[408,1280]{1,0:T(8,128)S(1)}, u32[]{:S(2)}, u32[]{:S(2)}) collective-permute-start(f32[408,1280]{1,0:T(8,128)S(1)} %get-tuple-element.84), channel_id=1, source_target_pairs={{2,4},{6,8},{10,12},{14,16},{18,20},{22,24},{26,28},{30,0},{3,5},{... | collective-permute-start | bytes 6266888 | tf_op jit(solution)/shard_map/ppermute | solution.py:603
  17.4 3.5 %collective-permute-start.3 = (f32[2048]{0:T(1024)S(1)}, f32[2048]{0:T(1024)S(1)}, u32[]{:S(2)}, u32[]{:S(2)}) collective-permute-start(f32[2048]{0:T(1024)S(1)} %collective-permute-done), channel_id=1, source_target_pairs={{0,4},{4,8},{8,12},{12,16},{16,20},{20,24},{24,28},{28,0},{1,5},{5... | collective-permute-start | bytes 24584 | tf_op jit(solution)/shard_map/ppermute | solution.py:598
  20.8 4.9 %collective-permute-done.3 = f32[2048]{0:T(1024)S(1)} collective-permute-done((f32[2048]{0:T(1024)S(1)}, f32[2048]{0:T(1024)S(1)}, u32[]{:S(2)}, u32[]{:S(2)}) %collective-permute-start.3) | collective-permute-done | bytes 8224 | tf_op jit(solution)/shard_map/ppermute | solution.py:598
  25.8 18.5 %collective-permute-done.4.refs_14_ = f32[400,2048]{1,0:T(8,128)S(1)} collective-permute-done((f32[400,2048]{1,0:T(8,128)}, f32[400,2048]{1,0:T(8,128)S(1)}, u32[]{:S(2)}, u32[]{:S(2)}) %collective-permute-start.4) | collective-permute-done | bytes 3276832 | tf_op jit(solution)/shard_map/ppermute | solution.py:595
  44.3 8.8 %first_far.1 = (f32[400,2048]{1,0:T(8,128)S(1)}, f32[1,2048]{1,0:T(1,128)S(1)}, f32[32,400]{1,0:T(8,128)S(1)}, f32[408,1024]{1,0:T(8,128)S(1)}, f32[400,1024]{1,0:T(8,128)S(1)}) custom-call(f32[400,2048]{1,0:T(8,128)S(1)} %bitcast.11, f32[1,2048]{1,0:T(1,128)S(1)} %get-tuple-element.68.refs_1_, ...), custom_call_target="tpu_custom_call", output_to_operand_aliasing={{0}: (15, {})} | custom-call | flops 1000000 | bytes 100000 | tf_op jit(solution)/shard_map/first_far/pallas_call | solution.py:319
  53.1 1.4 %collective-permute-start.8 = (f32[408,1024]{1,0:T(8,128)S(1)}, f32[408,1024]{1,0:T(8,128)S(1)}, u32[]{:S(2)}, u32[]{:S(2)}) collective-permute-start(f32[408,1024]{1,0:T(8,128)S(1)} %get-tuple-element.87), channel_id=1, source_target_pairs={{0,2},{4,6},{8,10},{12,14},{16,18},{20,22},{24,26},{28,30},{1,3},{... | collective-permute-start | bytes 5013512 | tf_op jit(solution)/shard_map/ppermute | solution.py:607
  54.5 1.4 %collective-permute-start.9 = (f32[400,1024]{1,0:T(8,128)S(1)}, f32[400,1024]{1,0:T(8,128)S(1)}, u32[]{:S(2)}, u32[]{:S(2)}) collective-permute-start(f32[400,1024]{1,0:T(8,128)S(1)} %get-tuple-element.88), channel_id=1, source_target_pairs={{0,2},{4,6},{8,10},{12,14},{16,18},{20,22},{24,26},{28,30},{1,3},{... | collective-permute-start | bytes 4915208 | tf_op jit(solution)/shard_map/ppermute | solution.py:607
  55.9 1.3 %collective-permute-start.6 = (f32[400,512]{1,0:T(8,128)S(1)}, f32[400,512]{1,0:T(8,128)S(1)}, u32[]{:S(2)}, u32[]{:S(2)}) collective-permute-start(f32[400,512]{1,0:T(8,128)S(1)} %get-tuple-element.83), channel_id=1, source_target_pairs={{2,4},{6,8},{10,12},{14,16},{18,20},{22,24},{26,28},{30,0},{3,5},{... | collective-permute-start | bytes 2457608 | tf_op jit(solution)/shard_map/ppermute | solution.py:603
  57.2 1.3 %collective-permute-start.5 = (f32[400,256]{1,0:T(8,128)S(1)}, f32[400,256]{1,0:T(8,128)S(1)}, u32[]{:S(2)}, u32[]{:S(2)}) collective-permute-start(f32[400,256]{1,0:T(8,128)S(1)} %get-tuple-element.73), channel_id=1, source_target_pairs={{2,4},{6,8},{10,12},{14,16},{18,20},{22,24},{26,28},{30,0},{3,5},{... | collective-permute-start | bytes 1228808 | tf_op jit(solution)/shard_map/ppermute | solution.py:603
  58.5 3.6 %prepare1.1 = (f32[400,256]{1,0:T(8,128)S(1)}, f32[400,256]{1,0:T(8,128)S(1)}, bf16[400,256]{1,0:T(8,128)(2,1)S(1)}, bf16[256,400]{1,0:T(8,128)(2,1)S(1)}, bf16[...) custom-call(f32[400,2048]{1,0:T(8,128)S(1)} %get-tuple-element.71.le, ...), custom_call_target="tpu_custom_call" | custom-call | flops 1000000 | bytes 100000 | tf_op jit(solution)/shard_map/prepare1/pallas_call | solution.py:319
  62.1 0.0 collective-permute-done.9.refs_15_
  62.1 0.0 collective-permute-done.8.refs_14_
  62.1 0.4 last_near.1
  62.5 4.2 %collective-permute-done.7.refs_0_ = f32[408,1280]{1,0:T(8,128)S(1)} collective-permute-done((f32[408,1280]{1,0:T(8,128)S(1)}, f32[408,1280]{1,0:T(8,128)S(1)}, u32[]{:S(2)}, u32[]{:S(2)}) %collective-permute-start.7) | collective-permute-done | bytes 2088992 | tf_op jit(solution)/shard_map/ppermute | solution.py:603
  66.7 2.5 %last_piece0.1 = (f32[400,256]{1,0:T(8,128)S(1)}, f32[400,256]{1,0:T(8,128)S(1)}, f32[400,1280]{1,0:T(8,128)S(1)}) custom-call(f32[408,1280]{1,0:T(8,128)S(1)} %collective-permute-done.7.refs_0_, bf16[400,256]{1,0:T(8,128)(2,1)S(1)} %get-tuple-element.76.refs_6_.refs_1_.query, bf16[256,400]{1,0:T(8,128)(2,1)S(1)} %get-tuple-element.77.refs_7_.refs_2_.query_rows, ...), custom_call_target="tpu_custom_call" | custom-call | flops 1000000 | bytes 100000 | tf_op jit(solution)/shard_map/last_piece0/pallas_call | solution.py:319
  69.2 1.5 %early_edges0.1.refs_2_ = bf16[800,256]{1,0:T(8,128)(2,1)S(1)} custom-call(f32[400,256]{1,0:T(8,128)S(1)} %get-tuple-element.74.refs_4_.refs_0_.weight, f32[400,256]{1,0:T(8,128)S(1)} %get-tuple-element.75.refs_5_.refs_1_.source, f32[400,256]{1,0:T(8,128)S(1)} %get-tuple-element.90.refs_2_.refs_5_, ...), custom_call_target="tpu_custom_call" | custom-call | flops 1000000 | bytes 100000 | tf_op jit(solution)/shard_map/early_edges0/pallas_call | solution.py:319
  70.7 1.9 %early_right0.1 = (f32[400,2048]{1,0:T(8,128)}, f32[1,2048]{1,0:T(1,128)S(1)}) custom-call(f32[408,1280]{1,0:T(8,128)S(1)} %collective-permute-done.7.refs_0_, f32[400,1280]{1,0:T(8,128)S(1)} %get-tuple-element.92.refs_1_, bf16[800,256]{1,0:T(8,128)(2,1)S(1)} %early_edges0.1.refs_2_, ...), custom_call_target="tpu_custom_call", output_to_operand_aliasing={{0}: (4, {})} | custom-call | flops 1000000 | bytes 100000 | tf_op jit(solution)/shard_map/early_right0/pallas_call | solution.py:319
  72.7 2.8 %collective-permute-done.6.refs_0_ = f32[400,512]{1,0:T(8,128)S(1)} collective-permute-done((f32[400,512]{1,0:T(8,128)S(1)}, f32[400,512]{1,0:T(8,128)S(1)}, u32[]{:S(2)}, u32[]{:S(2)}) %collective-permute-start.6) | collective-permute-done | bytes 819232 | tf_op jit(solution)/shard_map/ppermute | solution.py:603
  75.5 1.2 %last_piece1.1 = (f32[400,256]{1,0:T(8,128)S(1)}, f32[400,256]{1,0:T(8,128)S(1)}, f32[400,512]{1,0:T(8,128)S(1)}) custom-call(f32[400,512]{1,0:T(8,128)S(1)} %collective-permute-done.6.refs_0_, bf16[400,256]{1,0:T(8,128)(2,1)S(1)} %get-tuple-element.76.refs_6_.refs_1_.query, ...), custom_call_target="tpu_custom_call", output_to_operand_aliasing={{0}: (5, {}), {1}: (6, {})} | custom-call | flops 1000000 | bytes 100000 | tf_op jit(solution)/shard_map/last_piece1/pallas_call | solution.py:319
  76.7 1.5 %early_edges1.1.refs_2_ = bf16[800,256]{1,0:T(8,128)(2,1)S(1)} custom-call(f32[400,256]{1,0:T(8,128)S(1)} %get-tuple-element.74.refs_4_.refs_0_.weight, f32[400,256]{1,0:T(8,128)S(1)} %get-tuple-element.75.refs_5_.refs_1_.source, f32[400,256]{1,0:T(8,128)S(1)} %get-tuple-element.95.refs_2_.held_t, ...), custom_call_target="tpu_custom_call" | custom-call | flops 1000000 | bytes 100000 | tf_op jit(solution)/shard_map/early_edges1/pallas_call | solution.py:319
  78.2 1.5 %early_right1.1 = (f32[400,2048]{1,0:T(8,128)}, f32[1,2048]{1,0:T(1,128)S(1)}) custom-call(f32[400,512]{1,0:T(8,128)S(1)} %collective-permute-done.6.refs_0_, f32[400,512]{1,0:T(8,128)S(1)} %get-tuple-element.98.refs_1_, bf16[800,256]{1,0:T(8,128)(2,1)S(1)} %early_edges1.1.refs_2_, ...), custom_call_target="tpu_custom_call", output_to_operand_aliasing={{0}: (5, {})} | custom-call | flops 1000000 | bytes 100000 | tf_op jit(solution)/shard_map/early_right1/pallas_call | solution.py:319
  79.8 0.1 collective-permute-done.5.piece.refs_8_
  79.9 2.7 %late_edges.1 = (f32[400,256]{1,0:T(8,128)S(1)}, bf16[800,256]{1,0:T(8,128)(2,1)S(1)}, bf16[800,256]{1,0:T(8,128)(2,1)S(1)}, f32[32,400]{1,0:T(8,128)S(1)}, bf16...) custom-call(f32[400,256]{1,0:T(8,128)S(1)} %collective-permute-done.5.piece.refs_8_, ...), custom_call_target="tpu_custom_call" | custom-call | flops 1000000 | bytes 100000 | tf_op jit(solution)/shard_map/late_edges/pallas_call | solution.py:319
  82.6 1.1 %ahead_left.1 = (f32[400,1024]{1,0:T(8,128)S(1)}, f32[32,400]{1,0:T(8,128)S(1)}) custom-call(f32[400,2048]{1,0:T(8,128)S(1)} %get-tuple-element.71.left.refs_0_, f32[1,2048]{1,0:T(1,128)S(1)} %get-tuple-element.72.refs_1_, bf16[800,256]{1,0:T(8,128)(2,1)S(1)} %get-tuple-element.101.refs_2_, ...), custom_call_target="tpu_custom_call", output_to_operand_aliasing={{1}: (7, {})} | custom-call | flops 1000000 | bytes 100000 | tf_op jit(solution)/shard_map/ahead_left/pallas_call | solution.py:319
  83.7 1.6 %collective-permute-start.10 = (f32[32,400]{1,0:T(8,128)S(1)}, f32[32,400]{1,0:T(8,128)S(1)}, u32[]{:S(2)}, u32[]{:S(2)}) collective-permute-start(f32[32,400]{1,0:T(8,128)S(1)} %get-tuple-element.112.rest_0_), channel_id=1, source_target_pairs={{0,1},{1,0},{2,3},{3,2},{4,5},{5,4},{6,7},{7,6},{8,9},{9,8},{10,11... | collective-permute-start | bytes 153608 | tf_op jit(solution)/shard_map/ppermute | solution.py:625
  85.3 0.0 copy-start.8
  85.3 2.2 %late_slabs.1 = (f32[400,2048]{1,0:T(8,128)}, f32[400,2048]{1,0:T(8,128)}) custom-call(f32[400,2048]{1,0:T(8,128)S(1)} %get-tuple-element.71.left.refs_0_, f32[1,2048]{1,0:T(1,128)S(1)} %get-tuple-element.72.refs_1_, bf16[800,256]{1,0:T(8,128)(2,1)S(1)} %get-tuple-element.101.refs_2_, ...), custom_call_target="tpu_custom_call", output_to_operand_aliasing={{0}: (13, {}), {1}: (14, {})} | custom-call | flops 1000000 | bytes 100000 | tf_op jit(solution)/shard_map/late_slabs/pallas_call | solution.py:319
  87.5 0.5 collective-permute-done.10.rest_1_
  88.1 0.0 copy-done.8
  88.1 0.7 relation_update.1
  (1 shorter events, 0.0 us)
Async XLA Ops:
  0.6 11.3 %copy-start.9 = (f32[2048]{0:T(1024)S(1)}, f32[2048]{0:T(1024)}, u32[]{:S(2)}) copy-start(f32[2048]{0:T(1024)} %param.14) | copy-start | bytes 24580
  0.6 11.4 %copy-start = (f32[2048,400]{0,1:T(8,128)S(1)}, f32[2048,400]{0,1:T(8,128)}, u32[]{:S(2)}) copy-start(f32[2048,400]{0,1:T(8,128)} %param.11) | copy-start | bytes 9830404
  0.7 11.4 %copy-start.1 = (f32[32,400]{1,0:T(8,128)S(1)}, f32[32,400]{1,0:T(8,128)}, u32[]{:S(2)}) copy-start(f32[32,400]{1,0:T(8,128)} %relations.5) | copy-start | bytes 153604
  0.7 11.4 %copy-start.2 = (s32[2,256]{1,0:T(2,128)S(1)}, s32[2,256]{1,0:T(2,128)}, u32[]{:S(2)}) copy-start(s32[2,256]{1,0:T(2,128)} %dst.5) | copy-start | bytes 6148
  0.7 11.4 %copy-start.3 = (s32[2,1000]{1,0:T(2,128)S(1)}, s32[2,1000]{1,0:T(2,128)}, u32[]{:S(2)}) copy-start(s32[2,1000]{1,0:T(2,128)} %nsrc.3) | copy-start | bytes 24004
  0.7 11.4 %copy-start.4 = (s32[2,1000]{1,0:T(2,128)S(1)}, s32[2,1000]{1,0:T(2,128)}, u32[]{:S(2)}) copy-start(s32[2,1000]{1,0:T(2,128)} %ndst.3) | copy-start | bytes 24004
  0.7 11.4 %copy-start.6 = (s32[2,256]{1,0:T(2,128)S(1)}, s32[2,256]{1,0:T(2,128)}, u32[]{:S(2)}) copy-start(s32[2,256]{1,0:T(2,128)} %src.3) | copy-start | bytes 6148
  0.7 11.4 %copy-start.7 = (s32[2,256]{1,0:T(2,128)S(1)}, s32[2,256]{1,0:T(2,128)}, u32[]{:S(2)}) copy-start(s32[2,256]{1,0:T(2,128)} %rid.3) | copy-start | bytes 6148
  0.7 43.6 %collective-permute-start.4 = (f32[400,2048]{1,0:T(8,128)}, f32[400,2048]{1,0:T(8,128)S(1)}, u32[]{:S(2)}, u32[]{:S(2)}) collective-permute-start(f32[400,2048]{1,0:T(8,128)} %bitcast.18), channel_id=1, source_target_pairs={{2,4},{6,8},{10,12},{14,16},{18,20},{22,24},{26,28},{30,0},{3,5},{... | collective-permute-start | bytes 9830408 | tf_op jit(solution)/shard_map/ppermute | solution.py:595
  4.6 11.3 %copy-start.5 = (f32[2048]{0:T(1024)S(1)}, f32[2048]{0:T(1024)}, u32[]{:S(2)}) copy-start(f32[2048]{0:T(1024)} %param.12) | copy-start | bytes 24580
  4.6 11.3 %collective-permute-start.2 = (f32[400,1024]{1,0:T(8,128)S(1)}, f32[400,1024]{1,0:T(8,128)S(1)}, u32[]{:S(2)}, u32[]{:S(2)}) collective-permute-start(f32[400,1024]{1,0:T(8,128)S(1)} %get-tuple-element.113), channel_id=1, source_target_pairs={{0,2},{4,6},{8,10},{12,14},{16,18},{20,22},{24,26},{28,30},{1,3},{... | collective-permute-start | bytes 4915208 | tf_op jit(solution)/shard_map/ppermute | solution.py:596
  10.5 5.4 %collective-permute-start.1 = (f32[400,1024]{1,0:T(8,128)S(1)}, f32[400,1024]{1,0:T(8,128)S(1)}, u32[]{:S(2)}, u32[]{:S(2)}) collective-permute-start(f32[400,1024]{1,0:T(8,128)S(1)} %get-tuple-element.114), channel_id=1, source_target_pairs={{0,2},{4,6},{8,10},{12,14},{16,18},{20,22},{24,26},{28,30},{1,3},{... | collective-permute-start | bytes 4915208 | tf_op jit(solution)/shard_map/ppermute | solution.py:596
  11.9 4.0 %collective-permute-start = (f32[2048]{0:T(1024)S(1)}, f32[2048]{0:T(1024)S(1)}, u32[]{:S(2)}, u32[]{:S(2)}) collective-permute-start(f32[2048]{0:T(1024)S(1)} %copy-done.9), channel_id=1, source_target_pairs={{0,2},{4,6},{8,10},{12,14},{16,18},{20,22},{24,26},{28,30},{2,0},{... | collective-permute-start | bytes 24584 | tf_op jit(solution)/shard_map/ppermute | solution.py:597
  16.1 50.6 %collective-permute-start.7 = (f32[408,1280]{1,0:T(8,128)S(1)}, f32[408,1280]{1,0:T(8,128)S(1)}, u32[]{:S(2)}, u32[]{:S(2)}) collective-permute-start(f32[408,1280]{1,0:T(8,128)S(1)} %get-tuple-element.84), channel_id=1, source_target_pairs={{2,4},{6,8},{10,12},{14,16},{18,20},{22,24},{26,28},{30,0},{3,5},{... | collective-permute-start | bytes 6266888 | tf_op jit(solution)/shard_map/ppermute | solution.py:603
  17.4 8.4 %collective-permute-start.3 = (f32[2048]{0:T(1024)S(1)}, f32[2048]{0:T(1024)S(1)}, u32[]{:S(2)}, u32[]{:S(2)}) collective-permute-start(f32[2048]{0:T(1024)S(1)} %collective-permute-done), channel_id=1, source_target_pairs={{0,4},{4,8},{8,12},{12,16},{16,20},{20,24},{24,28},{28,0},{1,5},{5... | collective-permute-start | bytes 24584 | tf_op jit(solution)/shard_map/ppermute | solution.py:598
  53.1 9.0 %collective-permute-start.8 = (f32[408,1024]{1,0:T(8,128)S(1)}, f32[408,1024]{1,0:T(8,128)S(1)}, u32[]{:S(2)}, u32[]{:S(2)}) collective-permute-start(f32[408,1024]{1,0:T(8,128)S(1)} %get-tuple-element.87), channel_id=1, source_target_pairs={{0,2},{4,6},{8,10},{12,14},{16,18},{20,22},{24,26},{28,30},{1,3},{... | collective-permute-start | bytes 5013512 | tf_op jit(solution)/shard_map/ppermute | solution.py:607
  54.5 7.6 %collective-permute-start.9 = (f32[400,1024]{1,0:T(8,128)S(1)}, f32[400,1024]{1,0:T(8,128)S(1)}, u32[]{:S(2)}, u32[]{:S(2)}) collective-permute-start(f32[400,1024]{1,0:T(8,128)S(1)} %get-tuple-element.88), channel_id=1, source_target_pairs={{0,2},{4,6},{8,10},{12,14},{16,18},{20,22},{24,26},{28,30},{1,3},{... | collective-permute-start | bytes 4915208 | tf_op jit(solution)/shard_map/ppermute | solution.py:607
  55.9 19.6 %collective-permute-start.6 = (f32[400,512]{1,0:T(8,128)S(1)}, f32[400,512]{1,0:T(8,128)S(1)}, u32[]{:S(2)}, u32[]{:S(2)}) collective-permute-start(f32[400,512]{1,0:T(8,128)S(1)} %get-tuple-element.83), channel_id=1, source_target_pairs={{2,4},{6,8},{10,12},{14,16},{18,20},{22,24},{26,28},{30,0},{3,5},{... | collective-permute-start | bytes 2457608 | tf_op jit(solution)/shard_map/ppermute | solution.py:603
  57.2 22.7 %collective-permute-start.5 = (f32[400,256]{1,0:T(8,128)S(1)}, f32[400,256]{1,0:T(8,128)S(1)}, u32[]{:S(2)}, u32[]{:S(2)}) collective-permute-start(f32[400,256]{1,0:T(8,128)S(1)} %get-tuple-element.73), channel_id=1, source_target_pairs={{2,4},{6,8},{10,12},{14,16},{18,20},{22,24},{26,28},{30,0},{3,5},{... | collective-permute-start | bytes 1228808 | tf_op jit(solution)/shard_map/ppermute | solution.py:603
  83.7 4.3 %collective-permute-start.10 = (f32[32,400]{1,0:T(8,128)S(1)}, f32[32,400]{1,0:T(8,128)S(1)}, u32[]{:S(2)}, u32[]{:S(2)}) collective-permute-start(f32[32,400]{1,0:T(8,128)S(1)} %get-tuple-element.112.rest_0_), channel_id=1, source_target_pairs={{0,1},{1,0},{2,3},{3,2},{4,5},{5,4},{6,7},{7,6},{8,9},{9,8},{10,11... | collective-permute-start | bytes 153608 | tf_op jit(solution)/shard_map/ppermute | solution.py:625
  85.3 2.8 %copy-start.8 = (f32[32]{0:T(128)S(1)}, f32[32]{0:T(128)}, u32[]{:S(2)}) copy-start(f32[32]{0:T(128)} %param.16) | copy-start | bytes 388
where the time goes:
time: 89.1 us; the launch traced here: 88.8 us
  Pallas kernels  33.6 us (38%)
  waiting for transfers between devices  31.3 us (35%)
  starting transfers between devices  20.6 us (23%)
  local copies, waits for them, and re-layouts  2.37 us (3%)
  between operations  0.99 us (1%)
    pallas_call x15, Pallas kernels, call(): pl.pallas_call(kernel, out_shape=tuple(shapes), in_specs=[large if i in i...  33.6 us
    ppermute x1, waiting for transfers between devices, local(): right_far = lax.ppermute(right, 'blk', across)  18.5 us
    ppermute x2, starting transfers between devices, local(): lax.ppermute(right[:, at:at + size], 'blk', inside)  7.28 us
    ppermute x3, waiting for transfers between devices, local(): far = [lax.ppermute(piece, 'blk', across) for piece in far]  7.09 us
    ppermute x1, waiting for transfers between devices, local(): state_far = lax.ppermute(state_near, 'blk', skip).reshape(1, rows)  4.93 us
    ppermute x3, starting transfers between devices, local(): far = [lax.ppermute(piece, 'blk', across) for piece in far]  3.88 us
    ppermute x1, starting transfers between devices, local(): state_far = lax.ppermute(state_near, 'blk', skip).reshape(1, rows)  3.46 us
    ppermute x2, starting transfers between devices, local(): near = [lax.ppermute(piece, 'blk', inside) for piece in near]  2.79 us
  transfers between devices with their start and end apart: 11, of which 7 were waited for; matrix products, arithmetic and copies ran while one was open for 3% of the time, Pallas kernels for 33%

commit v1 on v0

--- a/solution.py
+++ b/solution.py
@@ -93,6 +93,10 @@
     return (0.5 * x).T.astype(BF16)
 
 
+def half_product(a, b):
+    return (0.5 * (a * b).astype(BF16).astype(F32)).astype(BF16)
+
+
 def negative_weights(rows16, query_rows, number):
     half = 0.5 / number
     return (jnp.tanh(mul(query_rows, rows16, NN)) * half + half).astype(BF16)
@@ -108,7 +112,7 @@
 
 
 def prepare(step, left, relations, src, dst, rid, nsrc, ndst,
-            weight, source, query, query_rows, left16, oh_src, oh_dst, count_l, count_r, kind):
+            weight, source, query, query_rows, left16, oh_src, oh_dst, count_l, count_r, kind, weight_rows):
     rows = left.shape[1]
     here = slice(step, step + 1)
     row_onehot(src[here, :], oh_src)
@@ -118,6 +122,7 @@
     kinds = lax.broadcasted_iota(jnp.int32, kind.shape, 0)
     kind[...] = jnp.where(rid[here, :] == kinds, 1.0, 0.0).astype(BF16)
     weight[...] = sum(mul(part, kind[...], TN) for part in split(relations[...], 3))
+    weight_rows[...] = weight[...].T
     source[...] = jnp.zeros_like(source)
 
     size = step_of(rows)
@@ -261,9 +266,9 @@
 def train(parity, number, last, fixed, kept, takes, gives, *refs):
     refs = list(refs)
     (left, lstate, rstate_in, rel_in) = refs[:4]
-    (weight, source, query, query_rows, left16, oh_src, oh_dst, count_l, count_r, kind) = refs[4:14]
-    right = refs[14 : 14 + takes]
-    refs = refs[14 + takes + kept :]
+    (weight, source, query, query_rows, left16, oh_src, oh_dst, count_l, count_r, kind, _rows) = refs[4:15]
+    right = refs[15 : 15 + takes]
+    refs = refs[15 + takes + kept :]
     left_out, lstate_out, rel_out = refs[:3]
     right_out = refs[3 : 3 + len(gives)]
     (target, gq, rgrad, probe, probe_rows, gp, lgrad, to_src, to_dst, rstate, spare, sems) = refs[3 + len(gives) :]
@@ -292,9 +297,9 @@
                 for old, begin, length in rows_of(right, at, size):
                     cut = slice(begin, begin + length)
                     here = slice(begin - at, begin - at + length)
-                    adagrad(old, rstate_in.at[:, cut], rgrad.at[:, cut], to_dst, oh_dst, begin, out.at[:, here], spare.at[:, cut], None, fixed)
+                    adagrad(old, rstate_in.at[:, cut], rgrad.at[:, cut], to_dst, oh_dst, begin, out.at[:, here], spare.at[:, cut])
             pack_state(spare, right_out[STATE], depth)
-            adagrad(left, lstate, lgrad, to_src, oh_src, 0, left_out, lstate_out, None, fixed)
+            adagrad(left, lstate, lgrad, to_src, oh_src, 0, left_out, lstate_out)
 
 
 def shape(*dims, dtype=F32):
@@ -305,7 +310,7 @@
     return (
         shape(depth, edges), shape(depth, edges), shape(depth, edges, dtype=BF16), shape(edges, depth, dtype=BF16),
         shape(depth, rows, dtype=BF16), shape(edges, rows, dtype=BF16), shape(edges, rows, dtype=BF16),
-        shape(rows // LANES, LANES), shape(rows // LANES, LANES), shape(kinds, edges, dtype=BF16),
+        shape(rows // LANES, LANES), shape(rows // LANES, LANES), shape(kinds, edges, dtype=BF16), shape(edges, depth),
     )
 
 
@@ -356,7 +361,7 @@
         [slab, shape(1, rows), shape(*rel.shape), *blocks],
         out_large=(0, 3) if last else (),
         scratch_shapes=[*scratch(inner), pltpu.SemaphoreType.DMA((2, rows // 256))],
-        aliases={14 + len(right) + i: 0 for i in range(len(keep))},
+        aliases={15 + len(right) + i: 0 for i in range(len(keep))},
     )
     return left_out, lstate_out, right_out, rel_out
 
@@ -371,7 +376,7 @@
 
 
 def last_piece(parity, name, number, at, piece, ready, after, held=()):
-    (_weight, _source, query, query_rows, _left16, _oh_src, oh_dst, _count_l, count_r, _kind) = ready
+    (_weight, _source, query, query_rows, _left16, _oh_src, oh_dst, _count_l, count_r, _kind, _rows) = ready
     depth, edges = query.shape
 
     def body(piece, query, query_rows, oh_dst, count_r, *rest):
@@ -385,7 +390,7 @@
     )
 
 
-def source_scores(number, probe, probe_rows, left16, count_l, gp, weights=None):
+def source_scores(number, probe_rows, left16, count_l, gp, weights=None):
     rows = left16.shape[1]
     size = step_of(rows, 1024)
     gp[...] = jnp.zeros_like(gp)
@@ -399,26 +404,25 @@
 
 
 def early_edges(parity, name, number, step, low, high, target, ready, dst):
-    (weight, source, _query, _query_rows, left16, _oh_src, _oh_dst, count_l, _count_r, _kind) = ready
+    (weight, source, _query, _query_rows, left16, _oh_src, _oh_dst, count_l, _count_r, _kind, weight_rows) = ready
     depth = left16.shape[0]
     edges = weight.shape[1]
 
-    def body(weight, source, target, left16, count_l, dst, to_dst, gp, probe, probe_rows):
+    def body(weight, source, target, left16, count_l, dst, weight_rows, to_dst, target_rows, gp, probe_rows):
         w, s, t = weight[...], source[...], target[...]
-        product = (w * t).astype(BF16)
-        probe[...] = product
-        probe_rows[...] = half_rows(product.astype(F32))
-        source_scores(number, probe, probe_rows, left16, count_l, gp)
+        target_rows[...] = t.T
+        probe_rows[...] = half_product(weight_rows[...], target_rows[...])
+        source_scores(number, probe_rows, left16, count_l, gp)
         at = dst[step : step + 1, :]
         here = jnp.logical_and(at >= low, at < high)
         coef = -jax.nn.sigmoid(-jnp.sum(s * w * t, axis=0, keepdims=True))
         to_dst[0:depth, :], to_dst[depth:, :] = split(jnp.where(here, coef * w * s + gp[...] * w, 0.0), 2)
 
     return call(
-        only_on(parity, body), name, [weight, source, target, left16, count_l, dst],
-        [shape(2 * depth, edges, dtype=BF16)],
-        scratch_shapes=scratch([shape(depth, edges), shape(depth, edges, dtype=BF16), shape(edges, depth, dtype=BF16)]),
-    )[0]
+        only_on(parity, body), name, [weight, source, target, left16, count_l, dst, weight_rows],
+        [shape(2 * depth, edges, dtype=BF16), shape(edges, depth)],
+        scratch_shapes=scratch([shape(depth, edges), shape(edges, depth, dtype=BF16)]),
+    )
 
 
 def early_right(parity, name, at, piece, state, rgrad, to_dst, oh_dst, keep):
@@ -442,41 +446,42 @@
     )
 
 
-def late_edges(parity, number, step, at, piece, ready, dst, target, gq, rel, after):
-    (weight, source, query, query_rows, left16, _oh_src, oh_dst, count_l, count_r, kind) = ready
+def late_edges(parity, number, step, at, piece, ready, dst, target, target_rows, gq, rel, after):
+    (weight, source, query, query_rows, left16, _oh_src, oh_dst, count_l, count_r, kind, weight_rows) = ready
     depth, rows = left16.shape
     edges = weight.shape[1]
     pair16 = shape(2 * depth, edges, dtype=BF16)
 
-    def body(piece, weight, source, query, query_rows, left16, oh_dst, count_l, count_r, kind, dst, held_t, held_q, rel_in,
-             _after, rgrad, to_src, to_dst, rel_out, probe, weights, gp, probe_rows):
-        rel_out[...] = rel_in[...]
-
-        @on_parity(parity)
-        def _():
-            size = piece.shape[1]
-            parts = split(piece[...], 3)
-            w, s = weight[...], source[...]
-            t = held_t[...] + mul_parts(parts, oh_dst[:, at : at + size], NT)
-            product = (w * t).astype(BF16)
-            probe[...] = product
-            probe_rows[...] = half_rows(product.astype(F32))
-            source_scores(number, probe, probe_rows, left16, count_l, gp, weights)
-            rgrad[...], more = negatives(parts[0], query[...], query_rows[...], times_at(count_r, 0, size, at), number)
-            q = held_q[...] + more
-            p = gp[...]
-            coef = -jax.nn.sigmoid(-jnp.sum(s * w * t, axis=0, keepdims=True))
-            g_weight = coef * s * t + q * s + p * t
-            rel_out[...] = rel_in[...] + sum(mul(kind[...], part, NT) for part in split(g_weight, 2))
-            to_src[0:depth, :], to_src[depth:, :] = split(coef * w * t + q * w, 2)
-            here = dst[step : step + 1, :] >= at
-            to_dst[0:depth, :], to_dst[depth:, :] = split(jnp.where(here, coef * w * s + p * w, 0.0), 2)
+    def body(piece, weight, source, query, query_rows, left16, oh_dst, count_l, count_r, kind, dst, weight_rows,
+             held_t, held_rows, held_q, rel_in, _after,
+             rgrad, to_src, to_dst, rel_out, probe, weights, gp, probe_rows):
+        size = piece.shape[1]
+        parts = split(piece[...], 3)
+        hits = oh_dst[:, at : at + size]
+        slab = jnp.concatenate(parts, axis=1)
+        table = jnp.concatenate([hits] * 3, axis=1)
+        probe_rows[...] = half_product(weight_rows[...], held_rows[...] + mul(table, slab, NT))
+        source_scores(number, probe_rows, left16, count_l, gp, weights)
+        w, s = weight[...], source[...]
+        t = held_t[...] + mul(slab, table, NT)
+        probe[...] = (w * t).astype(BF16)
+        rgrad[...], more = negatives(parts[0], query[...], query_rows[...], times_at(count_r, 0, size, at), number)
+        q = held_q[...] + more
+        p = gp[...]
+        coef = -jax.nn.sigmoid(-jnp.sum(s * w * t, axis=0, keepdims=True))
+        g_weight = coef * s * t + q * s + p * t
+        rel_out[...] = rel_in[...] + sum(mul(kind[...], part, NT) for part in split(g_weight, 2))
+        to_src[0:depth, :], to_src[depth:, :] = split(coef * w * t + q * w, 2)
+        here = dst[step : step + 1, :] >= at
+        to_dst[0:depth, :], to_dst[depth:, :] = split(jnp.where(here, coef * w * s + p * w, 0.0), 2)
 
     return call(
-        body, "late_edges",
-        [piece, weight, source, query, query_rows, left16, oh_dst, count_l, count_r, kind, dst, target, gq, rel, after],
+        only_on(parity, body), "late_edges",
+        [piece, weight, source, query, query_rows, left16, oh_dst, count_l, count_r, kind, dst, weight_rows,
+         target, target_rows, gq, rel, after],
         [shape(depth, piece.shape[1]), pair16, pair16, shape(*rel.shape), shape(depth, edges, dtype=BF16), shape(edges, rows, dtype=BF16)],
         scratch_shapes=scratch([shape(depth, edges), shape(edges, depth, dtype=BF16)]),
+        aliases={15: 3},
     )
 
 
@@ -489,6 +494,10 @@
     return left[:, cut] - g * (rate * lax.rsqrt(new))
 
 
+def ahead_rows(rows):
+    return rows // 4
+
+
 def first_along_rel():
     return lax.axis_index("rel") < lax.axis_size("rel") // 2
 
@@ -499,13 +508,13 @@
     def body(left, lstate, to_src, oh_src, probe, weights, count_l, _rel, result, _rel_out):
         @pl.when(first_along_rel())
         def _():
-            for i in range(rows // 512):
+            for i in range(ahead_rows(rows) // 256):
                 cut = slice(i * 256, (i + 1) * 256)
                 result[:, cut] = left_rows(cut, left, lstate, to_src, oh_src, probe, weights, count_l)
 
     return call(
         only_on(parity, body), "ahead_left", [left, lstate, to_src, oh_src, probe, weights, count_l, rel],
-        [shape(depth, rows // 2), shape(*rel.shape)], aliases={7: 1},
+        [shape(depth, ahead_rows(rows)), shape(*rel.shape)], aliases={7: 1},
     )
 
 
@@ -516,7 +525,7 @@
     def body(left, lstate, to_src, oh_src, probe, weights, count_l, ahead, piece, state, rgrad, to_dst, oh_dst,
              _keep_left, _keep_right, left_out, right_out, result, spare, sems):
         def made_ahead():
-            return pltpu.make_async_copy(ahead, left_out.at[:, 0 : rows // 2], sems.at[0, 0])
+            return pltpu.make_async_copy(ahead, left_out.at[:, 0 : ahead_rows(rows)], sems.at[0, 0])
 
         def copy(i):
             cut = slice(i * 256, (i + 1) * 256)
@@ -525,9 +534,19 @@
         def make(i):
             cut = slice(i * 256, (i + 1) * 256)
             result[:, cut] = left_rows(cut, left, lstate, to_src, oh_src, probe, weights, count_l)
-            copy(i).start()
 
         count = rows // 256
+        first = ahead_rows(rows) // 256
+
+        @pl.when(jnp.logical_not(first_along_rel()))
+        def _():
+            for i in range(first):
+                make(i)
+
+        half = (count + first) // 2
+        for i in range(first, half):
+            make(i)
+        wait = update_and_send([piece], state, [rgrad], to_dst, oh_dst, spare, right_out, sems.at[1], fixed=True, start=at)
 
         @pl.when(first_along_rel())
         def _():
@@ -535,12 +554,14 @@
 
         @pl.when(jnp.logical_not(first_along_rel()))
         def _():
-            for i in range(count // 2):
-                make(i)
-
-        wait = update_and_send([piece], state, [rgrad], to_dst, oh_dst, spare, right_out, sems.at[1], fixed=True, start=at)
-        for i in range(count // 2, count):
+            for i in range(first):
+                copy(i).start()
+
+        for i in range(first, half):
+            copy(i).start()
+        for i in range(half, count):
             make(i)
+            copy(i).start()
         wait()
 
         @pl.when(first_along_rel())
@@ -549,10 +570,10 @@
 
         @pl.when(jnp.logical_not(first_along_rel()))
         def _():
-            for i in range(count // 2):
+            for i in range(first):
                 copy(i).wait()
 
-        for i in range(count // 2, count):
+        for i in range(first, count):
             copy(i).wait()
 
     operands = [left, lstate, to_src, oh_src, probe, weights, count_l, ahead, piece, state, rgrad, to_dst, oh_dst, keep_left, keep_right]
@@ -616,10 +637,10 @@
         after = lstate if state is None else state
         target, gq, rgrad = last_piece(0, "last_piece%d" % i, number, at, far[i], ready, after, held)
         held = (target, gq)
-        to_dst = early_edges(0, "early_edges%d" % i, number, 1, at, at + size, target, ready, dst_index)
+        to_dst, target_rows = early_edges(0, "early_edges%d" % i, number, 1, at, at + size, target, ready, dst_index)
         right_b, state = early_right(0, "early_right%d" % i, at, far[i], state, rgrad, to_dst, ready[6], right_b)
     at = cuts[-1][0]
-    rgrad, to_src, to_dst, rel, probe, weights = late_edges(0, number, 1, at, far[-1], ready, dst_index, target, gq, rel, state)
+    rgrad, to_src, to_dst, rel, probe, weights = late_edges(0, number, 1, at, far[-1], ready, dst_index, target, target_rows, gq, rel, state)
     ahead, rel = ahead_left(0, left_a, first_lstate, to_src, ready[5], probe, weights, ready[7], rel)
     if lax.axis_size("rel") == 2:
         rels = [rel, lax.ppermute(rel, "rel", [(0, 1), (1, 0)])]

time: 89.1 us -> 89 us (level)
  waiting for transfers between devices: 31.3 us -> 28.4 us
  Pallas kernels: 33.6 us -> 36.1 us
    pallas_call x15, Pallas kernels: 33.6 us -> 36.1 us  [call(): pl.pallas_call(kernel, out_shape=tuple(shapes), in_specs=[large if i in i...]
    ppermute x3, waiting for transfers between devices: 7.09 us -> 4.72 us  [local(): far = [lax.ppermute(piece, 'blk', across) for piece in far]]
  transfers between devices with their start and end apart: 11 -> 11, of which waited for: 7 -> 5; matrix products, arithmetic and copies ran while one was open for 3% -> 2% of each run, Pallas kernels for 33% -> 36%
where the time goes in v1:
time: 89 us; the launch traced here: 88.7 us
  Pallas kernels  36.1 us (41%)
  waiting for transfers between devices  28.4 us (32%)
  starting transfers between devices  21 us (24%)
  local copies, waits for them, and re-layouts  2.21 us (2%)
  between operations  0.98 us (1%)
    pallas_call x15, Pallas kernels, call(): pl.pallas_call(kernel, out_shape=tuple(shapes), in_specs=[large if i in i...  36.1 us
    ppermute x1, waiting for transfers between devices, local(): right_far = lax.ppermute(right, 'blk', across)  18.7 us
    ppermute x2, starting transfers between devices, local(): lax.ppermute(right[:, at:at + size], 'blk', inside)  7.28 us
    ppermute x1, waiting for transfers between devices, local(): state_far = lax.ppermute(state_near, 'blk', skip).reshape(1, rows)  4.93 us
    ppermute x3, waiting for transfers between devices, local(): far = [lax.ppermute(piece, 'blk', across) for piece in far]  4.72 us
    ppermute x3, starting transfers between devices, local(): far = [lax.ppermute(piece, 'blk', across) for piece in far]  3.88 us
    ppermute x1, starting transfers between devices, local(): state_far = lax.ppermute(state_near, 'blk', skip).reshape(1, rows)  3.46 us
    ppermute x2, starting transfers between devices, local(): near = [lax.ppermute(piece, 'blk', inside) for piece in near]  2.79 us
  transfers between devices with their start and end apart: 11, of which 5 were waited for; matrix products, arithmetic and copies ran while one was open for 2% of the time, Pallas kernels for 36%

profile of v1, /device:TPU:0, one launch (start us, length us, event | category | flops | bytes accessed | tf_op | source)
XLA Modules:
  0.0 88.7 jit_solution(2025872463539399523)
XLA Ops:
  0.6 0.0 copy-start.9
  0.6 0.0 copy-start
  0.7 0.0 copy-start.1
  0.7 0.0 copy-start.2
  0.7 0.0 copy-start.3
  0.7 0.0 copy-start.4
  0.7 0.0 copy-start.6
  0.7 0.0 copy-start.7
  0.7 1.6 %collective-permute-start.4 = (f32[400,2048]{1,0:T(8,128)}, f32[400,2048]{1,0:T(8,128)S(1)}, u32[]{:S(2)}, u32[]{:S(2)}) collective-permute-start(f32[400,2048]{1,0:T(8,128)} %bitcast.18), channel_id=1, source_target_pairs={{2,4},{6,8},{10,12},{14,16},{18,20},{22,24},{26,28},{30,0},{3,5},{... | collective-permute-start | bytes 9830408 | tf_op jit(solution)/shard_map/ppermute | solution.py:616
  2.3 2.2 %fusion = (f32[400,1024]{1,0:T(8,128)S(1)}, f32[400,1024]{1,0:T(8,128)S(1)}) fusion(f32[400,2048]{1,0:T(8,128)} %bitcast.19), kind=kLoop, calls=%fused_computation | loop fusion | bytes 6553600 | tf_op jit(solution)/shard_map/slice | solution.py:617
  4.4 0.0 copy-start.5
  4.4 5.9 %collective-permute-start.2 = (f32[400,1024]{1,0:T(8,128)S(1)}, f32[400,1024]{1,0:T(8,128)S(1)}, u32[]{:S(2)}, u32[]{:S(2)}) collective-permute-start(f32[400,1024]{1,0:T(8,128)S(1)} %get-tuple-element.123), channel_id=1, source_target_pairs={{0,2},{4,6},{8,10},{12,14},{16,18},{20,22},{24,26},{28,30},{1,3},{... | collective-permute-start | bytes 4915208 | tf_op jit(solution)/shard_map/ppermute | solution.py:617
  10.3 1.4 %collective-permute-start.1 = (f32[400,1024]{1,0:T(8,128)S(1)}, f32[400,1024]{1,0:T(8,128)S(1)}, u32[]{:S(2)}, u32[]{:S(2)}) collective-permute-start(f32[400,1024]{1,0:T(8,128)S(1)} %get-tuple-element.124), channel_id=1, source_target_pairs={{0,2},{4,6},{8,10},{12,14},{16,18},{20,22},{24,26},{28,30},{1,3},{... | collective-permute-start | bytes 4915208 | tf_op jit(solution)/shard_map/ppermute | solution.py:617
  11.7 0.0 copy-done.9
  11.8 0.1 collective-permute-start
  11.8 0.0 copy-done
  11.8 0.0 copy-done.1
  11.9 0.0 copy-done.2
  11.9 0.0 copy-done.3
  11.9 0.0 copy-done.4
  11.9 0.0 copy-done.6
  11.9 0.0 copy-done.7
  11.9 3.7 %prepare0.1 = (f32[400,256]{1,0:T(8,128)S(1)}, f32[400,256]{1,0:T(8,128)S(1)}, bf16[400,256]{1,0:T(8,128)(2,1)S(1)}, bf16[256,400]{1,0:T(8,128)(2,1)S(1)}, bf16[...) custom-call(f32[400,2048]{1,0:T(8,128)S(1)} %bitcast.9, ...), custom_call_target="tpu_custom_call" | custom-call | flops 1000000 | bytes 100000 | tf_op jit(solution)/shard_map/prepare0/pallas_call | solution.py:324
  15.7 0.0 collective-permute-done
  15.7 0.0 collective-permute-done.2.refs_16_
  15.7 0.0 collective-permute-done.1.refs_15_
  15.7 0.0 copy-done.5
  15.7 0.2 first_near.1
  15.9 1.3 %collective-permute-start.7 = (f32[408,1280]{1,0:T(8,128)S(1)}, f32[408,1280]{1,0:T(8,128)S(1)}, u32[]{:S(2)}, u32[]{:S(2)}) collective-permute-start(f32[408,1280]{1,0:T(8,128)S(1)} %get-tuple-element.91), channel_id=1, source_target_pairs={{2,4},{6,8},{10,12},{14,16},{18,20},{22,24},{26,28},{30,0},{3,5},{... | collective-permute-start | bytes 6266888 | tf_op jit(solution)/shard_map/ppermute | solution.py:624
  17.2 3.5 %collective-permute-start.3 = (f32[2048]{0:T(1024)S(1)}, f32[2048]{0:T(1024)S(1)}, u32[]{:S(2)}, u32[]{:S(2)}) collective-permute-start(f32[2048]{0:T(1024)S(1)} %collective-permute-done), channel_id=1, source_target_pairs={{0,4},{4,8},{8,12},{12,16},{16,20},{20,24},{24,28},{28,0},{1,5},{5... | collective-permute-start | bytes 24584 | tf_op jit(solution)/shard_map/ppermute | solution.py:619
  20.7 4.9 %collective-permute-done.3 = f32[2048]{0:T(1024)S(1)} collective-permute-done((f32[2048]{0:T(1024)S(1)}, f32[2048]{0:T(1024)S(1)}, u32[]{:S(2)}, u32[]{:S(2)}) %collective-permute-start.3) | collective-permute-done | bytes 8224 | tf_op jit(solution)/shard_map/ppermute | solution.py:619
  25.6 18.7 %collective-permute-done.4.refs_15_ = f32[400,2048]{1,0:T(8,128)S(1)} collective-permute-done((f32[400,2048]{1,0:T(8,128)}, f32[400,2048]{1,0:T(8,128)S(1)}, u32[]{:S(2)}, u32[]{:S(2)}) %collective-permute-start.4) | collective-permute-done | bytes 3276832 | tf_op jit(solution)/shard_map/ppermute | solution.py:616
  44.3 10.3 %first_far.1 = (f32[400,2048]{1,0:T(8,128)S(1)}, f32[1,2048]{1,0:T(1,128)S(1)}, f32[32,400]{1,0:T(8,128)S(1)}, f32[408,1024]{1,0:T(8,128)S(1)}, f32[400,1024]{1,0:T(8,128)S(1)}) custom-call(f32[400,2048]{1,0:T(8,128)S(1)} %bitcast.11, f32[1,2048]{1,0:T(1,128)S(1)} %get-tuple-element.74.refs_1_, ...), custom_call_target="tpu_custom_call", output_to_operand_aliasing={{0}: (16, {})} | custom-call | flops 1000000 | bytes 100000 | tf_op jit(solution)/shard_map/first_far/pallas_call | solution.py:324
  54.7 1.4 %collective-permute-start.8 = (f32[408,1024]{1,0:T(8,128)S(1)}, f32[408,1024]{1,0:T(8,128)S(1)}, u32[]{:S(2)}, u32[]{:S(2)}) collective-permute-start(f32[408,1024]{1,0:T(8,128)S(1)} %get-tuple-element.94), channel_id=1, source_target_pairs={{0,2},{4,6},{8,10},{12,14},{16,18},{20,22},{24,26},{28,30},{1,3},{... | collective-permute-start | bytes 5013512 | tf_op jit(solution)/shard_map/ppermute | solution.py:628
  56.1 1.4 %collective-permute-start.9 = (f32[400,1024]{1,0:T(8,128)S(1)}, f32[400,1024]{1,0:T(8,128)S(1)}, u32[]{:S(2)}, u32[]{:S(2)}) collective-permute-start(f32[400,1024]{1,0:T(8,128)S(1)} %get-tuple-element.95), channel_id=1, source_target_pairs={{0,2},{4,6},{8,10},{12,14},{16,18},{20,22},{24,26},{28,30},{1,3},{... | collective-permute-start | bytes 4915208 | tf_op jit(solution)/shard_map/ppermute | solution.py:628
  57.5 1.3 %collective-permute-start.6 = (f32[400,512]{1,0:T(8,128)S(1)}, f32[400,512]{1,0:T(8,128)S(1)}, u32[]{:S(2)}, u32[]{:S(2)}) collective-permute-start(f32[400,512]{1,0:T(8,128)S(1)} %get-tuple-element.90), channel_id=1, source_target_pairs={{2,4},{6,8},{10,12},{14,16},{18,20},{22,24},{26,28},{30,0},{3,5},{... | collective-permute-start | bytes 2457608 | tf_op jit(solution)/shard_map/ppermute | solution.py:624
  58.8 1.3 %collective-permute-start.5 = (f32[400,256]{1,0:T(8,128)S(1)}, f32[400,256]{1,0:T(8,128)S(1)}, u32[]{:S(2)}, u32[]{:S(2)}) collective-permute-start(f32[400,256]{1,0:T(8,128)S(1)} %get-tuple-element.79), channel_id=1, source_target_pairs={{2,4},{6,8},{10,12},{14,16},{18,20},{22,24},{26,28},{30,0},{3,5},{... | collective-permute-start | bytes 1228808 | tf_op jit(solution)/shard_map/ppermute | solution.py:624
  60.1 3.7 %prepare1.1 = (f32[400,256]{1,0:T(8,128)S(1)}, f32[400,256]{1,0:T(8,128)S(1)}, bf16[400,256]{1,0:T(8,128)(2,1)S(1)}, bf16[256,400]{1,0:T(8,128)(2,1)S(1)}, bf16[...) custom-call(f32[400,2048]{1,0:T(8,128)S(1)} %get-tuple-element.77.le, ...), custom_call_target="tpu_custom_call" | custom-call | flops 1000000 | bytes 100000 | tf_op jit(solution)/shard_map/prepare1/pallas_call | solution.py:324
  63.8 0.0 collective-permute-done.9.refs_16_
  63.8 0.0 collective-permute-done.8.refs_15_
  63.8 0.4 last_near.1
  64.2 2.5 %collective-permute-done.7.refs_0_ = f32[408,1280]{1,0:T(8,128)S(1)} collective-permute-done((f32[408,1280]{1,0:T(8,128)S(1)}, f32[408,1280]{1,0:T(8,128)S(1)}, u32[]{:S(2)}, u32[]{:S(2)}) %collective-permute-start.7) | collective-permute-done | bytes 2088992 | tf_op jit(solution)/shard_map/ppermute | solution.py:624
  66.7 2.5 %last_piece0.1 = (f32[400,256]{1,0:T(8,128)S(1)}, f32[400,256]{1,0:T(8,128)S(1)}, f32[400,1280]{1,0:T(8,128)S(1)}) custom-call(f32[408,1280]{1,0:T(8,128)S(1)} %collective-permute-done.7.refs_0_, bf16[400,256]{1,0:T(8,128)(2,1)S(1)} %get-tuple-element.82.refs_6_.refs_1_.refs_3_, bf16[256,400]{1,0:T(8,128)(2,1)S(1)} %get-tuple-element.83.refs_7_.refs_2_.refs_4_, ...), custom_call_target="tpu_custom_call" | custom-call | flops 1000000 | bytes 100000 | tf_op jit(solution)/shard_map/last_piece0/pallas_call | solution.py:324
  69.2 2.3 %early_edges0.1 = (bf16[800,256]{1,0:T(8,128)(2,1)S(1)}, f32[256,400]{1,0:T(8,128)}) custom-call(f32[400,256]{1,0:T(8,128)S(1)} %get-tuple-element.80.refs_4_.refs_0_.refs_1_, f32[400,256]{1,0:T(8,128)S(1)} %get-tuple-element.81.refs_5_.refs_1_.refs_2_, f32[400,256]{1,0:T(8,128)S(1)} %get-tuple-element.97.refs_2_.refs_5_, ...), custom_call_target="tpu_custom_call" | custom-call | flops 1000000 | bytes 100000 | tf_op jit(solution)/shard_map/early_edges0/pallas_call | solution.py:324
  71.5 1.9 %early_right0.1 = (f32[400,2048]{1,0:T(8,128)}, f32[1,2048]{1,0:T(1,128)S(1)}) custom-call(f32[408,1280]{1,0:T(8,128)S(1)} %collective-permute-done.7.refs_0_, f32[400,1280]{1,0:T(8,128)S(1)} %get-tuple-element.99.refs_1_, bf16[800,256]{1,0:T(8,128)(2,1)S(1)} %get-tuple-element.100.refs_2_, ...), custom_call_target="tpu_custom_call", output_to_operand_aliasing={{0}: (4, {})} | custom-call | flops 1000000 | bytes 100000 | tf_op jit(solution)/shard_map/early_right0/pallas_call | solution.py:324
  73.4 2.1 %collective-permute-done.6.refs_0_ = f32[400,512]{1,0:T(8,128)S(1)} collective-permute-done((f32[400,512]{1,0:T(8,128)S(1)}, f32[400,512]{1,0:T(8,128)S(1)}, u32[]{:S(2)}, u32[]{:S(2)}) %collective-permute-start.6) | collective-permute-done | bytes 819232 | tf_op jit(solution)/shard_map/ppermute | solution.py:624
  75.5 1.2 %last_piece1.1 = (f32[400,256]{1,0:T(8,128)S(1)}, f32[400,256]{1,0:T(8,128)S(1)}, f32[400,512]{1,0:T(8,128)S(1)}) custom-call(f32[400,512]{1,0:T(8,128)S(1)} %collective-permute-done.6.refs_0_, bf16[400,256]{1,0:T(8,128)(2,1)S(1)} %get-tuple-element.82.refs_6_.refs_1_.refs_3_, ...), custom_call_target="tpu_custom_call", output_to_operand_aliasing={{0}: (5, {}), {1}: (6, {})} | custom-call | flops 1000000 | bytes 100000 | tf_op jit(solution)/shard_map/last_piece1/pallas_call | solution.py:324
  76.7 1.5 %early_edges1.1 = (bf16[800,256]{1,0:T(8,128)(2,1)S(1)}, f32[256,400]{1,0:T(8,128)S(1)}) custom-call(f32[400,256]{1,0:T(8,128)S(1)} %get-tuple-element.80.refs_4_.refs_0_.refs_1_, f32[400,256]{1,0:T(8,128)S(1)} %get-tuple-element.81.refs_5_.refs_1_.refs_2_, f32[400,256]{1,0:T(8,128)S(1)} %get-tuple-element.103.refs_2_.refs_12_, ...), custom_call_target="tpu_custom_call" | custom-call | flops 1000000 | bytes 100000 | tf_op jit(solution)/shard_map/early_edges1/pallas_call | solution.py:324
  78.2 1.5 %early_right1.1 = (f32[400,2048]{1,0:T(8,128)}, f32[1,2048]{1,0:T(1,128)S(1)}) custom-call(f32[400,512]{1,0:T(8,128)S(1)} %collective-permute-done.6.refs_0_, f32[400,512]{1,0:T(8,128)S(1)} %get-tuple-element.107.refs_1_, bf16[800,256]{1,0:T(8,128)(2,1)S(1)} %get-tuple-element.108.refs_2_, ...), custom_call_target="tpu_custom_call", output_to_operand_aliasing={{0}: (5, {})} | custom-call | flops 1000000 | bytes 100000 | tf_op jit(solution)/shard_map/early_right1/pallas_call | solution.py:324
  79.7 0.2 collective-permute-done.5.refs_0_.refs_8_
  79.9 2.4 %late_edges.1 = (f32[400,256]{1,0:T(8,128)S(1)}, bf16[800,256]{1,0:T(8,128)(2,1)S(1)}, bf16[800,256]{1,0:T(8,128)(2,1)S(1)}, f32[32,400]{1,0:T(8,128)S(1)}, bf16...) custom-call(f32[400,256]{1,0:T(8,128)S(1)} %collective-permute-done.5.refs_0_.refs_8_, ...), custom_call_target="tpu_custom_call", output_to_operand_aliasing={{3}: (15, {})} | custom-call | flops 1000000 | bytes 100000 | tf_op jit(solution)/shard_map/late_edges/pallas_call | solution.py:324
  82.3 0.7 ahead_left.1
  82.9 2.0 %collective-permute-start.10 = (f32[32,400]{1,0:T(8,128)S(1)}, f32[32,400]{1,0:T(8,128)S(1)}, u32[]{:S(2)}, u32[]{:S(2)}) collective-permute-start(f32[32,400]{1,0:T(8,128)S(1)} %get-tuple-element.122.rest_0_), channel_id=1, source_target_pairs={{0,1},{1,0},{2,3},{3,2},{4,5},{5,4},{6,7},{7,6},{8,9},{9,8},{10,11... | collective-permute-start | bytes 153608 | tf_op jit(solution)/shard_map/ppermute | solution.py:646
  84.9 0.0 copy-start.8
  84.9 3.0 %late_slabs.1 = (f32[400,2048]{1,0:T(8,128)}, f32[400,2048]{1,0:T(8,128)}) custom-call(f32[400,2048]{1,0:T(8,128)S(1)} %get-tuple-element.77.left.refs_0_, f32[1,2048]{1,0:T(1,128)S(1)} %get-tuple-element.78.refs_1_, bf16[800,256]{1,0:T(8,128)(2,1)S(1)} %get-tuple-element.111.refs_2_, ...), custom_call_target="tpu_custom_call", output_to_operand_aliasing={{0}: (13, {}), {1}: (14, {})} | custom-call | flops 1000000 | bytes 100000 | tf_op jit(solution)/shard_map/late_slabs/pallas_call | solution.py:324
  88.0 0.0 collective-permute-done.10.rest_1_
  88.0 0.0 copy-done.8
  88.0 0.7 relation_update.1
  (1 shorter events, 0.0 us)
Async XLA Ops:
  0.6 11.1 %copy-start.9 = (f32[2048]{0:T(1024)S(1)}, f32[2048]{0:T(1024)}, u32[]{:S(2)}) copy-start(f32[2048]{0:T(1024)} %param.14) | copy-start | bytes 24580
  0.6 11.2 %copy-start = (f32[2048,400]{0,1:T(8,128)S(1)}, f32[2048,400]{0,1:T(8,128)}, u32[]{:S(2)}) copy-start(f32[2048,400]{0,1:T(8,128)} %param.11) | copy-start | bytes 9830404
  0.7 11.2 %copy-start.1 = (f32[32,400]{1,0:T(8,128)S(1)}, f32[32,400]{1,0:T(8,128)}, u32[]{:S(2)}) copy-start(f32[32,400]{1,0:T(8,128)} %relations.5) | copy-start | bytes 153604
  0.7 11.2 %copy-start.2 = (s32[2,256]{1,0:T(2,128)S(1)}, s32[2,256]{1,0:T(2,128)}, u32[]{:S(2)}) copy-start(s32[2,256]{1,0:T(2,128)} %refs_10_.1) | copy-start | bytes 6148
  0.7 11.2 %copy-start.3 = (s32[2,1000]{1,0:T(2,128)S(1)}, s32[2,1000]{1,0:T(2,128)}, u32[]{:S(2)}) copy-start(s32[2,1000]{1,0:T(2,128)} %nsrc.3) | copy-start | bytes 24004
  0.7 11.2 %copy-start.4 = (s32[2,1000]{1,0:T(2,128)S(1)}, s32[2,1000]{1,0:T(2,128)}, u32[]{:S(2)}) copy-start(s32[2,1000]{1,0:T(2,128)} %ndst.3) | copy-start | bytes 24004
  0.7 11.2 %copy-start.6 = (s32[2,256]{1,0:T(2,128)S(1)}, s32[2,256]{1,0:T(2,128)}, u32[]{:S(2)}) copy-start(s32[2,256]{1,0:T(2,128)} %src.3) | copy-start | bytes 6148
  0.7 11.2 %copy-start.7 = (s32[2,256]{1,0:T(2,128)S(1)}, s32[2,256]{1,0:T(2,128)}, u32[]{:S(2)}) copy-start(s32[2,256]{1,0:T(2,128)} %rid.3) | copy-start | bytes 6148
  0.7 43.6 %collective-permute-start.4 = (f32[400,2048]{1,0:T(8,128)}, f32[400,2048]{1,0:T(8,128)S(1)}, u32[]{:S(2)}, u32[]{:S(2)}) collective-permute-start(f32[400,2048]{1,0:T(8,128)} %bitcast.18), channel_id=1, source_target_pairs={{2,4},{6,8},{10,12},{14,16},{18,20},{22,24},{26,28},{30,0},{3,5},{... | collective-permute-start | bytes 9830408 | tf_op jit(solution)/shard_map/ppermute | solution.py:616
  4.4 11.3 %copy-start.5 = (f32[2048]{0:T(1024)S(1)}, f32[2048]{0:T(1024)}, u32[]{:S(2)}) copy-start(f32[2048]{0:T(1024)} %param.12) | copy-start | bytes 24580
  4.4 11.3 %collective-permute-start.2 = (f32[400,1024]{1,0:T(8,128)S(1)}, f32[400,1024]{1,0:T(8,128)S(1)}, u32[]{:S(2)}, u32[]{:S(2)}) collective-permute-start(f32[400,1024]{1,0:T(8,128)S(1)} %get-tuple-element.123), channel_id=1, source_target_pairs={{0,2},{4,6},{8,10},{12,14},{16,18},{20,22},{24,26},{28,30},{1,3},{... | collective-permute-start | bytes 4915208 | tf_op jit(solution)/shard_map/ppermute | solution.py:617
  10.3 5.4 %collective-permute-start.1 = (f32[400,1024]{1,0:T(8,128)S(1)}, f32[400,1024]{1,0:T(8,128)S(1)}, u32[]{:S(2)}, u32[]{:S(2)}) collective-permute-start(f32[400,1024]{1,0:T(8,128)S(1)} %get-tuple-element.124), channel_id=1, source_target_pairs={{0,2},{4,6},{8,10},{12,14},{16,18},{20,22},{24,26},{28,30},{1,3},{... | collective-permute-start | bytes 4915208 | tf_op jit(solution)/shard_map/ppermute | solution.py:617
  11.8 4.0 %collective-permute-start = (f32[2048]{0:T(1024)S(1)}, f32[2048]{0:T(1024)S(1)}, u32[]{:S(2)}, u32[]{:S(2)}) collective-permute-start(f32[2048]{0:T(1024)S(1)} %copy-done.9), channel_id=1, source_target_pairs={{0,2},{4,6},{8,10},{12,14},{16,18},{20,22},{24,26},{28,30},{2,0},{... | collective-permute-start | bytes 24584 | tf_op jit(solution)/shard_map/ppermute | solution.py:618
  15.9 50.8 %collective-permute-start.7 = (f32[408,1280]{1,0:T(8,128)S(1)}, f32[408,1280]{1,0:T(8,128)S(1)}, u32[]{:S(2)}, u32[]{:S(2)}) collective-permute-start(f32[408,1280]{1,0:T(8,128)S(1)} %get-tuple-element.91), channel_id=1, source_target_pairs={{2,4},{6,8},{10,12},{14,16},{18,20},{22,24},{26,28},{30,0},{3,5},{... | collective-permute-start | bytes 6266888 | tf_op jit(solution)/shard_map/ppermute | solution.py:624
  17.2 8.4 %collective-permute-start.3 = (f32[2048]{0:T(1024)S(1)}, f32[2048]{0:T(1024)S(1)}, u32[]{:S(2)}, u32[]{:S(2)}) collective-permute-start(f32[2048]{0:T(1024)S(1)} %collective-permute-done), channel_id=1, source_target_pairs={{0,4},{4,8},{8,12},{12,16},{16,20},{20,24},{24,28},{28,0},{1,5},{5... | collective-permute-start | bytes 24584 | tf_op jit(solution)/shard_map/ppermute | solution.py:619
  54.7 9.2 %collective-permute-start.8 = (f32[408,1024]{1,0:T(8,128)S(1)}, f32[408,1024]{1,0:T(8,128)S(1)}, u32[]{:S(2)}, u32[]{:S(2)}) collective-permute-start(f32[408,1024]{1,0:T(8,128)S(1)} %get-tuple-element.94), channel_id=1, source_target_pairs={{0,2},{4,6},{8,10},{12,14},{16,18},{20,22},{24,26},{28,30},{1,3},{... | collective-permute-start | bytes 5013512 | tf_op jit(solution)/shard_map/ppermute | solution.py:628
  56.1 7.8 %collective-permute-start.9 = (f32[400,1024]{1,0:T(8,128)S(1)}, f32[400,1024]{1,0:T(8,128)S(1)}, u32[]{:S(2)}, u32[]{:S(2)}) collective-permute-start(f32[400,1024]{1,0:T(8,128)S(1)} %get-tuple-element.95), channel_id=1, source_target_pairs={{0,2},{4,6},{8,10},{12,14},{16,18},{20,22},{24,26},{28,30},{1,3},{... | collective-permute-start | bytes 4915208 | tf_op jit(solution)/shard_map/ppermute | solution.py:628
  57.5 18.0 %collective-permute-start.6 = (f32[400,512]{1,0:T(8,128)S(1)}, f32[400,512]{1,0:T(8,128)S(1)}, u32[]{:S(2)}, u32[]{:S(2)}) collective-permute-start(f32[400,512]{1,0:T(8,128)S(1)} %get-tuple-element.90), channel_id=1, source_target_pairs={{2,4},{6,8},{10,12},{14,16},{18,20},{22,24},{26,28},{30,0},{3,5},{... | collective-permute-start | bytes 2457608 | tf_op jit(solution)/shard_map/ppermute | solution.py:624
  58.8 21.1 %collective-permute-start.5 = (f32[400,256]{1,0:T(8,128)S(1)}, f32[400,256]{1,0:T(8,128)S(1)}, u32[]{:S(2)}, u32[]{:S(2)}) collective-permute-start(f32[400,256]{1,0:T(8,128)S(1)} %get-tuple-element.79), channel_id=1, source_target_pairs={{2,4},{6,8},{10,12},{14,16},{18,20},{22,24},{26,28},{30,0},{3,5},{... | collective-permute-start | bytes 1228808 | tf_op jit(solution)/shard_map/ppermute | solution.py:624
  82.9 5.0 %collective-permute-start.10 = (f32[32,400]{1,0:T(8,128)S(1)}, f32[32,400]{1,0:T(8,128)S(1)}, u32[]{:S(2)}, u32[]{:S(2)}) collective-permute-start(f32[32,400]{1,0:T(8,128)S(1)} %get-tuple-element.122.rest_0_), channel_id=1, source_target_pairs={{0,1},{1,0},{2,3},{3,2},{4,5},{5,4},{6,7},{7,6},{8,9},{9,8},{10,11... | collective-permute-start | bytes 153608 | tf_op jit(solution)/shard_map/ppermute | solution.py:646
  84.9 3.0 %copy-start.8 = (f32[32]{0:T(128)S(1)}, f32[32]{0:T(128)}, u32[]{:S(2)}) copy-start(f32[32]{0:T(128)} %param.16) | copy-start | bytes 388

commit v2 on v1

--- a/solution.py
+++ b/solution.py
@@ -263,7 +263,7 @@
     return found
 
 
-def train(parity, number, last, fixed, kept, takes, gives, *refs):
+def train(parity, number, last, fixed, kept, takes, gives, packs, *refs):
     refs = list(refs)
     (left, lstate, rstate_in, rel_in) = refs[:4]
     (weight, source, query, query_rows, left16, oh_src, oh_dst, count_l, count_r, kind, _rows) = refs[4:15]
@@ -271,7 +271,8 @@
     refs = refs[15 + takes + kept :]
     left_out, lstate_out, rel_out = refs[:3]
     right_out = refs[3 : 3 + len(gives)]
-    (target, gq, rgrad, probe, probe_rows, gp, lgrad, to_src, to_dst, rstate, spare, sems) = refs[3 + len(gives) :]
+    state_out = refs[3 + len(gives)]
+    (target, gq, rgrad, probe, probe_rows, gp, lgrad, to_src, to_dst, rstate, spare, sems) = refs[4 + len(gives) :]
     depth, rows = left.shape
     lstate_out[...] = lstate[...]
     rel_out[...] = rel_in[...]
@@ -298,7 +299,10 @@
                     cut = slice(begin, begin + length)
                     here = slice(begin - at, begin - at + length)
                     adagrad(old, rstate_in.at[:, cut], rgrad.at[:, cut], to_dst, oh_dst, begin, out.at[:, here], spare.at[:, cut])
-            pack_state(spare, right_out[STATE], depth)
+            if packs:
+                pack_state(spare, right_out[STATE], depth)
+            else:
+                state_out[...] = spare[...]
             adagrad(left, lstate, lgrad, to_src, oh_src, 0, left_out, lstate_out)
 
 
@@ -342,28 +346,28 @@
     )
 
 
-def trained(parity, name, number, fixed, gives, left, lstate, right, rstate, rel, ready, keep=()):
+def trained(parity, name, number, fixed, gives, left, lstate, right, rstate, rel, ready, keep=(), packs=False, after=()):
     depth, rows = left.shape
     edges = ready[0].shape[1]
     last = not gives
     blocks = [shape(depth, size) for _at, size in pieces_of(rows, gives or (8,))]
-    if not last:
+    if packs:
         blocks[STATE] = shape(depth + 8, blocks[STATE].shape[1])
     edge = shape(depth, edges)
     edge16 = shape(depth, edges, dtype=BF16)
     pair16 = shape(2 * depth, edges, dtype=BF16)
     slab = shape(depth, rows)
     inner = [edge, edge, slab, edge16, shape(edges, depth, dtype=BF16), edge, slab, pair16, pair16, shape(1, rows), shape(1, rows)]
-    left_out, lstate_out, rel_out, *right_out = call(
-        functools.partial(train, parity, number, last, fixed, len(keep), len(right), gives or (8,)),
+    left_out, lstate_out, rel_out, *right_out, state_out = call(
+        functools.partial(train, parity, number, last, fixed, len(keep) + len(after), len(right), gives or (8,), packs),
         name,
-        [left, lstate, rstate, rel, *ready, *right, *keep],
-        [slab, shape(1, rows), shape(*rel.shape), *blocks],
+        [left, lstate, rstate, rel, *ready, *right, *keep, *after],
+        [slab, shape(1, rows), shape(*rel.shape), *blocks, shape(1, rows)],
         out_large=(0, 3) if last else (),
         scratch_shapes=[*scratch(inner), pltpu.SemaphoreType.DMA((2, rows // 256))],
         aliases={15 + len(right) + i: 0 for i in range(len(keep))},
     )
-    return left_out, lstate_out, right_out, rel_out
+    return left_out, lstate_out, right_out, rel_out, state_out
 
 
 def only_on(parity, body):
@@ -425,24 +429,17 @@
     )
 
 
-def early_right(parity, name, at, piece, state, rgrad, to_dst, oh_dst, keep):
+def early_right(parity, name, at, piece, state, rgrad, to_dst, oh_dst, keep, order):
     depth, rows = keep.shape
 
-    def body(piece, rgrad, to_dst, oh_dst, *rest):
-        out, new_state, spare, sems = rest[-4:]
-        if state is None:
-            unpack_state(piece, depth, new_state)
-        else:
-            new_state[...] = rest[0][...]
-        update_and_send([piece], new_state, [rgrad], to_dst, oh_dst, spare, out, sems, fixed=True, start=at)()
-
-    operands = [piece, rgrad, to_dst, oh_dst, *([] if state is None else [state]), keep]
-    place = len(operands) - 1
+    def body(piece, state, rgrad, to_dst, oh_dst, _order, _keep, out, _order_out, spare, sems):
+        update_and_send([piece], state, [rgrad], to_dst, oh_dst, spare, out, sems, fixed=True, start=at)()
+
     return call(
-        only_on(parity, body), name, operands, [shape(depth, rows), shape(1, rows)],
-        in_large=(place,), out_large=(0,),
+        only_on(parity, body), name, [piece, state, rgrad, to_dst, oh_dst, order, keep], [shape(depth, rows), shape(*order.shape)],
+        in_large=(6,), out_large=(0,),
         scratch_shapes=[*scratch([shape(1, rows)]), pltpu.SemaphoreType.DMA((rows // 256,))],
-        aliases={place: 0},
+        aliases={5: 1, 6: 0},
     )
 
 
@@ -495,7 +492,7 @@
 
 
 def ahead_rows(rows):
-    return rows // 4
+    return rows // 8 * 3
 
 
 def first_along_rel():
@@ -527,26 +524,22 @@
         def made_ahead():
             return pltpu.make_async_copy(ahead, left_out.at[:, 0 : ahead_rows(rows)], sems.at[0, 0])
 
-        def copy(i):
-            cut = slice(i * 256, (i + 1) * 256)
-            return pltpu.make_async_copy(result.at[:, cut], left_out.at[:, cut], sems.at[0, i])
-
-        def make(i):
-            cut = slice(i * 256, (i + 1) * 256)
+        def runs(start, stop):
+            out = []
+            while start < stop:
+                size = 512 if start % 512 == 0 and start + 512 <= stop else 256
+                out.append(slice(start, start + size))
+                start += size
+            return out
+
+        def copy(cut):
+            return pltpu.make_async_copy(result.at[:, cut], left_out.at[:, cut], sems.at[0, cut.start // 256])
+
+        def make(cut):
             result[:, cut] = left_rows(cut, left, lstate, to_src, oh_src, probe, weights, count_l)
-
-        count = rows // 256
-        first = ahead_rows(rows) // 256
-
-        @pl.when(jnp.logical_not(first_along_rel()))
-        def _():
-            for i in range(first):
-                make(i)
-
-        half = (count + first) // 2
-        for i in range(first, half):
-            make(i)
-        wait = update_and_send([piece], state, [rgrad], to_dst, oh_dst, spare, right_out, sems.at[1], fixed=True, start=at)
+            copy(cut).start()
+
+        first, others = runs(0, ahead_rows(rows)), runs(ahead_rows(rows), rows)
 
         @pl.when(first_along_rel())
         def _():
@@ -554,14 +547,12 @@
 
         @pl.when(jnp.logical_not(first_along_rel()))
         def _():
-            for i in range(first):
-                copy(i).start()
-
-        for i in range(first, half):
-            copy(i).start()
-        for i in range(half, count):
-            make(i)
-            copy(i).start()
+            for cut in first:
+                make(cut)
+
+        wait = update_and_send([piece], state, [rgrad], to_dst, oh_dst, spare, right_out, sems.at[1], fixed=True, start=at)
+        for cut in others:
+            make(cut)
         wait()
 
         @pl.when(first_along_rel())
@@ -570,11 +561,11 @@
 
         @pl.when(jnp.logical_not(first_along_rel()))
         def _():
-            for i in range(first):
-                copy(i).wait()
-
-        for i in range(first, count):
-            copy(i).wait()
+            for cut in first:
+                copy(cut).wait()
+
+        for cut in others:
+            copy(cut).wait()
 
     operands = [left, lstate, to_src, oh_src, probe, weights, count_l, ahead, piece, state, rgrad, to_dst, oh_dst, keep_left, keep_right]
     return call(
@@ -604,8 +595,9 @@
 ):
     peers = lax.axis_size("blk")
     inside = [(i, i + 1) for i in range(0, peers, 2)]
-    swap = inside + [(i + 1, i) for i in range(0, peers, 2)]
     across = [(i, (i + 1) % peers) for i in range(1, peers, 2)]
+    back = [(i + 1, i) for i in range(0, peers, 2)]
+    swap = inside + back
     skip = [(i, (i + 2) % peers) for i in range(0, peers, 2)]
     index = (src_index, dst_index, relation_id, neg_source, neg_target)
     left = left_slab.T
@@ -620,27 +612,27 @@
     state_near = state_near.reshape(1, rows)
     rel = jnp.zeros(relations.shape, F32)
     ready = prepared(0, left, relations, index)
-    left_a, lstate, far, rel = trained(1, "first_near", number, False, FAR, left, lstate, right_near, state_near, rel, ready)
+    left_a, lstate, far, rel, state = trained(1, "first_near", number, False, FAR, left, lstate, right_near, state_near, rel, ready)
     far = [lax.ppermute(piece, "blk", across) for piece in far]
-    left_a, lstate, near, rel = trained(
-        0, "first_far", number, True, NEAR, left, lstate, [right_far], state_far, rel, ready, (left_a,)
+    state = lax.ppermute(lax.ppermute(state, "blk", back), "blk", skip)
+    left_a, lstate, near, rel, _ = trained(
+        0, "first_far", number, True, NEAR, left, lstate, [right_far], state_far, rel, ready, (left_a,), True, (state,)
     )
     near = [lax.ppermute(piece, "blk", inside) for piece in near]
     ready = prepared(1, left_a, relations, index)
     first_lstate = lstate
-    left_b, lstate, right_b, rel = trained(1, "last_near", number, False, (), left_a, lstate, near, state_near, rel, ready)
+    left_b, lstate, right_b, rel, _ = trained(1, "last_near", number, False, (), left_a, lstate, near, state_near, rel, ready)
     cuts = pieces_of(rows, FAR)
     right_b, = right_b
     held = ()
-    state = None
+    order = lstate
     for i, (at, size) in enumerate(cuts[:-1]):
-        after = lstate if state is None else state
-        target, gq, rgrad = last_piece(0, "last_piece%d" % i, number, at, far[i], ready, after, held)
+        target, gq, rgrad = last_piece(0, "last_piece%d" % i, number, at, far[i], ready, order, held)
         held = (target, gq)
         to_dst, target_rows = early_edges(0, "early_edges%d" % i, number, 1, at, at + size, target, ready, dst_index)
-        right_b, state = early_right(0, "early_right%d" % i, at, far[i], state, rgrad, to_dst, ready[6], right_b)
+        right_b, order = early_right(0, "early_right%d" % i, at, far[i], state, rgrad, to_dst, ready[6], right_b, order)
     at = cuts[-1][0]
-    rgrad, to_src, to_dst, rel, probe, weights = late_edges(0, number, 1, at, far[-1], ready, dst_index, target, target_rows, gq, rel, state)
+    rgrad, to_src, to_dst, rel, probe, weights = late_edges(0, number, 1, at, far[-1], ready, dst_index, target, target_rows, gq, rel, order)
     ahead, rel = ahead_left(0, left_a, first_lstate, to_src, ready[5], probe, weights, ready[7], rel)
     if lax.axis_size("rel") == 2:
         rels = [rel, lax.ppermute(rel, "rel", [(0, 1), (1, 0)])]

time: 89 us -> 88.3 us (level)
  waiting for transfers between devices: 28.4 us -> 22.2 us
  starting transfers between devices: 21 us -> 25.6 us
  Pallas kernels: 36.1 us -> 37 us
    ppermute x0 -> x2, waiting for transfers between devices: none -> 16.1 us  [local(): state = lax.ppermute(lax.ppermute(state, 'blk', back), 'blk', skip)]
    ppermute x1, waiting for transfers between devices: 18.7 us -> 2.87 us  [local(): right_far = lax.ppermute(right, 'blk', across)]
    ppermute x1, waiting for transfers between devices: 4.93 us -> 0.01 us  [local(): state_far = lax.ppermute(state_near, 'blk', skip).reshape(1, rows)]
    ppermute x0 -> x2, starting transfers between devices: none -> 4.74 us  [local(): state = lax.ppermute(lax.ppermute(state, 'blk', back), 'blk', skip)]
    ppermute x3, waiting for transfers between devices: 4.72 us -> 3.14 us  [local(): far = [lax.ppermute(piece, 'blk', across) for piece in far]]
    pallas_call x15, Pallas kernels: 36.1 us -> 37 us  [call(): pl.pallas_call(kernel, out_shape=tuple(shapes), in_specs=[large if i in i...]
  transfers between devices with their start and end apart: 11 -> 13, of which waited for: 5 -> 7; matrix products, arithmetic and copies ran while one was open for 2% -> 2% of each run, Pallas kernels for 36% -> 37%
where the time goes in v2:
time: 88.3 us; the launch traced here: 88 us
  Pallas kernels  37 us (42%)
  starting transfers between devices  25.6 us (29%)
  waiting for transfers between devices  22.2 us (25%)
  local copies, waits for them, and re-layouts  2.21 us (3%)
  between operations  1 us (1%)
    pallas_call x15, Pallas kernels, call(): pl.pallas_call(kernel, out_shape=tuple(shapes), in_specs=[large if i in i...  37 us
    ppermute x2, waiting for transfers between devices, local(): state = lax.ppermute(lax.ppermute(state, 'blk', back), 'blk', skip)  16.1 us
    ppermute x2, starting transfers between devices, local(): lax.ppermute(right[:, at:at + size], 'blk', inside)  7.28 us
    ppermute x2, starting transfers between devices, local(): state = lax.ppermute(lax.ppermute(state, 'blk', back), 'blk', skip)  4.74 us
    ppermute x3, starting transfers between devices, local(): far = [lax.ppermute(piece, 'blk', across) for piece in far]  3.88 us
    ppermute x1, starting transfers between devices, local(): state_far = lax.ppermute(state_near, 'blk', skip).reshape(1, rows)  3.46 us
    ppermute x3, waiting for transfers between devices, local(): far = [lax.ppermute(piece, 'blk', across) for piece in far]  3.14 us
    ppermute x1, waiting for transfers between devices, local(): right_far = lax.ppermute(right, 'blk', across)  2.87 us
  transfers between devices with their start and end apart: 13, of which 7 were waited for; matrix products, arithmetic and copies ran while one was open for 2% of the time, Pallas kernels for 37%

profile of v2, /device:TPU:0, one launch (start us, length us, event | category | flops | bytes accessed | tf_op | source)
XLA Modules:
  0.0 88.0 jit_solution(18237859764484866638)
XLA Ops:
  0.6 0.0 copy-start.9
  0.6 0.0 copy-start
  0.7 0.0 copy-start.1
  0.7 0.0 copy-start.2
  0.7 0.0 copy-start.3
  0.7 0.0 copy-start.4
  0.7 0.0 copy-start.6
  0.7 0.0 copy-start.7
  0.7 1.6 %collective-permute-start.4 = (f32[400,2048]{1,0:T(8,128)}, f32[400,2048]{1,0:T(8,128)S(1)}, u32[]{:S(2)}, u32[]{:S(2)}) collective-permute-start(f32[400,2048]{1,0:T(8,128)} %bitcast.18), channel_id=1, source_target_pairs={{2,4},{6,8},{10,12},{14,16},{18,20},{22,24},{26,28},{30,0},{3,5},{... | collective-permute-start | bytes 9830408 | tf_op jit(solution)/shard_map/ppermute | solution.py:608
  2.3 2.2 %fusion = (f32[400,1024]{1,0:T(8,128)S(1)}, f32[400,1024]{1,0:T(8,128)S(1)}) fusion(f32[400,2048]{1,0:T(8,128)} %bitcast.19), kind=kLoop, calls=%fused_computation | loop fusion | bytes 6553600 | tf_op jit(solution)/shard_map/slice | solution.py:609
  4.4 0.0 copy-start.5
  4.4 5.9 %collective-permute-start.2 = (f32[400,1024]{1,0:T(8,128)S(1)}, f32[400,1024]{1,0:T(8,128)S(1)}, u32[]{:S(2)}, u32[]{:S(2)}) collective-permute-start(f32[400,1024]{1,0:T(8,128)S(1)} %get-tuple-element.125), channel_id=1, source_target_pairs={{0,2},{4,6},{8,10},{12,14},{16,18},{20,22},{24,26},{28,30},{1,3},{... | collective-permute-start | bytes 4915208 | tf_op jit(solution)/shard_map/ppermute | solution.py:609
  10.3 1.4 %collective-permute-start.1 = (f32[400,1024]{1,0:T(8,128)S(1)}, f32[400,1024]{1,0:T(8,128)S(1)}, u32[]{:S(2)}, u32[]{:S(2)}) collective-permute-start(f32[400,1024]{1,0:T(8,128)S(1)} %get-tuple-element.126), channel_id=1, source_target_pairs={{0,2},{4,6},{8,10},{12,14},{16,18},{20,22},{24,26},{28,30},{1,3},{... | collective-permute-start | bytes 4915208 | tf_op jit(solution)/shard_map/ppermute | solution.py:609
  11.7 0.0 copy-done.9
  11.8 0.1 collective-permute-start
  11.8 0.0 copy-done
  11.8 0.0 copy-done.1
  11.9 0.0 copy-done.2
  11.9 0.0 copy-done.3
  11.9 0.0 copy-done.4
  11.9 0.0 copy-done.6
  11.9 0.0 copy-done.7
  11.9 3.7 %prepare0.1 = (f32[400,256]{1,0:T(8,128)S(1)}, f32[400,256]{1,0:T(8,128)S(1)}, bf16[400,256]{1,0:T(8,128)(2,1)S(1)}, bf16[256,400]{1,0:T(8,128)(2,1)S(1)}, bf16[...) custom-call(f32[400,2048]{1,0:T(8,128)S(1)} %bitcast.9, ...), custom_call_target="tpu_custom_call" | custom-call | flops 1000000 | bytes 100000 | tf_op jit(solution)/shard_map/prepare0/pallas_call | solution.py:328
  15.6 0.1 collective-permute-done
  15.7 0.0 collective-permute-done.2.refs_16_
  15.7 0.0 collective-permute-done.1.refs_15_
  15.7 0.0 copy-done.5
  15.7 0.2 first_near.1
  15.9 1.3 %collective-permute-start.9 = (f32[400,1280]{1,0:T(8,128)S(1)}, f32[400,1280]{1,0:T(8,128)S(1)}, u32[]{:S(2)}, u32[]{:S(2)}) collective-permute-start(f32[400,1280]{1,0:T(8,128)S(1)} %get-tuple-element.93), channel_id=1, source_target_pairs={{2,4},{6,8},{10,12},{14,16},{18,20},{22,24},{26,28},{30,0},{3,5},{... | collective-permute-start | bytes 6144008 | tf_op jit(solution)/shard_map/ppermute | solution.py:616
  17.2 1.3 %collective-permute-start.5 = (f32[1,2048]{1,0:T(1,128)S(1)}, f32[1,2048]{1,0:T(1,128)S(1)}, u32[]{:S(2)}, u32[]{:S(2)}) collective-permute-start(f32[1,2048]{1,0:T(1,128)S(1)} %get-tuple-element.78), channel_id=1, source_target_pairs={{2,0},{6,4},{10,8},{14,12},{18,16},{22,20},{26,24},{30,28},{3,1},{... | collective-permute-start | bytes 24584 | tf_op jit(solution)/shard_map/ppermute | solution.py:617
  18.5 3.5 %collective-permute-start.3 = (f32[2048]{0:T(1024)S(1)}, f32[2048]{0:T(1024)S(1)}, u32[]{:S(2)}, u32[]{:S(2)}) collective-permute-start(f32[2048]{0:T(1024)S(1)} %collective-permute-done), channel_id=1, source_target_pairs={{0,4},{4,8},{8,12},{12,16},{16,20},{20,24},{24,28},{28,0},{1,5},{5... | collective-permute-start | bytes 24584 | tf_op jit(solution)/shard_map/ppermute | solution.py:611
  22.0 11.2 %collective-permute-done.5 = f32[1,2048]{1,0:T(1,128)S(1)} collective-permute-done((f32[1,2048]{1,0:T(1,128)S(1)}, f32[1,2048]{1,0:T(1,128)S(1)}, u32[]{:S(2)}, u32[]{:S(2)}) %collective-permute-start.5) | collective-permute-done | bytes 8224 | tf_op jit(solution)/shard_map/ppermute | solution.py:617
  33.2 3.4 %collective-permute-start.6 = (f32[1,2048]{1,0:T(1,128)S(1)}, f32[1,2048]{1,0:T(1,128)S(1)}, u32[]{:S(2)}, u32[]{:S(2)}) collective-permute-start(f32[1,2048]{1,0:T(1,128)S(1)} %collective-permute-done.5), channel_id=1, source_target_pairs={{0,4},{4,8},{8,12},{12,16},{16,20},{20,24},{24,28},{28,0},{1,5},{5... | collective-permute-start | bytes 24584 | tf_op jit(solution)/shard_map/ppermute | solution.py:617
  36.6 0.0 collective-permute-done.3
  36.6 4.9 %collective-permute-done.6.refs_17_.refs_1_.refs_9_ = f32[1,2048]{1,0:T(1,128)S(1)} collective-permute-done((f32[1,2048]{1,0:T(1,128)S(1)}, f32[1,2048]{1,0:T(1,128)S(1)}, u32[]{:S(2)}, u32[]{:S(2)}) %collective-permute-start.6) | collective-permute-done | bytes 8224 | tf_op jit(solution)/shard_map/ppermute | solution.py:617
  41.5 2.9 %collective-permute-done.4.refs_15_ = f32[400,2048]{1,0:T(8,128)S(1)} collective-permute-done((f32[400,2048]{1,0:T(8,128)}, f32[400,2048]{1,0:T(8,128)S(1)}, u32[]{:S(2)}, u32[]{:S(2)}) %collective-permute-start.4) | collective-permute-done | bytes 3276832 | tf_op jit(solution)/shard_map/ppermute | solution.py:608
  44.4 10.9 %first_far.1 = (f32[400,2048]{1,0:T(8,128)S(1)}, f32[1,2048]{1,0:T(1,128)S(1)}, f32[32,400]{1,0:T(8,128)S(1)}, f32[408,1024]{1,0:T(8,128)S(1)}, f32[400,1024]{1,0:T(8,128)S(1)}, /*index=5*/f32[1,2048]{1,0:T(1,128)}) custom-call(f32[400,2048]{1,0:T(8,128)S(1)} %bitcast.11, f32[1,2048]{1,0:T(1,128)S(1)} %get-tuple-element.75.refs_1_, ...), custom_call_target="tpu_custom_call", output_to_operand_aliasing={{0}: (16, {})} | custom-call | flops 1000000 | bytes 100000 | tf_op jit(solution)/shard_map/first_far/pallas_call | solution.py:328
  55.3 1.4 %collective-permute-start.10 = (f32[408,1024]{1,0:T(8,128)S(1)}, f32[408,1024]{1,0:T(8,128)S(1)}, u32[]{:S(2)}, u32[]{:S(2)}) collective-permute-start(f32[408,1024]{1,0:T(8,128)S(1)} %get-tuple-element.96), channel_id=1, source_target_pairs={{0,2},{4,6},{8,10},{12,14},{16,18},{20,22},{24,26},{28,30},{1,3},{... | collective-permute-start | bytes 5013512 | tf_op jit(solution)/shard_map/ppermute | solution.py:621
  56.7 1.4 %collective-permute-start.11 = (f32[400,1024]{1,0:T(8,128)S(1)}, f32[400,1024]{1,0:T(8,128)S(1)}, u32[]{:S(2)}, u32[]{:S(2)}) collective-permute-start(f32[400,1024]{1,0:T(8,128)S(1)} %get-tuple-element.97), channel_id=1, source_target_pairs={{0,2},{4,6},{8,10},{12,14},{16,18},{20,22},{24,26},{28,30},{1,3},{... | collective-permute-start | bytes 4915208 | tf_op jit(solution)/shard_map/ppermute | solution.py:621
  58.1 1.3 %collective-permute-start.8 = (f32[400,512]{1,0:T(8,128)S(1)}, f32[400,512]{1,0:T(8,128)S(1)}, u32[]{:S(2)}, u32[]{:S(2)}) collective-permute-start(f32[400,512]{1,0:T(8,128)S(1)} %get-tuple-element.92), channel_id=1, source_target_pairs={{2,4},{6,8},{10,12},{14,16},{18,20},{22,24},{26,28},{30,0},{3,5},{... | collective-permute-start | bytes 2457608 | tf_op jit(solution)/shard_map/ppermute | solution.py:616
  59.4 1.3 %collective-permute-start.7 = (f32[400,256]{1,0:T(8,128)S(1)}, f32[400,256]{1,0:T(8,128)S(1)}, u32[]{:S(2)}, u32[]{:S(2)}) collective-permute-start(f32[400,256]{1,0:T(8,128)S(1)} %get-tuple-element.81), channel_id=1, source_target_pairs={{2,4},{6,8},{10,12},{14,16},{18,20},{22,24},{26,28},{30,0},{3,5},{... | collective-permute-start | bytes 1228808 | tf_op jit(solution)/shard_map/ppermute | solution.py:616
  60.7 3.7 %prepare1.1 = (f32[400,256]{1,0:T(8,128)S(1)}, f32[400,256]{1,0:T(8,128)S(1)}, bf16[400,256]{1,0:T(8,128)(2,1)S(1)}, bf16[256,400]{1,0:T(8,128)(2,1)S(1)}, bf16[...) custom-call(f32[400,2048]{1,0:T(8,128)S(1)} %get-tuple-element.79.le, ...), custom_call_target="tpu_custom_call" | custom-call | flops 1000000 | bytes 100000 | tf_op jit(solution)/shard_map/prepare1/pallas_call | solution.py:328
  64.4 0.0 collective-permute-done.11.refs_16_
  64.5 0.0 collective-permute-done.10.refs_15_
  64.5 1.0 %last_near.1 = (f32[400,2048]{1,0:T(8,128)}, f32[1,2048]{1,0:T(1,128)S(1)}, f32[32,400]{1,0:T(8,128)S(1)}, f32[400,2048]{1,0:T(8,128)}, f32[1,2048]{1,0:T(1,128)}) custom-call(f32[400,2048]{1,0:T(8,128)S(1)} %get-tuple-element.79.left.refs_0_, f32[1,2048]{1,0:T(1,128)S(1)} %get-tuple-element.80.refs_1_, f32[1,2048]{1,0:T(1,128)S(1)} %bitcast.13, ...), custom_call_target="tpu_custom_call" | custom-call | flops 1000000 | bytes 100000 | tf_op jit(solution)/shard_map/last_near/pallas_call | solution.py:328
  65.5 0.9 %collective-permute-done.9.refs_0_ = f32[400,1280]{1,0:T(8,128)S(1)} collective-permute-done((f32[400,1280]{1,0:T(8,128)S(1)}, f32[400,1280]{1,0:T(8,128)S(1)}, u32[]{:S(2)}, u32[]{:S(2)}) %collective-permute-start.9) | collective-permute-done | bytes 2048032 | tf_op jit(solution)/shard_map/ppermute | solution.py:616
  66.4 2.5 %last_piece0.1 = (f32[400,256]{1,0:T(8,128)S(1)}, f32[400,256]{1,0:T(8,128)S(1)}, f32[400,1280]{1,0:T(8,128)S(1)}) custom-call(f32[400,1280]{1,0:T(8,128)S(1)} %collective-permute-done.9.refs_0_, bf16[400,256]{1,0:T(8,128)(2,1)S(1)} %get-tuple-element.84.refs_6_.refs_1_.refs_3_, bf16[256,400]{1,0:T(8,128)(2,1)S(1)} %get-tuple-element.85.refs_7_.refs_2_.refs_4_, ...), custom_call_target="tpu_custom_call" | custom-call | flops 1000000 | bytes 100000 | tf_op jit(solution)/shard_map/last_piece0/pallas_call | solution.py:328
  68.9 2.3 %early_edges0.1 = (bf16[800,256]{1,0:T(8,128)(2,1)S(1)}, f32[256,400]{1,0:T(8,128)}) custom-call(f32[400,256]{1,0:T(8,128)S(1)} %get-tuple-element.82.refs_4_.refs_0_.refs_1_, f32[400,256]{1,0:T(8,128)S(1)} %get-tuple-element.83.refs_5_.refs_1_.refs_2_, f32[400,256]{1,0:T(8,128)S(1)} %get-tuple-element.99.refs_2_.refs_5_, ...), custom_call_target="tpu_custom_call" | custom-call | flops 1000000 | bytes 100000 | tf_op jit(solution)/shard_map/early_edges0/pallas_call | solution.py:328
  71.2 1.9 %early_right0.1 = (f32[400,2048]{1,0:T(8,128)}, f32[1,2048]{1,0:T(1,128)S(1)}) custom-call(f32[400,1280]{1,0:T(8,128)S(1)} %collective-permute-done.9.refs_0_, f32[1,2048]{1,0:T(1,128)S(1)} %collective-permute-done.6.refs_17_.refs_1_.refs_9_, f32[400,1280]{1,0:T(8,128)S(1)} %get-tuple-element.101.refs_2_, ...), custom_call_target="tpu_custom_call", output_to_operand_aliasing={{1}: (5, {}), {0}: (6, {})} | custom-call | flops 1000000 | bytes 100000 | tf_op jit(solution)/shard_map/early_right0/pallas_call | solution.py:328
  73.0 2.1 %collective-permute-done.8.refs_0_ = f32[400,512]{1,0:T(8,128)S(1)} collective-permute-done((f32[400,512]{1,0:T(8,128)S(1)}, f32[400,512]{1,0:T(8,128)S(1)}, u32[]{:S(2)}, u32[]{:S(2)}) %collective-permute-start.8) | collective-permute-done | bytes 819232 | tf_op jit(solution)/shard_map/ppermute | solution.py:616
  75.1 1.2 %last_piece1.1 = (f32[400,256]{1,0:T(8,128)S(1)}, f32[400,256]{1,0:T(8,128)S(1)}, f32[400,512]{1,0:T(8,128)S(1)}) custom-call(f32[400,512]{1,0:T(8,128)S(1)} %collective-permute-done.8.refs_0_, bf16[400,256]{1,0:T(8,128)(2,1)S(1)} %get-tuple-element.84.refs_6_.refs_1_.refs_3_, ...), custom_call_target="tpu_custom_call", output_to_operand_aliasing={{0}: (5, {}), {1}: (6, {})} | custom-call | flops 1000000 | bytes 100000 | tf_op jit(solution)/shard_map/last_piece1/pallas_call | solution.py:328
  76.4 1.5 %early_edges1.1 = (bf16[800,256]{1,0:T(8,128)(2,1)S(1)}, f32[256,400]{1,0:T(8,128)S(1)}) custom-call(f32[400,256]{1,0:T(8,128)S(1)} %get-tuple-element.82.refs_4_.refs_0_.refs_1_, f32[400,256]{1,0:T(8,128)S(1)} %get-tuple-element.83.refs_5_.refs_1_.refs_2_, f32[400,256]{1,0:T(8,128)S(1)} %get-tuple-element.105.refs_2_.refs_12_, ...), custom_call_target="tpu_custom_call" | custom-call | flops 1000000 | bytes 100000 | tf_op jit(solution)/shard_map/early_edges1/pallas_call | solution.py:328
  77.9 1.5 %early_right1.1 = (f32[400,2048]{1,0:T(8,128)}, f32[1,2048]{1,0:T(1,128)S(1)}) custom-call(f32[400,512]{1,0:T(8,128)S(1)} %collective-permute-done.8.refs_0_, f32[1,2048]{1,0:T(1,128)S(1)} %collective-permute-done.6.refs_17_.refs_1_.refs_9_, f32[400,512]{1,0:T(8,128)S(1)} %get-tuple-element.109.refs_2_, ...), custom_call_target="tpu_custom_call", output_to_operand_aliasing={{1}: (5, {}), {0}: (6, {})} | custom-call | flops 1000000 | bytes 100000 | tf_op jit(solution)/shard_map/early_right1/pallas_call | solution.py:328
  79.4 0.1 collective-permute-done.7.refs_0_.refs_8_
  79.5 2.5 %late_edges.1 = (f32[400,256]{1,0:T(8,128)S(1)}, bf16[800,256]{1,0:T(8,128)(2,1)S(1)}, bf16[800,256]{1,0:T(8,128)(2,1)S(1)}, f32[32,400]{1,0:T(8,128)S(1)}, bf16...) custom-call(f32[400,256]{1,0:T(8,128)S(1)} %collective-permute-done.7.refs_0_.refs_8_, ...), custom_call_target="tpu_custom_call", output_to_operand_aliasing={{3}: (15, {})} | custom-call | flops 1000000 | bytes 100000 | tf_op jit(solution)/shard_map/late_edges/pallas_call | solution.py:328
  82.0 0.9 ahead_left.1
  82.9 1.8 %collective-permute-start.12 = (f32[32,400]{1,0:T(8,128)S(1)}, f32[32,400]{1,0:T(8,128)S(1)}, u32[]{:S(2)}, u32[]{:S(2)}) collective-permute-start(f32[32,400]{1,0:T(8,128)S(1)} %get-tuple-element.124.rest_0_), channel_id=1, source_target_pairs={{0,1},{1,0},{2,3},{3,2},{4,5},{5,4},{6,7},{7,6},{8,9},{9,8},{10,11... | collective-permute-start | bytes 153608 | tf_op jit(solution)/shard_map/ppermute | solution.py:638
  84.7 0.0 copy-start.8
  84.7 2.5 %late_slabs.1 = (f32[400,2048]{1,0:T(8,128)}, f32[400,2048]{1,0:T(8,128)}) custom-call(f32[400,2048]{1,0:T(8,128)S(1)} %get-tuple-element.79.left.refs_0_, f32[1,2048]{1,0:T(1,128)S(1)} %get-tuple-element.80.refs_1_, bf16[800,256]{1,0:T(8,128)(2,1)S(1)} %get-tuple-element.113.refs_2_, ...), custom_call_target="tpu_custom_call", output_to_operand_aliasing={{0}: (13, {}), {1}: (14, {})} | custom-call | flops 1000000 | bytes 100000 | tf_op jit(solution)/shard_map/late_slabs/pallas_call | solution.py:328
  87.2 0.0 collective-permute-done.12.rest_1_
  87.2 0.0 copy-done.8
  87.2 0.7 relation_update.1
  (1 shorter events, 0.0 us)
Async XLA Ops:
  0.6 11.1 %copy-start.9 = (f32[2048]{0:T(1024)S(1)}, f32[2048]{0:T(1024)}, u32[]{:S(2)}) copy-start(f32[2048]{0:T(1024)} %param.14) | copy-start | bytes 24580
  0.6 11.2 %copy-start = (f32[2048,400]{0,1:T(8,128)S(1)}, f32[2048,400]{0,1:T(8,128)}, u32[]{:S(2)}) copy-start(f32[2048,400]{0,1:T(8,128)} %param.11) | copy-start | bytes 9830404
  0.7 11.2 %copy-start.1 = (f32[32,400]{1,0:T(8,128)S(1)}, f32[32,400]{1,0:T(8,128)}, u32[]{:S(2)}) copy-start(f32[32,400]{1,0:T(8,128)} %relations.5) | copy-start | bytes 153604
  0.7 11.2 %copy-start.2 = (s32[2,256]{1,0:T(2,128)S(1)}, s32[2,256]{1,0:T(2,128)}, u32[]{:S(2)}) copy-start(s32[2,256]{1,0:T(2,128)} %refs_10_.1) | copy-start | bytes 6148
  0.7 11.2 %copy-start.3 = (s32[2,1000]{1,0:T(2,128)S(1)}, s32[2,1000]{1,0:T(2,128)}, u32[]{:S(2)}) copy-start(s32[2,1000]{1,0:T(2,128)} %nsrc.3) | copy-start | bytes 24004
  0.7 11.2 %copy-start.4 = (s32[2,1000]{1,0:T(2,128)S(1)}, s32[2,1000]{1,0:T(2,128)}, u32[]{:S(2)}) copy-start(s32[2,1000]{1,0:T(2,128)} %ndst.3) | copy-start | bytes 24004
  0.7 11.2 %copy-start.6 = (s32[2,256]{1,0:T(2,128)S(1)}, s32[2,256]{1,0:T(2,128)}, u32[]{:S(2)}) copy-start(s32[2,256]{1,0:T(2,128)} %src.3) | copy-start | bytes 6148
  0.7 11.2 %copy-start.7 = (s32[2,256]{1,0:T(2,128)S(1)}, s32[2,256]{1,0:T(2,128)}, u32[]{:S(2)}) copy-start(s32[2,256]{1,0:T(2,128)} %rid.3) | copy-start | bytes 6148
  0.7 43.7 %collective-permute-start.4 = (f32[400,2048]{1,0:T(8,128)}, f32[400,2048]{1,0:T(8,128)S(1)}, u32[]{:S(2)}, u32[]{:S(2)}) collective-permute-start(f32[400,2048]{1,0:T(8,128)} %bitcast.18), channel_id=1, source_target_pairs={{2,4},{6,8},{10,12},{14,16},{18,20},{22,24},{26,28},{30,0},{3,5},{... | collective-permute-start | bytes 9830408 | tf_op jit(solution)/shard_map/ppermute | solution.py:608
  4.4 11.3 %copy-start.5 = (f32[2048]{0:T(1024)S(1)}, f32[2048]{0:T(1024)}, u32[]{:S(2)}) copy-start(f32[2048]{0:T(1024)} %param.12) | copy-start | bytes 24580
  4.4 11.3 %collective-permute-start.2 = (f32[400,1024]{1,0:T(8,128)S(1)}, f32[400,1024]{1,0:T(8,128)S(1)}, u32[]{:S(2)}, u32[]{:S(2)}) collective-permute-start(f32[400,1024]{1,0:T(8,128)S(1)} %get-tuple-element.125), channel_id=1, source_target_pairs={{0,2},{4,6},{8,10},{12,14},{16,18},{20,22},{24,26},{28,30},{1,3},{... | collective-permute-start | bytes 4915208 | tf_op jit(solution)/shard_map/ppermute | solution.py:609
  10.3 5.4 %collective-permute-start.1 = (f32[400,1024]{1,0:T(8,128)S(1)}, f32[400,1024]{1,0:T(8,128)S(1)}, u32[]{:S(2)}, u32[]{:S(2)}) collective-permute-start(f32[400,1024]{1,0:T(8,128)S(1)} %get-tuple-element.126), channel_id=1, source_target_pairs={{0,2},{4,6},{8,10},{12,14},{16,18},{20,22},{24,26},{28,30},{1,3},{... | collective-permute-start | bytes 4915208 | tf_op jit(solution)/shard_map/ppermute | solution.py:609
  11.8 4.0 %collective-permute-start = (f32[2048]{0:T(1024)S(1)}, f32[2048]{0:T(1024)S(1)}, u32[]{:S(2)}, u32[]{:S(2)}) collective-permute-start(f32[2048]{0:T(1024)S(1)} %copy-done.9), channel_id=1, source_target_pairs={{0,2},{4,6},{8,10},{12,14},{16,18},{20,22},{24,26},{28,30},{2,0},{... | collective-permute-start | bytes 24584 | tf_op jit(solution)/shard_map/ppermute | solution.py:610
  15.9 50.4 %collective-permute-start.9 = (f32[400,1280]{1,0:T(8,128)S(1)}, f32[400,1280]{1,0:T(8,128)S(1)}, u32[]{:S(2)}, u32[]{:S(2)}) collective-permute-start(f32[400,1280]{1,0:T(8,128)S(1)} %get-tuple-element.93), channel_id=1, source_target_pairs={{2,4},{6,8},{10,12},{14,16},{18,20},{22,24},{26,28},{30,0},{3,5},{... | collective-permute-start | bytes 6144008 | tf_op jit(solution)/shard_map/ppermute | solution.py:616
  17.2 16.0 %collective-permute-start.5 = (f32[1,2048]{1,0:T(1,128)S(1)}, f32[1,2048]{1,0:T(1,128)S(1)}, u32[]{:S(2)}, u32[]{:S(2)}) collective-permute-start(f32[1,2048]{1,0:T(1,128)S(1)} %get-tuple-element.78), channel_id=1, source_target_pairs={{2,0},{6,4},{10,8},{14,12},{18,16},{22,20},{26,24},{30,28},{3,1},{... | collective-permute-start | bytes 24584 | tf_op jit(solution)/shard_map/ppermute | solution.py:617
  18.5 18.1 %collective-permute-start.3 = (f32[2048]{0:T(1024)S(1)}, f32[2048]{0:T(1024)S(1)}, u32[]{:S(2)}, u32[]{:S(2)}) collective-permute-start(f32[2048]{0:T(1024)S(1)} %collective-permute-done), channel_id=1, source_target_pairs={{0,4},{4,8},{8,12},{12,16},{16,20},{20,24},{24,28},{28,0},{1,5},{5... | collective-permute-start | bytes 24584 | tf_op jit(solution)/shard_map/ppermute | solution.py:611
  33.2 8.4 %collective-permute-start.6 = (f32[1,2048]{1,0:T(1,128)S(1)}, f32[1,2048]{1,0:T(1,128)S(1)}, u32[]{:S(2)}, u32[]{:S(2)}) collective-permute-start(f32[1,2048]{1,0:T(1,128)S(1)} %collective-permute-done.5), channel_id=1, source_target_pairs={{0,4},{4,8},{8,12},{12,16},{16,20},{20,24},{24,28},{28,0},{1,5},{5... | collective-permute-start | bytes 24584 | tf_op jit(solution)/shard_map/ppermute | solution.py:617
  55.3 9.1 %collective-permute-start.10 = (f32[408,1024]{1,0:T(8,128)S(1)}, f32[408,1024]{1,0:T(8,128)S(1)}, u32[]{:S(2)}, u32[]{:S(2)}) collective-permute-start(f32[408,1024]{1,0:T(8,128)S(1)} %get-tuple-element.96), channel_id=1, source_target_pairs={{0,2},{4,6},{8,10},{12,14},{16,18},{20,22},{24,26},{28,30},{1,3},{... | collective-permute-start | bytes 5013512 | tf_op jit(solution)/shard_map/ppermute | solution.py:621
  56.7 7.7 %collective-permute-start.11 = (f32[400,1024]{1,0:T(8,128)S(1)}, f32[400,1024]{1,0:T(8,128)S(1)}, u32[]{:S(2)}, u32[]{:S(2)}) collective-permute-start(f32[400,1024]{1,0:T(8,128)S(1)} %get-tuple-element.97), channel_id=1, source_target_pairs={{0,2},{4,6},{8,10},{12,14},{16,18},{20,22},{24,26},{28,30},{1,3},{... | collective-permute-start | bytes 4915208 | tf_op jit(solution)/shard_map/ppermute | solution.py:621
  58.1 17.0 %collective-permute-start.8 = (f32[400,512]{1,0:T(8,128)S(1)}, f32[400,512]{1,0:T(8,128)S(1)}, u32[]{:S(2)}, u32[]{:S(2)}) collective-permute-start(f32[400,512]{1,0:T(8,128)S(1)} %get-tuple-element.92), channel_id=1, source_target_pairs={{2,4},{6,8},{10,12},{14,16},{18,20},{22,24},{26,28},{30,0},{3,5},{... | collective-permute-start | bytes 2457608 | tf_op jit(solution)/shard_map/ppermute | solution.py:616
  59.4 20.1 %collective-permute-start.7 = (f32[400,256]{1,0:T(8,128)S(1)}, f32[400,256]{1,0:T(8,128)S(1)}, u32[]{:S(2)}, u32[]{:S(2)}) collective-permute-start(f32[400,256]{1,0:T(8,128)S(1)} %get-tuple-element.81), channel_id=1, source_target_pairs={{2,4},{6,8},{10,12},{14,16},{18,20},{22,24},{26,28},{30,0},{3,5},{... | collective-permute-start | bytes 1228808 | tf_op jit(solution)/shard_map/ppermute | solution.py:616
  82.9 4.3 %collective-permute-start.12 = (f32[32,400]{1,0:T(8,128)S(1)}, f32[32,400]{1,0:T(8,128)S(1)}, u32[]{:S(2)}, u32[]{:S(2)}) collective-permute-start(f32[32,400]{1,0:T(8,128)S(1)} %get-tuple-element.124.rest_0_), channel_id=1, source_target_pairs={{0,1},{1,0},{2,3},{3,2},{4,5},{5,4},{6,7},{7,6},{8,9},{9,8},{10,11... | collective-permute-start | bytes 153608 | tf_op jit(solution)/shard_map/ppermute | solution.py:638
  84.7 2.5 %copy-start.8 = (f32[32]{0:T(128)S(1)}, f32[32]{0:T(128)}, u32[]{:S(2)}) copy-start(f32[32]{0:T(128)} %param.16) | copy-start | bytes 388

commit v3 on v2

--- a/solution.py
+++ b/solution.py
@@ -47,7 +47,7 @@
 
 
 def step_of(rows, most=512):
-    return next(size for size in (1024, 512, 256) if size <= most and rows % size == 0)
+    return next(size for size in (2048, 1024, 512, 256) if size <= most and rows % size == 0)
 
 
 def each(count, body, fixed=False):
@@ -396,15 +396,17 @@
 
 def source_scores(number, probe_rows, left16, count_l, gp, weights=None):
     rows = left16.shape[1]
-    size = step_of(rows, 1024)
-    gp[...] = jnp.zeros_like(gp)
+    size = step_of(rows, 2048)
+    total = None
     for i in range(rows // size):
         cut = lanes_at(i, size)
         rows16 = left16[:, cut]
         part = negative_weights(rows16, probe_rows[...], number)
         if weights is not None:
             weights[:, cut] = part
-        gp[...] += mul(rows16, often(part, times_at(count_l, i, size)), NT)
+        more = mul(rows16, often(part, times_at(count_l, i, size)), NT)
+        total = more if total is None else total + more
+    gp[...] = total
 
 
 def early_edges(parity, name, number, step, low, high, target, ready, dst):
@@ -443,24 +445,25 @@
     )
 
 
-def late_edges(parity, number, step, at, piece, ready, dst, target, target_rows, gq, rel, after):
+def late_edges(parity, number, step, at, piece, ready, dst, target_rows, gq, rel, after):
     (weight, source, query, query_rows, left16, _oh_src, oh_dst, count_l, count_r, kind, weight_rows) = ready
     depth, rows = left16.shape
     edges = weight.shape[1]
     pair16 = shape(2 * depth, edges, dtype=BF16)
 
     def body(piece, weight, source, query, query_rows, left16, oh_dst, count_l, count_r, kind, dst, weight_rows,
-             held_t, held_rows, held_q, rel_in, _after,
+             held_rows, held_q, rel_in, _after,
              rgrad, to_src, to_dst, rel_out, probe, weights, gp, probe_rows):
         size = piece.shape[1]
         parts = split(piece[...], 3)
         hits = oh_dst[:, at : at + size]
         slab = jnp.concatenate(parts, axis=1)
         table = jnp.concatenate([hits] * 3, axis=1)
-        probe_rows[...] = half_product(weight_rows[...], held_rows[...] + mul(table, slab, NT))
+        t_rows = held_rows[...] + mul(table, slab, NT)
+        probe_rows[...] = half_product(weight_rows[...], t_rows)
         source_scores(number, probe_rows, left16, count_l, gp, weights)
         w, s = weight[...], source[...]
-        t = held_t[...] + mul(slab, table, NT)
+        t = t_rows.T
         probe[...] = (w * t).astype(BF16)
         rgrad[...], more = negatives(parts[0], query[...], query_rows[...], times_at(count_r, 0, size, at), number)
         q = held_q[...] + more
@@ -475,10 +478,10 @@
     return call(
         only_on(parity, body), "late_edges",
         [piece, weight, source, query, query_rows, left16, oh_dst, count_l, count_r, kind, dst, weight_rows,
-         target, target_rows, gq, rel, after],
+         target_rows, gq, rel, after],
         [shape(depth, piece.shape[1]), pair16, pair16, shape(*rel.shape), shape(depth, edges, dtype=BF16), shape(edges, rows, dtype=BF16)],
         scratch_shapes=scratch([shape(depth, edges), shape(edges, depth, dtype=BF16)]),
-        aliases={15: 3},
+        aliases={14: 3},
     )
 
 
@@ -527,7 +530,7 @@
         def runs(start, stop):
             out = []
             while start < stop:
-                size = 512 if start % 512 == 0 and start + 512 <= stop else 256
+                size = 512 if start % 512 == 0 and start + 512 < rows and start + 512 <= stop else 256
                 out.append(slice(start, start + size))
                 start += size
             return out
@@ -632,7 +635,7 @@
         to_dst, target_rows = early_edges(0, "early_edges%d" % i, number, 1, at, at + size, target, ready, dst_index)
         right_b, order = early_right(0, "early_right%d" % i, at, far[i], state, rgrad, to_dst, ready[6], right_b, order)
     at = cuts[-1][0]
-    rgrad, to_src, to_dst, rel, probe, weights = late_edges(0, number, 1, at, far[-1], ready, dst_index, target, target_rows, gq, rel, order)
+    rgrad, to_src, to_dst, rel, probe, weights = late_edges(0, number, 1, at, far[-1], ready, dst_index, target_rows, gq, rel, order)
     ahead, rel = ahead_left(0, left_a, first_lstate, to_src, ready[5], probe, weights, ready[7], rel)
     if lax.axis_size("rel") == 2:
         rels = [rel, lax.ppermute(rel, "rel", [(0, 1), (1, 0)])]

time: 88.3 us -> 88.1 us (level)
  no operation moved by 1% of the time
where the time goes in v3:
time: 88.1 us; the launch traced here: 87.8 us
  Pallas kernels  36.4 us (41%)
  starting transfers between devices  25.6 us (29%)
  waiting for transfers between devices  22.5 us (26%)
  local copies, waits for them, and re-layouts  2.21 us (3%)
  between operations  1 us (1%)
    pallas_call x15, Pallas kernels, call(): pl.pallas_call(kernel, out_shape=tuple(shapes), in_specs=[large if i in i...  36.4 us
    ppermute x2, waiting for transfers between devices, local(): state = lax.ppermute(lax.ppermute(state, 'blk', back), 'blk', skip)  16.1 us
    ppermute x2, starting transfers between devices, local(): lax.ppermute(right[:, at:at + size], 'blk', inside)  7.28 us
    ppermute x2, starting transfers between devices, local(): state = lax.ppermute(lax.ppermute(state, 'blk', back), 'blk', skip)  4.74 us
    ppermute x3, starting transfers between devices, local(): far = [lax.ppermute(piece, 'blk', across) for piece in far]  3.88 us
    ppermute x1, starting transfers between devices, local(): state_far = lax.ppermute(state_near, 'blk', skip).reshape(1, rows)  3.46 us
    ppermute x3, waiting for transfers between devices, local(): far = [lax.ppermute(piece, 'blk', across) for piece in far]  3.42 us
    ppermute x1, waiting for transfers between devices, local(): right_far = lax.ppermute(right, 'blk', across)  2.87 us
  transfers between devices with their start and end apart: 13, of which 7 were waited for; matrix products, arithmetic and copies ran while one was open for 2% of the time, Pallas kernels for 37%

profile of v3, /device:TPU:0, one launch (start us, length us, event | category | flops | bytes accessed | tf_op | source)
XLA Modules:
  0.0 87.8 jit_solution(1980404098415462659)
XLA Ops:
  0.6 0.0 copy-start.9
  0.6 0.0 copy-start
  0.7 0.0 copy-start.1
  0.7 0.0 copy-start.2
  0.7 0.0 copy-start.3
  0.7 0.0 copy-start.4
  0.7 0.0 copy-start.6
  0.7 0.0 copy-start.7
  0.7 1.6 %collective-permute-start.4 = (f32[400,2048]{1,0:T(8,128)}, f32[400,2048]{1,0:T(8,128)S(1)}, u32[]{:S(2)}, u32[]{:S(2)}) collective-permute-start(f32[400,2048]{1,0:T(8,128)} %bitcast.18), channel_id=1, source_target_pairs={{2,4},{6,8},{10,12},{14,16},{18,20},{22,24},{26,28},{30,0},{3,5},{... | collective-permute-start | bytes 9830408 | tf_op jit(solution)/shard_map/ppermute | solution.py:611
  2.3 2.2 %fusion = (f32[400,1024]{1,0:T(8,128)S(1)}, f32[400,1024]{1,0:T(8,128)S(1)}) fusion(f32[400,2048]{1,0:T(8,128)} %bitcast.19), kind=kLoop, calls=%fused_computation | loop fusion | bytes 6553600 | tf_op jit(solution)/shard_map/slice | solution.py:612
  4.4 0.0 copy-start.5
  4.4 5.9 %collective-permute-start.2 = (f32[400,1024]{1,0:T(8,128)S(1)}, f32[400,1024]{1,0:T(8,128)S(1)}, u32[]{:S(2)}, u32[]{:S(2)}) collective-permute-start(f32[400,1024]{1,0:T(8,128)S(1)} %get-tuple-element.125), channel_id=1, source_target_pairs={{0,2},{4,6},{8,10},{12,14},{16,18},{20,22},{24,26},{28,30},{1,3},{... | collective-permute-start | bytes 4915208 | tf_op jit(solution)/shard_map/ppermute | solution.py:612
  10.3 1.4 %collective-permute-start.1 = (f32[400,1024]{1,0:T(8,128)S(1)}, f32[400,1024]{1,0:T(8,128)S(1)}, u32[]{:S(2)}, u32[]{:S(2)}) collective-permute-start(f32[400,1024]{1,0:T(8,128)S(1)} %get-tuple-element.126), channel_id=1, source_target_pairs={{0,2},{4,6},{8,10},{12,14},{16,18},{20,22},{24,26},{28,30},{1,3},{... | collective-permute-start | bytes 4915208 | tf_op jit(solution)/shard_map/ppermute | solution.py:612
  11.7 0.0 copy-done.9
  11.8 0.1 collective-permute-start
  11.8 0.0 copy-done
  11.8 0.0 copy-done.1
  11.9 0.0 copy-done.2
  11.9 0.0 copy-done.3
  11.9 0.0 copy-done.4
  11.9 0.0 copy-done.6
  11.9 0.0 copy-done.7
  11.9 3.7 %prepare0.1 = (f32[400,256]{1,0:T(8,128)S(1)}, f32[400,256]{1,0:T(8,128)S(1)}, bf16[400,256]{1,0:T(8,128)(2,1)S(1)}, bf16[256,400]{1,0:T(8,128)(2,1)S(1)}, bf16[...) custom-call(f32[400,2048]{1,0:T(8,128)S(1)} %bitcast.9, ...), custom_call_target="tpu_custom_call" | custom-call | flops 1000000 | bytes 100000 | tf_op jit(solution)/shard_map/prepare0/pallas_call | solution.py:328
  15.6 0.1 collective-permute-done
  15.7 0.0 collective-permute-done.2.refs_16_
  15.7 0.0 collective-permute-done.1.refs_15_
  15.7 0.0 copy-done.5
  15.7 0.2 first_near.1
  15.9 1.3 %collective-permute-start.9 = (f32[400,1280]{1,0:T(8,128)S(1)}, f32[400,1280]{1,0:T(8,128)S(1)}, u32[]{:S(2)}, u32[]{:S(2)}) collective-permute-start(f32[400,1280]{1,0:T(8,128)S(1)} %get-tuple-element.93), channel_id=1, source_target_pairs={{2,4},{6,8},{10,12},{14,16},{18,20},{22,24},{26,28},{30,0},{3,5},{... | collective-permute-start | bytes 6144008 | tf_op jit(solution)/shard_map/ppermute | solution.py:619
  17.2 1.3 %collective-permute-start.5 = (f32[1,2048]{1,0:T(1,128)S(1)}, f32[1,2048]{1,0:T(1,128)S(1)}, u32[]{:S(2)}, u32[]{:S(2)}) collective-permute-start(f32[1,2048]{1,0:T(1,128)S(1)} %get-tuple-element.78), channel_id=1, source_target_pairs={{2,0},{6,4},{10,8},{14,12},{18,16},{22,20},{26,24},{30,28},{3,1},{... | collective-permute-start | bytes 24584 | tf_op jit(solution)/shard_map/ppermute | solution.py:620
  18.5 3.5 %collective-permute-start.3 = (f32[2048]{0:T(1024)S(1)}, f32[2048]{0:T(1024)S(1)}, u32[]{:S(2)}, u32[]{:S(2)}) collective-permute-start(f32[2048]{0:T(1024)S(1)} %collective-permute-done), channel_id=1, source_target_pairs={{0,4},{4,8},{8,12},{12,16},{16,20},{20,24},{24,28},{28,0},{1,5},{5... | collective-permute-start | bytes 24584 | tf_op jit(solution)/shard_map/ppermute | solution.py:614
  22.0 11.2 %collective-permute-done.5 = f32[1,2048]{1,0:T(1,128)S(1)} collective-permute-done((f32[1,2048]{1,0:T(1,128)S(1)}, f32[1,2048]{1,0:T(1,128)S(1)}, u32[]{:S(2)}, u32[]{:S(2)}) %collective-permute-start.5) | collective-permute-done | bytes 8224 | tf_op jit(solution)/shard_map/ppermute | solution.py:620
  33.2 3.4 %collective-permute-start.6 = (f32[1,2048]{1,0:T(1,128)S(1)}, f32[1,2048]{1,0:T(1,128)S(1)}, u32[]{:S(2)}, u32[]{:S(2)}) collective-permute-start(f32[1,2048]{1,0:T(1,128)S(1)} %collective-permute-done.5), channel_id=1, source_target_pairs={{0,4},{4,8},{8,12},{12,16},{16,20},{20,24},{24,28},{28,0},{1,5},{5... | collective-permute-start | bytes 24584 | tf_op jit(solution)/shard_map/ppermute | solution.py:620
  36.6 0.0 collective-permute-done.3
  36.6 4.9 %collective-permute-done.6.refs_17_.refs_1_.refs_9_ = f32[1,2048]{1,0:T(1,128)S(1)} collective-permute-done((f32[1,2048]{1,0:T(1,128)S(1)}, f32[1,2048]{1,0:T(1,128)S(1)}, u32[]{:S(2)}, u32[]{:S(2)}) %collective-permute-start.6) | collective-permute-done | bytes 8224 | tf_op jit(solution)/shard_map/ppermute | solution.py:620
  41.5 2.9 %collective-permute-done.4.refs_15_ = f32[400,2048]{1,0:T(8,128)S(1)} collective-permute-done((f32[400,2048]{1,0:T(8,128)}, f32[400,2048]{1,0:T(8,128)S(1)}, u32[]{:S(2)}, u32[]{:S(2)}) %collective-permute-start.4) | collective-permute-done | bytes 3276832 | tf_op jit(solution)/shard_map/ppermute | solution.py:611
  44.4 10.9 %first_far.1 = (f32[400,2048]{1,0:T(8,128)S(1)}, f32[1,2048]{1,0:T(1,128)S(1)}, f32[32,400]{1,0:T(8,128)S(1)}, f32[408,1024]{1,0:T(8,128)S(1)}, f32[400,1024]{1,0:T(8,128)S(1)}, /*index=5*/f32[1,2048]{1,0:T(1,128)}) custom-call(f32[400,2048]{1,0:T(8,128)S(1)} %bitcast.11, f32[1,2048]{1,0:T(1,128)S(1)} %get-tuple-element.75.refs_1_, ...), custom_call_target="tpu_custom_call", output_to_operand_aliasing={{0}: (16, {})} | custom-call | flops 1000000 | bytes 100000 | tf_op jit(solution)/shard_map/first_far/pallas_call | solution.py:328
  55.3 1.4 %collective-permute-start.10 = (f32[408,1024]{1,0:T(8,128)S(1)}, f32[408,1024]{1,0:T(8,128)S(1)}, u32[]{:S(2)}, u32[]{:S(2)}) collective-permute-start(f32[408,1024]{1,0:T(8,128)S(1)} %get-tuple-element.96), channel_id=1, source_target_pairs={{0,2},{4,6},{8,10},{12,14},{16,18},{20,22},{24,26},{28,30},{1,3},{... | collective-permute-start | bytes 5013512 | tf_op jit(solution)/shard_map/ppermute | solution.py:624
  56.7 1.4 %collective-permute-start.11 = (f32[400,1024]{1,0:T(8,128)S(1)}, f32[400,1024]{1,0:T(8,128)S(1)}, u32[]{:S(2)}, u32[]{:S(2)}) collective-permute-start(f32[400,1024]{1,0:T(8,128)S(1)} %get-tuple-element.97), channel_id=1, source_target_pairs={{0,2},{4,6},{8,10},{12,14},{16,18},{20,22},{24,26},{28,30},{1,3},{... | collective-permute-start | bytes 4915208 | tf_op jit(solution)/shard_map/ppermute | solution.py:624
  58.1 1.3 %collective-permute-start.8 = (f32[400,512]{1,0:T(8,128)S(1)}, f32[400,512]{1,0:T(8,128)S(1)}, u32[]{:S(2)}, u32[]{:S(2)}) collective-permute-start(f32[400,512]{1,0:T(8,128)S(1)} %get-tuple-element.92), channel_id=1, source_target_pairs={{2,4},{6,8},{10,12},{14,16},{18,20},{22,24},{26,28},{30,0},{3,5},{... | collective-permute-start | bytes 2457608 | tf_op jit(solution)/shard_map/ppermute | solution.py:619
  59.4 1.3 %collective-permute-start.7 = (f32[400,256]{1,0:T(8,128)S(1)}, f32[400,256]{1,0:T(8,128)S(1)}, u32[]{:S(2)}, u32[]{:S(2)}) collective-permute-start(f32[400,256]{1,0:T(8,128)S(1)} %get-tuple-element.81), channel_id=1, source_target_pairs={{2,4},{6,8},{10,12},{14,16},{18,20},{22,24},{26,28},{30,0},{3,5},{... | collective-permute-start | bytes 1228808 | tf_op jit(solution)/shard_map/ppermute | solution.py:619
  60.7 3.7 %prepare1.1 = (f32[400,256]{1,0:T(8,128)S(1)}, f32[400,256]{1,0:T(8,128)S(1)}, bf16[400,256]{1,0:T(8,128)(2,1)S(1)}, bf16[256,400]{1,0:T(8,128)(2,1)S(1)}, bf16[...) custom-call(f32[400,2048]{1,0:T(8,128)S(1)} %get-tuple-element.79.le, ...), custom_call_target="tpu_custom_call" | custom-call | flops 1000000 | bytes 100000 | tf_op jit(solution)/shard_map/prepare1/pallas_call | solution.py:328
  64.5 0.0 collective-permute-done.11.refs_16_
  64.5 0.0 collective-permute-done.10.refs_15_
  64.5 1.0 %last_near.1 = (f32[400,2048]{1,0:T(8,128)}, f32[1,2048]{1,0:T(1,128)S(1)}, f32[32,400]{1,0:T(8,128)S(1)}, f32[400,2048]{1,0:T(8,128)}, f32[1,2048]{1,0:T(1,128)}) custom-call(f32[400,2048]{1,0:T(8,128)S(1)} %get-tuple-element.79.left.refs_0_, f32[1,2048]{1,0:T(1,128)S(1)} %get-tuple-element.80.refs_1_, f32[1,2048]{1,0:T(1,128)S(1)} %bitcast.13, ...), custom_call_target="tpu_custom_call" | custom-call | flops 1000000 | bytes 100000 | tf_op jit(solution)/shard_map/last_near/pallas_call | solution.py:328
  65.5 0.9 collective-permute-done.9.refs_0_
  66.4 2.5 %last_piece0.1 = (f32[400,256]{1,0:T(8,128)S(1)}, f32[400,256]{1,0:T(8,128)S(1)}, f32[400,1280]{1,0:T(8,128)S(1)}) custom-call(f32[400,1280]{1,0:T(8,128)S(1)} %collective-permute-done.9.refs_0_, bf16[400,256]{1,0:T(8,128)(2,1)S(1)} %get-tuple-element.84.refs_6_.refs_1_.refs_3_, bf16[256,400]{1,0:T(8,128)(2,1)S(1)} %get-tuple-element.85.refs_7_.refs_2_.refs_4_, ...), custom_call_target="tpu_custom_call" | custom-call | flops 1000000 | bytes 100000 | tf_op jit(solution)/shard_map/last_piece0/pallas_call | solution.py:328
  68.9 2.1 %early_edges0.1 = (bf16[800,256]{1,0:T(8,128)(2,1)S(1)}, f32[256,400]{1,0:T(8,128)}) custom-call(f32[400,256]{1,0:T(8,128)S(1)} %get-tuple-element.82.refs_4_.refs_0_.refs_1_, f32[400,256]{1,0:T(8,128)S(1)} %get-tuple-element.83.refs_5_.refs_1_.refs_2_, f32[400,256]{1,0:T(8,128)S(1)} %get-tuple-element.99.refs_2_.refs_5_, ...), custom_call_target="tpu_custom_call" | custom-call | flops 1000000 | bytes 100000 | tf_op jit(solution)/shard_map/early_edges0/pallas_call | solution.py:328
  71.0 1.9 %early_right0.1 = (f32[400,2048]{1,0:T(8,128)}, f32[1,2048]{1,0:T(1,128)S(1)}) custom-call(f32[400,1280]{1,0:T(8,128)S(1)} %collective-permute-done.9.refs_0_, f32[1,2048]{1,0:T(1,128)S(1)} %collective-permute-done.6.refs_17_.refs_1_.refs_9_, f32[400,1280]{1,0:T(8,128)S(1)} %get-tuple-element.101.refs_2_, ...), custom_call_target="tpu_custom_call", output_to_operand_aliasing={{1}: (5, {}), {0}: (6, {})} | custom-call | flops 1000000 | bytes 100000 | tf_op jit(solution)/shard_map/early_right0/pallas_call | solution.py:328
  72.9 2.3 %collective-permute-done.8.refs_0_ = f32[400,512]{1,0:T(8,128)S(1)} collective-permute-done((f32[400,512]{1,0:T(8,128)S(1)}, f32[400,512]{1,0:T(8,128)S(1)}, u32[]{:S(2)}, u32[]{:S(2)}) %collective-permute-start.8) | collective-permute-done | bytes 819232 | tf_op jit(solution)/shard_map/ppermute | solution.py:619
  75.1 1.2 %last_piece1.1 = (f32[400,256]{1,0:T(8,128)S(1)}, f32[400,256]{1,0:T(8,128)S(1)}, f32[400,512]{1,0:T(8,128)S(1)}) custom-call(f32[400,512]{1,0:T(8,128)S(1)} %collective-permute-done.8.refs_0_, bf16[400,256]{1,0:T(8,128)(2,1)S(1)} %get-tuple-element.84.refs_6_.refs_1_.refs_3_, ...), custom_call_target="tpu_custom_call", output_to_operand_aliasing={{0}: (5, {}), {1}: (6, {})} | custom-call | flops 1000000 | bytes 100000 | tf_op jit(solution)/shard_map/last_piece1/pallas_call | solution.py:328
  76.4 1.3 %early_edges1.1 = (bf16[800,256]{1,0:T(8,128)(2,1)S(1)}, f32[256,400]{1,0:T(8,128)S(1)}) custom-call(f32[400,256]{1,0:T(8,128)S(1)} %get-tuple-element.82.refs_4_.refs_0_.refs_1_, f32[400,256]{1,0:T(8,128)S(1)} %get-tuple-element.83.refs_5_.refs_1_.refs_2_, f32[400,256]{1,0:T(8,128)S(1)} %get-tuple-element.105.refs_2_, ...), custom_call_target="tpu_custom_call" | custom-call | flops 1000000 | bytes 100000 | tf_op jit(solution)/shard_map/early_edges1/pallas_call | solution.py:328
  77.7 1.5 %early_right1.1 = (f32[400,2048]{1,0:T(8,128)}, f32[1,2048]{1,0:T(1,128)S(1)}) custom-call(f32[400,512]{1,0:T(8,128)S(1)} %collective-permute-done.8.refs_0_, f32[1,2048]{1,0:T(1,128)S(1)} %collective-permute-done.6.refs_17_.refs_1_.refs_9_, f32[400,512]{1,0:T(8,128)S(1)} %get-tuple-element.109.refs_2_, ...), custom_call_target="tpu_custom_call", output_to_operand_aliasing={{1}: (5, {}), {0}: (6, {})} | custom-call | flops 1000000 | bytes 100000 | tf_op jit(solution)/shard_map/early_right1/pallas_call | solution.py:328
  79.2 0.3 collective-permute-done.7.refs_0_.refs_8_
  79.5 2.3 %late_edges.1 = (f32[400,256]{1,0:T(8,128)S(1)}, bf16[800,256]{1,0:T(8,128)(2,1)S(1)}, bf16[800,256]{1,0:T(8,128)(2,1)S(1)}, f32[32,400]{1,0:T(8,128)S(1)}, bf16...) custom-call(f32[400,256]{1,0:T(8,128)S(1)} %collective-permute-done.7.refs_0_.refs_8_, ...), custom_call_target="tpu_custom_call", output_to_operand_aliasing={{3}: (14, {})} | custom-call | flops 1000000 | bytes 100000 | tf_op jit(solution)/shard_map/late_edges/pallas_call | solution.py:328
  81.8 0.9 %ahead_left.1 = (f32[400,768]{1,0:T(8,128)S(1)}, f32[32,400]{1,0:T(8,128)S(1)}) custom-call(f32[400,2048]{1,0:T(8,128)S(1)} %get-tuple-element.79.left.refs_0_, f32[1,2048]{1,0:T(1,128)S(1)} %get-tuple-element.80.refs_1_, bf16[800,256]{1,0:T(8,128)(2,1)S(1)} %get-tuple-element.113.refs_2_, ...), custom_call_target="tpu_custom_call", output_to_operand_aliasing={{1}: (7, {})} | custom-call | flops 1000000 | bytes 100000 | tf_op jit(solution)/shard_map/ahead_left/pallas_call | solution.py:328
  82.7 1.8 %collective-permute-start.12 = (f32[32,400]{1,0:T(8,128)S(1)}, f32[32,400]{1,0:T(8,128)S(1)}, u32[]{:S(2)}, u32[]{:S(2)}) collective-permute-start(f32[32,400]{1,0:T(8,128)S(1)} %get-tuple-element.124.rest_0_), channel_id=1, source_target_pairs={{0,1},{1,0},{2,3},{3,2},{4,5},{5,4},{6,7},{7,6},{8,9},{9,8},{10,11... | collective-permute-start | bytes 153608 | tf_op jit(solution)/shard_map/ppermute | solution.py:641
  84.5 0.0 copy-start.8
  84.5 2.4 %late_slabs.1 = (f32[400,2048]{1,0:T(8,128)}, f32[400,2048]{1,0:T(8,128)}) custom-call(f32[400,2048]{1,0:T(8,128)S(1)} %get-tuple-element.79.left.refs_0_, f32[1,2048]{1,0:T(1,128)S(1)} %get-tuple-element.80.refs_1_, bf16[800,256]{1,0:T(8,128)(2,1)S(1)} %get-tuple-element.113.refs_2_, ...), custom_call_target="tpu_custom_call", output_to_operand_aliasing={{0}: (13, {}), {1}: (14, {})} | custom-call | flops 1000000 | bytes 100000 | tf_op jit(solution)/shard_map/late_slabs/pallas_call | solution.py:328
  87.0 0.0 collective-permute-done.12.rest_1_
  87.0 0.0 copy-done.8
  87.0 0.7 relation_update.1
  (1 shorter events, 0.0 us)
Async XLA Ops:
  0.6 11.1 %copy-start.9 = (f32[2048]{0:T(1024)S(1)}, f32[2048]{0:T(1024)}, u32[]{:S(2)}) copy-start(f32[2048]{0:T(1024)} %param.14) | copy-start | bytes 24580
  0.6 11.2 %copy-start = (f32[2048,400]{0,1:T(8,128)S(1)}, f32[2048,400]{0,1:T(8,128)}, u32[]{:S(2)}) copy-start(f32[2048,400]{0,1:T(8,128)} %param.11) | copy-start | bytes 9830404
  0.7 11.2 %copy-start.1 = (f32[32,400]{1,0:T(8,128)S(1)}, f32[32,400]{1,0:T(8,128)}, u32[]{:S(2)}) copy-start(f32[32,400]{1,0:T(8,128)} %relations.5) | copy-start | bytes 153604
  0.7 11.2 %copy-start.2 = (s32[2,256]{1,0:T(2,128)S(1)}, s32[2,256]{1,0:T(2,128)}, u32[]{:S(2)}) copy-start(s32[2,256]{1,0:T(2,128)} %refs_10_.1) | copy-start | bytes 6148
  0.7 11.2 %copy-start.3 = (s32[2,1000]{1,0:T(2,128)S(1)}, s32[2,1000]{1,0:T(2,128)}, u32[]{:S(2)}) copy-start(s32[2,1000]{1,0:T(2,128)} %nsrc.3) | copy-start | bytes 24004
  0.7 11.2 %copy-start.4 = (s32[2,1000]{1,0:T(2,128)S(1)}, s32[2,1000]{1,0:T(2,128)}, u32[]{:S(2)}) copy-start(s32[2,1000]{1,0:T(2,128)} %ndst.3) | copy-start | bytes 24004
  0.7 11.2 %copy-start.6 = (s32[2,256]{1,0:T(2,128)S(1)}, s32[2,256]{1,0:T(2,128)}, u32[]{:S(2)}) copy-start(s32[2,256]{1,0:T(2,128)} %src.3) | copy-start | bytes 6148
  0.7 11.2 %copy-start.7 = (s32[2,256]{1,0:T(2,128)S(1)}, s32[2,256]{1,0:T(2,128)}, u32[]{:S(2)}) copy-start(s32[2,256]{1,0:T(2,128)} %rid.3) | copy-start | bytes 6148
  0.7 43.7 %collective-permute-start.4 = (f32[400,2048]{1,0:T(8,128)}, f32[400,2048]{1,0:T(8,128)S(1)}, u32[]{:S(2)}, u32[]{:S(2)}) collective-permute-start(f32[400,2048]{1,0:T(8,128)} %bitcast.18), channel_id=1, source_target_pairs={{2,4},{6,8},{10,12},{14,16},{18,20},{22,24},{26,28},{30,0},{3,5},{... | collective-permute-start | bytes 9830408 | tf_op jit(solution)/shard_map/ppermute | solution.py:611
  4.4 11.3 %copy-start.5 = (f32[2048]{0:T(1024)S(1)}, f32[2048]{0:T(1024)}, u32[]{:S(2)}) copy-start(f32[2048]{0:T(1024)} %param.12) | copy-start | bytes 24580
  4.4 11.3 %collective-permute-start.2 = (f32[400,1024]{1,0:T(8,128)S(1)}, f32[400,1024]{1,0:T(8,128)S(1)}, u32[]{:S(2)}, u32[]{:S(2)}) collective-permute-start(f32[400,1024]{1,0:T(8,128)S(1)} %get-tuple-element.125), channel_id=1, source_target_pairs={{0,2},{4,6},{8,10},{12,14},{16,18},{20,22},{24,26},{28,30},{1,3},{... | collective-permute-start | bytes 4915208 | tf_op jit(solution)/shard_map/ppermute | solution.py:612
  10.3 5.4 %collective-permute-start.1 = (f32[400,1024]{1,0:T(8,128)S(1)}, f32[400,1024]{1,0:T(8,128)S(1)}, u32[]{:S(2)}, u32[]{:S(2)}) collective-permute-start(f32[400,1024]{1,0:T(8,128)S(1)} %get-tuple-element.126), channel_id=1, source_target_pairs={{0,2},{4,6},{8,10},{12,14},{16,18},{20,22},{24,26},{28,30},{1,3},{... | collective-permute-start | bytes 4915208 | tf_op jit(solution)/shard_map/ppermute | solution.py:612
  11.8 4.0 %collective-permute-start = (f32[2048]{0:T(1024)S(1)}, f32[2048]{0:T(1024)S(1)}, u32[]{:S(2)}, u32[]{:S(2)}) collective-permute-start(f32[2048]{0:T(1024)S(1)} %copy-done.9), channel_id=1, source_target_pairs={{0,2},{4,6},{8,10},{12,14},{16,18},{20,22},{24,26},{28,30},{2,0},{... | collective-permute-start | bytes 24584 | tf_op jit(solution)/shard_map/ppermute | solution.py:613
  15.9 50.4 %collective-permute-start.9 = (f32[400,1280]{1,0:T(8,128)S(1)}, f32[400,1280]{1,0:T(8,128)S(1)}, u32[]{:S(2)}, u32[]{:S(2)}) collective-permute-start(f32[400,1280]{1,0:T(8,128)S(1)} %get-tuple-element.93), channel_id=1, source_target_pairs={{2,4},{6,8},{10,12},{14,16},{18,20},{22,24},{26,28},{30,0},{3,5},{... | collective-permute-start | bytes 6144008 | tf_op jit(solution)/shard_map/ppermute | solution.py:619
  17.2 15.9 %collective-permute-start.5 = (f32[1,2048]{1,0:T(1,128)S(1)}, f32[1,2048]{1,0:T(1,128)S(1)}, u32[]{:S(2)}, u32[]{:S(2)}) collective-permute-start(f32[1,2048]{1,0:T(1,128)S(1)} %get-tuple-element.78), channel_id=1, source_target_pairs={{2,0},{6,4},{10,8},{14,12},{18,16},{22,20},{26,24},{30,28},{3,1},{... | collective-permute-start | bytes 24584 | tf_op jit(solution)/shard_map/ppermute | solution.py:620
  18.5 18.1 %collective-permute-start.3 = (f32[2048]{0:T(1024)S(1)}, f32[2048]{0:T(1024)S(1)}, u32[]{:S(2)}, u32[]{:S(2)}) collective-permute-start(f32[2048]{0:T(1024)S(1)} %collective-permute-done), channel_id=1, source_target_pairs={{0,4},{4,8},{8,12},{12,16},{16,20},{20,24},{24,28},{28,0},{1,5},{5... | collective-permute-start | bytes 24584 | tf_op jit(solution)/shard_map/ppermute | solution.py:614
  33.2 8.4 %collective-permute-start.6 = (f32[1,2048]{1,0:T(1,128)S(1)}, f32[1,2048]{1,0:T(1,128)S(1)}, u32[]{:S(2)}, u32[]{:S(2)}) collective-permute-start(f32[1,2048]{1,0:T(1,128)S(1)} %collective-permute-done.5), channel_id=1, source_target_pairs={{0,4},{4,8},{8,12},{12,16},{16,20},{20,24},{24,28},{28,0},{1,5},{5... | collective-permute-start | bytes 24584 | tf_op jit(solution)/shard_map/ppermute | solution.py:620
  55.3 9.2 %collective-permute-start.10 = (f32[408,1024]{1,0:T(8,128)S(1)}, f32[408,1024]{1,0:T(8,128)S(1)}, u32[]{:S(2)}, u32[]{:S(2)}) collective-permute-start(f32[408,1024]{1,0:T(8,128)S(1)} %get-tuple-element.96), channel_id=1, source_target_pairs={{0,2},{4,6},{8,10},{12,14},{16,18},{20,22},{24,26},{28,30},{1,3},{... | collective-permute-start | bytes 5013512 | tf_op jit(solution)/shard_map/ppermute | solution.py:624
  56.7 7.7 %collective-permute-start.11 = (f32[400,1024]{1,0:T(8,128)S(1)}, f32[400,1024]{1,0:T(8,128)S(1)}, u32[]{:S(2)}, u32[]{:S(2)}) collective-permute-start(f32[400,1024]{1,0:T(8,128)S(1)} %get-tuple-element.97), channel_id=1, source_target_pairs={{0,2},{4,6},{8,10},{12,14},{16,18},{20,22},{24,26},{28,30},{1,3},{... | collective-permute-start | bytes 4915208 | tf_op jit(solution)/shard_map/ppermute | solution.py:624
  58.1 17.0 %collective-permute-start.8 = (f32[400,512]{1,0:T(8,128)S(1)}, f32[400,512]{1,0:T(8,128)S(1)}, u32[]{:S(2)}, u32[]{:S(2)}) collective-permute-start(f32[400,512]{1,0:T(8,128)S(1)} %get-tuple-element.92), channel_id=1, source_target_pairs={{2,4},{6,8},{10,12},{14,16},{18,20},{22,24},{26,28},{30,0},{3,5},{... | collective-permute-start | bytes 2457608 | tf_op jit(solution)/shard_map/ppermute | solution.py:619
  59.4 20.1 %collective-permute-start.7 = (f32[400,256]{1,0:T(8,128)S(1)}, f32[400,256]{1,0:T(8,128)S(1)}, u32[]{:S(2)}, u32[]{:S(2)}) collective-permute-start(f32[400,256]{1,0:T(8,128)S(1)} %get-tuple-element.81), channel_id=1, source_target_pairs={{2,4},{6,8},{10,12},{14,16},{18,20},{22,24},{26,28},{30,0},{3,5},{... | collective-permute-start | bytes 1228808 | tf_op jit(solution)/shard_map/ppermute | solution.py:619
  82.7 4.3 %collective-permute-start.12 = (f32[32,400]{1,0:T(8,128)S(1)}, f32[32,400]{1,0:T(8,128)S(1)}, u32[]{:S(2)}, u32[]{:S(2)}) collective-permute-start(f32[32,400]{1,0:T(8,128)S(1)} %get-tuple-element.124.rest_0_), channel_id=1, source_target_pairs={{0,1},{1,0},{2,3},{3,2},{4,5},{5,4},{6,7},{7,6},{8,9},{9,8},{10,11... | collective-permute-start | bytes 153608 | tf_op jit(solution)/shard_map/ppermute | solution.py:641
  84.5 2.5 %copy-start.8 = (f32[32]{0:T(128)S(1)}, f32[32]{0:T(128)}, u32[]{:S(2)}) copy-start(f32[32]{0:T(128)} %param.16) | copy-start | bytes 388

commit v4 on v3

--- a/solution.py
+++ b/solution.py
@@ -111,16 +111,39 @@
     return mul(query, weight, NN) * times, mul(rows16, often(weight, times), NT)
 
 
-def prepare(step, left, relations, src, dst, rid, nsrc, ndst,
-            weight, source, query, query_rows, left16, oh_src, oh_dst, count_l, count_r, kind, weight_rows):
+def late_last(bound, src, dst, rid):
+    edges = dst.shape[1]
+    first = lax.broadcasted_iota(jnp.int32, (edges, edges), 0)
+    second = lax.broadcasted_iota(jnp.int32, (edges, edges), 1)
+    late = jnp.where(dst >= bound, 1.0, 0.0)
+    ahead = jnp.where(first < second, 1.0, 0.0).astype(BF16)
+    before = mul(jnp.broadcast_to(late, (8, edges)).astype(BF16), ahead, NN)[0:1, :]
+    total = jnp.sum(late, axis=1, keepdims=True)
+    lane = lax.broadcasted_iota(jnp.int32, (1, edges), 1).astype(F32)
+    place = jnp.where(dst >= bound, edges - total + before, lane - before)
+    order = jnp.where(place == first.astype(F32), 1.0, 0.0).astype(BF16)
+    row = lax.broadcasted_iota(jnp.int32, (8, edges), 0)
+    packed = jnp.zeros((8, edges), jnp.int32)
+    for k, part in enumerate((src // 64, src % 64, dst // 64, dst % 64, rid)):
+        packed = jnp.where(row == k, part, packed)
+    moved = (mul(packed.astype(F32).astype(BF16), order, NT) + 0.5).astype(jnp.int32)
+    return moved[0:1] * 64 + moved[1:2], moved[2:3] * 64 + moved[3:4], moved[4:5]
+
+
+def prepare(step, bound, left, relations, src, dst, rid, nsrc, ndst,
+            weight, source, query, query_rows, left16, oh_src, oh_dst, count_l, count_r, kind, weight_rows, targets):
     rows = left.shape[1]
     here = slice(step, step + 1)
-    row_onehot(src[here, :], oh_src)
-    row_onehot(dst[here, :], oh_dst)
+    sources, aims, relation = src[here, :], dst[here, :], rid[here, :]
+    if bound is not None:
+        sources, aims, relation = late_last(bound, sources, aims, relation)
+    targets[...] = aims
+    row_onehot(sources, oh_src)
+    row_onehot(aims, oh_dst)
     count_l[...] = row_counts(nsrc[here, :], rows)
     count_r[...] = row_counts(ndst[here, :], rows)
     kinds = lax.broadcasted_iota(jnp.int32, kind.shape, 0)
-    kind[...] = jnp.where(rid[here, :] == kinds, 1.0, 0.0).astype(BF16)
+    kind[...] = jnp.where(relation == kinds, 1.0, 0.0).astype(BF16)
     weight[...] = sum(mul(part, kind[...], TN) for part in split(relations[...], 3))
     weight_rows[...] = weight[...].T
     source[...] = jnp.zeros_like(source)
@@ -145,7 +168,7 @@
         target[...] = jnp.zeros_like(target)
         gq[...] = jnp.zeros_like(gq)
 
-    size = step_of(piece.shape[1], 256 if fixed else 512)
+    size = step_of(piece.shape[1], 256)
 
     def part(i):
         cut = lanes_at(i, size)
@@ -160,14 +183,14 @@
 
 
 def join(number, weight, source, target, gq, left16, count_l, kind, rel_in,
-         probe, probe_rows, gp, lgrad, to_src, to_dst, rel_out, fixed=False):
+         probe, probe_rows, gp, lgrad, to_src, to_dst, rel_out, fixed=False, most=512):
     rows = left16.shape[1]
     product = weight[...] * target[...]
     probe[...] = product.astype(BF16)
     probe_rows[...] = half_rows(product.astype(BF16).astype(F32))
     gp[...] = jnp.zeros_like(gp)
 
-    size = step_of(rows)
+    size = step_of(rows, most)
 
     def part(i):
         cut = lanes_at(i, size)
@@ -266,9 +289,9 @@
 def train(parity, number, last, fixed, kept, takes, gives, packs, *refs):
     refs = list(refs)
     (left, lstate, rstate_in, rel_in) = refs[:4]
-    (weight, source, query, query_rows, left16, oh_src, oh_dst, count_l, count_r, kind, _rows) = refs[4:15]
-    right = refs[15 : 15 + takes]
-    refs = refs[15 + takes + kept :]
+    (weight, source, query, query_rows, left16, oh_src, oh_dst, count_l, count_r, kind, _rows, _targets) = refs[4:16]
+    right = refs[16 : 16 + takes]
+    refs = refs[16 + takes + kept :]
     left_out, lstate_out, rel_out = refs[:3]
     right_out = refs[3 : 3 + len(gives)]
     state_out = refs[3 + len(gives)]
@@ -286,7 +309,7 @@
             take_piece(number, at, piece, query, query_rows, oh_dst, count_r, target, gq, grads[-1], fixed)
             at += piece.shape[1]
         join(number, weight, source, target, gq, left16, count_l, kind, rel_in,
-             probe, probe_rows, gp, lgrad, to_src, to_dst, rel_out, fixed)
+             probe, probe_rows, gp, lgrad, to_src, to_dst, rel_out, fixed, 2048 if fixed else 1024 if last else 512)
         if last:
             unpack_state(right[STATE], depth, rstate)
             wait_right = update_and_send(right, rstate, grads, to_dst, oh_dst, spare, right_out[0], sems.at[0], fixed)
@@ -315,6 +338,7 @@
         shape(depth, edges), shape(depth, edges), shape(depth, edges, dtype=BF16), shape(edges, depth, dtype=BF16),
         shape(depth, rows, dtype=BF16), shape(edges, rows, dtype=BF16), shape(edges, rows, dtype=BF16),
         shape(rows // LANES, LANES), shape(rows // LANES, LANES), shape(kinds, edges, dtype=BF16), shape(edges, depth),
+        shape(1, edges, dtype=jnp.int32),
     )
 
 
@@ -338,10 +362,10 @@
     )(*operands)
 
 
-def prepared(step, left, relations, index):
+def prepared(step, bound, left, relations, index):
     depth, rows = left.shape
     return call(
-        functools.partial(prepare, step), "prepare%d" % step, [left, relations, *index],
+        functools.partial(prepare, step, bound), "prepare%d" % step, [left, relations, *index],
         prepared_shapes(depth, rows, index[0].shape[1], relations.shape[0]),
     )
 
@@ -365,7 +389,7 @@
         [slab, shape(1, rows), shape(*rel.shape), *blocks, shape(1, rows)],
         out_large=(0, 3) if last else (),
         scratch_shapes=[*scratch(inner), pltpu.SemaphoreType.DMA((2, rows // 256))],
-        aliases={15 + len(right) + i: 0 for i in range(len(keep))},
+        aliases={16 + len(right) + i: 0 for i in range(len(keep))},
     )
     return left_out, lstate_out, right_out, rel_out, state_out
 
@@ -380,7 +404,7 @@
 
 
 def last_piece(parity, name, number, at, piece, ready, after, held=()):
-    (_weight, _source, query, query_rows, _left16, _oh_src, oh_dst, _count_l, count_r, _kind, _rows) = ready
+    (_weight, _source, query, query_rows, _left16, _oh_src, oh_dst, _count_l, count_r, _kind, _rows, _targets) = ready
     depth, edges = query.shape
 
     def body(piece, query, query_rows, oh_dst, count_r, *rest):
@@ -394,40 +418,32 @@
     )
 
 
-def source_scores(number, probe_rows, left16, count_l, gp, weights=None):
-    rows = left16.shape[1]
-    size = step_of(rows, 2048)
-    total = None
-    for i in range(rows // size):
-        cut = lanes_at(i, size)
-        rows16 = left16[:, cut]
-        part = negative_weights(rows16, probe_rows[...], number)
-        if weights is not None:
-            weights[:, cut] = part
-        more = mul(rows16, often(part, times_at(count_l, i, size)), NT)
-        total = more if total is None else total + more
-    gp[...] = total
-
-
-def early_edges(parity, name, number, step, low, high, target, ready, dst):
-    (weight, source, _query, _query_rows, left16, _oh_src, _oh_dst, count_l, _count_r, _kind, weight_rows) = ready
-    depth = left16.shape[0]
+def source_scores(number, edges, probe_rows, left16, count_l, gp, weights):
+    rows16 = left16[...]
+    part = negative_weights(rows16, probe_rows[edges, :], number)
+    weights[edges, :] = part
+    gp[:, edges] = mul(rows16, often(part, times_at(count_l, 0, rows16.shape[1])), NT)
+
+
+def early_edges(parity, name, number, low, high, target, ready):
+    (weight, source, _query, _query_rows, left16, _oh_src, _oh_dst, count_l, _count_r, _kind, weight_rows, targets) = ready
+    depth, rows = left16.shape
     edges = weight.shape[1]
 
-    def body(weight, source, target, left16, count_l, dst, weight_rows, to_dst, target_rows, gp, probe_rows):
+    def body(weight, source, target, left16, count_l, weight_rows, targets, to_dst, target_rows, weights, gp, probe_rows):
         w, s, t = weight[...], source[...], target[...]
         target_rows[...] = t.T
         probe_rows[...] = half_product(weight_rows[...], target_rows[...])
-        source_scores(number, probe_rows, left16, count_l, gp)
-        at = dst[step : step + 1, :]
+        source_scores(number, slice(0, edges), probe_rows, left16, count_l, gp, weights)
+        at = targets[...]
         here = jnp.logical_and(at >= low, at < high)
         coef = -jax.nn.sigmoid(-jnp.sum(s * w * t, axis=0, keepdims=True))
         to_dst[0:depth, :], to_dst[depth:, :] = split(jnp.where(here, coef * w * s + gp[...] * w, 0.0), 2)
 
     return call(
-        only_on(parity, body), name, [weight, source, target, left16, count_l, dst, weight_rows],
-        [shape(2 * depth, edges, dtype=BF16), shape(edges, depth)],
-        scratch_shapes=scratch([shape(depth, edges), shape(edges, depth, dtype=BF16)]),
+        only_on(parity, body), name, [weight, source, target, left16, count_l, weight_rows, targets],
+        [shape(2 * depth, edges, dtype=BF16), shape(edges, depth), shape(edges, rows, dtype=BF16), shape(depth, edges)],
+        scratch_shapes=scratch([shape(edges, depth, dtype=BF16)]),
     )
 
 
@@ -445,25 +461,35 @@
     )
 
 
-def late_edges(parity, number, step, at, piece, ready, dst, target_rows, gq, rel, after):
-    (weight, source, query, query_rows, left16, _oh_src, oh_dst, count_l, count_r, kind, weight_rows) = ready
+def late_edges(parity, number, at, piece, ready, target_rows, weights, gp, gq, rel, after):
+    (weight, source, query, query_rows, left16, _oh_src, oh_dst, count_l, count_r, kind, weight_rows, targets) = ready
     depth, rows = left16.shape
     edges = weight.shape[1]
+    half = edges // 2
     pair16 = shape(2 * depth, edges, dtype=BF16)
 
-    def body(piece, weight, source, query, query_rows, left16, oh_dst, count_l, count_r, kind, dst, weight_rows,
-             held_rows, held_q, rel_in, _after,
-             rgrad, to_src, to_dst, rel_out, probe, weights, gp, probe_rows):
+    def body(piece, weight, source, query, query_rows, left16, oh_dst, count_l, count_r, kind, weight_rows, targets,
+             held_rows, _weights, _gp, held_q, rel_in, _after,
+             weights, gp, rel_out, rgrad, to_src, to_dst, probe, t_rows, probe_rows):
         size = piece.shape[1]
         parts = split(piece[...], 3)
         hits = oh_dst[:, at : at + size]
-        slab = jnp.concatenate(parts, axis=1)
-        table = jnp.concatenate([hits] * 3, axis=1)
-        t_rows = held_rows[...] + mul(table, slab, NT)
-        probe_rows[...] = half_product(weight_rows[...], t_rows)
-        source_scores(number, probe_rows, left16, count_l, gp, weights)
+        t_rows[...] = held_rows[...] + mul(
+            jnp.concatenate([hits] * 3, axis=1), jnp.concatenate(parts, axis=1), NT
+        )
+
+        def scores(some):
+            probe_rows[some, :] = half_product(weight_rows[some, :], t_rows[some, :])
+            source_scores(number, some, probe_rows, left16, count_l, gp, weights)
+
+        scores(slice(half, edges))
+
+        @pl.when(jnp.max(targets[:, 0:half]) >= at)
+        def _():
+            scores(slice(0, half))
+
         w, s = weight[...], source[...]
-        t = t_rows.T
+        t = t_rows[...].T
         probe[...] = (w * t).astype(BF16)
         rgrad[...], more = negatives(parts[0], query[...], query_rows[...], times_at(count_r, 0, size, at), number)
         q = held_q[...] + more
@@ -472,16 +498,17 @@
         g_weight = coef * s * t + q * s + p * t
         rel_out[...] = rel_in[...] + sum(mul(kind[...], part, NT) for part in split(g_weight, 2))
         to_src[0:depth, :], to_src[depth:, :] = split(coef * w * t + q * w, 2)
-        here = dst[step : step + 1, :] >= at
+        here = targets[...] >= at
         to_dst[0:depth, :], to_dst[depth:, :] = split(jnp.where(here, coef * w * s + p * w, 0.0), 2)
 
     return call(
         only_on(parity, body), "late_edges",
-        [piece, weight, source, query, query_rows, left16, oh_dst, count_l, count_r, kind, dst, weight_rows,
-         target_rows, gq, rel, after],
-        [shape(depth, piece.shape[1]), pair16, pair16, shape(*rel.shape), shape(depth, edges, dtype=BF16), shape(edges, rows, dtype=BF16)],
-        scratch_shapes=scratch([shape(depth, edges), shape(edges, depth, dtype=BF16)]),
-        aliases={14: 3},
+        [piece, weight, source, query, query_rows, left16, oh_dst, count_l, count_r, kind, weight_rows, targets,
+         target_rows, weights, gp, gq, rel, after],
+        [shape(edges, rows, dtype=BF16), shape(depth, edges), shape(*rel.shape),
+         shape(depth, piece.shape[1]), pair16, pair16, shape(depth, edges, dtype=BF16)],
+        scratch_shapes=scratch([shape(edges, depth), shape(edges, depth, dtype=BF16)]),
+        aliases={13: 0, 14: 1, 16: 2},
     )
 
 
@@ -614,7 +641,7 @@
     state_far = lax.ppermute(state_near, "blk", skip).reshape(1, rows)
     state_near = state_near.reshape(1, rows)
     rel = jnp.zeros(relations.shape, F32)
-    ready = prepared(0, left, relations, index)
+    ready = prepared(0, None, left, relations, index)
     left_a, lstate, far, rel, state = trained(1, "first_near", number, False, FAR, left, lstate, right_near, state_near, rel, ready)
     far = [lax.ppermute(piece, "blk", across) for piece in far]
     state = lax.ppermute(lax.ppermute(state, "blk", back), "blk", skip)
@@ -622,20 +649,22 @@
         0, "first_far", number, True, NEAR, left, lstate, [right_far], state_far, rel, ready, (left_a,), True, (state,)
     )
     near = [lax.ppermute(piece, "blk", inside) for piece in near]
-    ready = prepared(1, left_a, relations, index)
+    cuts = pieces_of(rows, FAR)
+    ready = prepared(1, cuts[-1][0], left_a, relations, index)
     first_lstate = lstate
     left_b, lstate, right_b, rel, _ = trained(1, "last_near", number, False, (), left_a, lstate, near, state_near, rel, ready)
-    cuts = pieces_of(rows, FAR)
     right_b, = right_b
     held = ()
     order = lstate
     for i, (at, size) in enumerate(cuts[:-1]):
         target, gq, rgrad = last_piece(0, "last_piece%d" % i, number, at, far[i], ready, order, held)
         held = (target, gq)
-        to_dst, target_rows = early_edges(0, "early_edges%d" % i, number, 1, at, at + size, target, ready, dst_index)
+        to_dst, target_rows, weights, gp = early_edges(0, "early_edges%d" % i, number, at, at + size, target, ready)
         right_b, order = early_right(0, "early_right%d" % i, at, far[i], state, rgrad, to_dst, ready[6], right_b, order)
     at = cuts[-1][0]
-    rgrad, to_src, to_dst, rel, probe, weights = late_edges(0, number, 1, at, far[-1], ready, dst_index, target_rows, gq, rel, order)
+    weights, gp, rel, rgrad, to_src, to_dst, probe = late_edges(
+        0, number, at, far[-1], ready, target_rows, weights, gp, gq, rel, order
+    )
     ahead, rel = ahead_left(0, left_a, first_lstate, to_src, ready[5], probe, weights, ready[7], rel)
     if lax.axis_size("rel") == 2:
         rels = [rel, lax.ppermute(rel, "rel", [(0, 1), (1, 0)])]

time: 88.1 us -> 88.1 us (level)
  Pallas kernels: 36.4 us -> 38.3 us
  waiting for transfers between devices: 22.5 us -> 20.7 us
    pallas_call x15, Pallas kernels: 36.4 us -> 38.3 us  [call(): pl.pallas_call(kernel, out_shape=tuple(shapes), in_specs=[large if i in i...]
    ppermute x3, waiting for transfers between devices: 3.42 us -> 1.65 us  [local(): far = [lax.ppermute(piece, 'blk', across) for piece in far]]
  transfers between devices with their start and end apart: 13 -> 13, of which waited for: 7 -> 6; matrix products, arithmetic and copies ran while one was open for 2% -> 2% of each run, Pallas kernels for 37% -> 39%
where the time goes in v4:
time: 88.1 us; the launch traced here: 87.8 us
  Pallas kernels  38.3 us (43%)
  starting transfers between devices  25.5 us (29%)
  waiting for transfers between devices  20.7 us (23%)
  local copies, waits for them, and re-layouts  2.21 us (3%)
  between operations  1 us (1%)
    pallas_call x15, Pallas kernels, call(): pl.pallas_call(kernel, out_shape=tuple(shapes), in_specs=[large if i in i...  38.3 us
    ppermute x2, waiting for transfers between devices, local(): state = lax.ppermute(lax.ppermute(state, 'blk', back), 'blk', skip)  15.5 us
    ppermute x2, starting transfers between devices, local(): lax.ppermute(right[:, at:at + size], 'blk', inside)  7.28 us
    ppermute x2, starting transfers between devices, local(): state = lax.ppermute(lax.ppermute(state, 'blk', back), 'blk', skip)  4.74 us
    ppermute x3, starting transfers between devices, local(): far = [lax.ppermute(piece, 'blk', across) for piece in far]  3.88 us
    ppermute x1, starting transfers between devices, local(): state_far = lax.ppermute(state_near, 'blk', skip).reshape(1, rows)  3.46 us
    ppermute x1, waiting for transfers between devices, local(): right_far = lax.ppermute(right, 'blk', across)  3.43 us
    ppermute x2, starting transfers between devices, local(): near = [lax.ppermute(piece, 'blk', inside) for piece in near]  2.79 us
  transfers between devices with their start and end apart: 13, of which 6 were waited for; matrix products, arithmetic and copies ran while one was open for 2% of the time, Pallas kernels for 39%

profile of v4, /device:TPU:0, one launch (start us, length us, event | category | flops | bytes accessed | tf_op | source)
XLA Modules:
  0.0 87.8 jit_solution(3164347043346572063)
XLA Ops:
  0.6 0.0 copy-start.9
  0.6 0.0 copy-start
  0.7 0.0 copy-start.1
  0.7 0.0 copy-start.2
  0.7 0.0 copy-start.3
  0.7 0.0 copy-start.5
  0.7 0.0 copy-start.6
  0.7 0.0 copy-start.7
  0.7 1.6 %collective-permute-start.4 = (f32[400,2048]{1,0:T(8,128)}, f32[400,2048]{1,0:T(8,128)S(1)}, u32[]{:S(2)}, u32[]{:S(2)}) collective-permute-start(f32[400,2048]{1,0:T(8,128)} %bitcast.18), channel_id=1, source_target_pairs={{2,4},{6,8},{10,12},{14,16},{18,20},{22,24},{26,28},{30,0},{3,5},{... | collective-permute-start | bytes 9830408 | tf_op jit(solution)/shard_map/ppermute | solution.py:638
  2.3 2.2 %fusion = (f32[400,1024]{1,0:T(8,128)S(1)}, f32[400,1024]{1,0:T(8,128)S(1)}) fusion(f32[400,2048]{1,0:T(8,128)} %bitcast.19), kind=kLoop, calls=%fused_computation | loop fusion | bytes 6553600 | tf_op jit(solution)/shard_map/slice | solution.py:639
  4.4 0.0 copy-start.4
  4.5 5.9 %collective-permute-start.2 = (f32[400,1024]{1,0:T(8,128)S(1)}, f32[400,1024]{1,0:T(8,128)S(1)}, u32[]{:S(2)}, u32[]{:S(2)}) collective-permute-start(f32[400,1024]{1,0:T(8,128)S(1)} %get-tuple-element.133), channel_id=1, source_target_pairs={{0,2},{4,6},{8,10},{12,14},{16,18},{20,22},{24,26},{28,30},{1,3},{... | collective-permute-start | bytes 4915208 | tf_op jit(solution)/shard_map/ppermute | solution.py:639
  10.3 1.4 %collective-permute-start.1 = (f32[400,1024]{1,0:T(8,128)S(1)}, f32[400,1024]{1,0:T(8,128)S(1)}, u32[]{:S(2)}, u32[]{:S(2)}) collective-permute-start(f32[400,1024]{1,0:T(8,128)S(1)} %get-tuple-element.134), channel_id=1, source_target_pairs={{0,2},{4,6},{8,10},{12,14},{16,18},{20,22},{24,26},{28,30},{1,3},{... | collective-permute-start | bytes 4915208 | tf_op jit(solution)/shard_map/ppermute | solution.py:639
  11.7 0.0 copy-done.9
  11.8 0.1 collective-permute-start
  11.8 0.0 copy-done
  11.8 0.0 copy-done.1
  11.9 0.0 copy-done.2
  11.9 0.0 copy-done.3
  11.9 0.0 copy-done.5
  11.9 0.0 copy-done.6
  11.9 0.0 copy-done.7
  11.9 3.8 %prepare0.1 = (f32[400,256]{1,0:T(8,128)S(1)}, f32[400,256]{1,0:T(8,128)S(1)}, bf16[400,256]{1,0:T(8,128)(2,1)S(1)}, bf16[256,400]{1,0:T(8,128)(2,1)S(1)}, bf16[...) custom-call(f32[400,2048]{1,0:T(8,128)S(1)} %bitcast.9, ...), custom_call_target="tpu_custom_call" | custom-call | flops 1000000 | bytes 100000 | tf_op jit(solution)/shard_map/prepare0/pallas_call | solution.py:352
  15.7 0.0 collective-permute-done
  15.7 0.0 collective-permute-done.2.refs_17_
  15.7 0.0 collective-permute-done.1.refs_16_
  15.7 0.0 copy-done.4
  15.7 0.2 first_near.1
  15.9 1.3 %collective-permute-start.9 = (f32[400,1280]{1,0:T(8,128)S(1)}, f32[400,1280]{1,0:T(8,128)S(1)}, u32[]{:S(2)}, u32[]{:S(2)}) collective-permute-start(f32[400,1280]{1,0:T(8,128)S(1)} %get-tuple-element.99), channel_id=1, source_target_pairs={{2,4},{6,8},{10,12},{14,16},{18,20},{22,24},{26,28},{30,0},{3,5},{... | collective-permute-start | bytes 6144008 | tf_op jit(solution)/shard_map/ppermute | solution.py:646
  17.2 1.3 %collective-permute-start.5 = (f32[1,2048]{1,0:T(1,128)S(1)}, f32[1,2048]{1,0:T(1,128)S(1)}, u32[]{:S(2)}, u32[]{:S(2)}) collective-permute-start(f32[1,2048]{1,0:T(1,128)S(1)} %get-tuple-element.83), channel_id=1, source_target_pairs={{2,0},{6,4},{10,8},{14,12},{18,16},{22,20},{26,24},{30,28},{3,1},{... | collective-permute-start | bytes 24584 | tf_op jit(solution)/shard_map/ppermute | solution.py:647
  18.5 3.5 %collective-permute-start.3 = (f32[2048]{0:T(1024)S(1)}, f32[2048]{0:T(1024)S(1)}, u32[]{:S(2)}, u32[]{:S(2)}) collective-permute-start(f32[2048]{0:T(1024)S(1)} %collective-permute-done), channel_id=1, source_target_pairs={{0,4},{4,8},{8,12},{12,16},{16,20},{20,24},{24,28},{28,0},{1,5},{5... | collective-permute-start | bytes 24584 | tf_op jit(solution)/shard_map/ppermute | solution.py:641
  22.0 10.6 %collective-permute-done.5 = f32[1,2048]{1,0:T(1,128)S(1)} collective-permute-done((f32[1,2048]{1,0:T(1,128)S(1)}, f32[1,2048]{1,0:T(1,128)S(1)}, u32[]{:S(2)}, u32[]{:S(2)}) %collective-permute-start.5) | collective-permute-done | bytes 8224 | tf_op jit(solution)/shard_map/ppermute | solution.py:647
  32.6 3.4 %collective-permute-start.6 = (f32[1,2048]{1,0:T(1,128)S(1)}, f32[1,2048]{1,0:T(1,128)S(1)}, u32[]{:S(2)}, u32[]{:S(2)}) collective-permute-start(f32[1,2048]{1,0:T(1,128)S(1)} %collective-permute-done.5), channel_id=1, source_target_pairs={{0,4},{4,8},{8,12},{12,16},{16,20},{20,24},{24,28},{28,0},{1,5},{5... | collective-permute-start | bytes 24584 | tf_op jit(solution)/shard_map/ppermute | solution.py:647
  36.0 0.0 collective-permute-done.3
  36.1 4.9 %collective-permute-done.6.refs_18_.refs_1_.refs_9_ = f32[1,2048]{1,0:T(1,128)S(1)} collective-permute-done((f32[1,2048]{1,0:T(1,128)S(1)}, f32[1,2048]{1,0:T(1,128)S(1)}, u32[]{:S(2)}, u32[]{:S(2)}) %collective-permute-start.6) | collective-permute-done | bytes 8224 | tf_op jit(solution)/shard_map/ppermute | solution.py:647
  41.0 3.4 %collective-permute-done.4.refs_16_ = f32[400,2048]{1,0:T(8,128)S(1)} collective-permute-done((f32[400,2048]{1,0:T(8,128)}, f32[400,2048]{1,0:T(8,128)S(1)}, u32[]{:S(2)}, u32[]{:S(2)}) %collective-permute-start.4) | collective-permute-done | bytes 3276832 | tf_op jit(solution)/shard_map/ppermute | solution.py:638
  44.4 11.6 %first_far.1 = (f32[400,2048]{1,0:T(8,128)S(1)}, f32[1,2048]{1,0:T(1,128)S(1)}, f32[32,400]{1,0:T(8,128)S(1)}, f32[408,1024]{1,0:T(8,128)S(1)}, f32[400,1024]{1,0:T(8,128)}, /*index=5*/f32[1,2048]{1,0:T(1,128)}) custom-call(f32[400,2048]{1,0:T(8,128)S(1)} %bitcast.11, f32[1,2048]{1,0:T(1,128)S(1)} %get-tuple-element.80.refs_1_, ...), custom_call_target="tpu_custom_call", output_to_operand_aliasing={{0}: (17, {})} | custom-call | flops 1000000 | bytes 100000 | tf_op jit(solution)/shard_map/first_far/pallas_call | solution.py:352
  56.0 1.4 %collective-permute-start.10 = (f32[408,1024]{1,0:T(8,128)S(1)}, f32[408,1024]{1,0:T(8,128)S(1)}, u32[]{:S(2)}, u32[]{:S(2)}) collective-permute-start(f32[408,1024]{1,0:T(8,128)S(1)} %get-tuple-element.102), channel_id=1, source_target_pairs={{0,2},{4,6},{8,10},{12,14},{16,18},{20,22},{24,26},{28,30},{1,3},{... | collective-permute-start | bytes 5013512 | tf_op jit(solution)/shard_map/ppermute | solution.py:651
  57.4 1.4 %collective-permute-start.11 = (f32[400,1024]{1,0:T(8,128)}, f32[400,1024]{1,0:T(8,128)S(1)}, u32[]{:S(2)}, u32[]{:S(2)}) collective-permute-start(f32[400,1024]{1,0:T(8,128)} %get-tuple-element.103), channel_id=1, source_target_pairs={{0,2},{4,6},{8,10},{12,14},{16,18},{20,22},{24,26},{28,30},{1,3},{... | collective-permute-start | bytes 4915208 | tf_op jit(solution)/shard_map/ppermute | solution.py:651
  58.8 1.3 %collective-permute-start.8 = (f32[400,512]{1,0:T(8,128)S(1)}, f32[400,512]{1,0:T(8,128)S(1)}, u32[]{:S(2)}, u32[]{:S(2)}) collective-permute-start(f32[400,512]{1,0:T(8,128)S(1)} %get-tuple-element.98), channel_id=1, source_target_pairs={{2,4},{6,8},{10,12},{14,16},{18,20},{22,24},{26,28},{30,0},{3,5},{... | collective-permute-start | bytes 2457608 | tf_op jit(solution)/shard_map/ppermute | solution.py:646
  60.1 1.3 %collective-permute-start.7 = (f32[400,256]{1,0:T(8,128)S(1)}, f32[400,256]{1,0:T(8,128)S(1)}, u32[]{:S(2)}, u32[]{:S(2)}) collective-permute-start(f32[400,256]{1,0:T(8,128)S(1)} %get-tuple-element.86), channel_id=1, source_target_pairs={{2,4},{6,8},{10,12},{14,16},{18,20},{22,24},{26,28},{30,0},{3,5},{... | collective-permute-start | bytes 1228808 | tf_op jit(solution)/shard_map/ppermute | solution.py:646
  61.4 4.2 %prepare1.1 = (f32[400,256]{1,0:T(8,128)S(1)}, f32[400,256]{1,0:T(8,128)S(1)}, bf16[400,256]{1,0:T(8,128)(2,1)S(1)}, bf16[256,400]{1,0:T(8,128)(2,1)S(1)}, bf16[...) custom-call(f32[400,2048]{1,0:T(8,128)S(1)} %get-tuple-element.84.le, ...), custom_call_target="tpu_custom_call" | custom-call | flops 1000000 | bytes 100000 | tf_op jit(solution)/shard_map/prepare1/pallas_call | solution.py:352
  65.6 0.0 collective-permute-done.11.refs_17_
  65.6 0.0 collective-permute-done.10.refs_16_
  65.6 0.8 last_near.1
  66.4 0.0 collective-permute-done.9.refs_0_
  66.4 2.8 %last_piece0.1 = (f32[400,256]{1,0:T(8,128)S(1)}, f32[400,256]{1,0:T(8,128)S(1)}, f32[400,1280]{1,0:T(8,128)S(1)}) custom-call(f32[400,1280]{1,0:T(8,128)S(1)} %collective-permute-done.9.refs_0_, bf16[400,256]{1,0:T(8,128)(2,1)S(1)} %get-tuple-element.89.refs_6_.refs_1_.refs_3_, bf16[256,400]{1,0:T(8,128)(2,1)S(1)} %get-tuple-element.90.refs_7_.refs_2_.refs_4_, ...), custom_call_target="tpu_custom_call" | custom-call | flops 1000000 | bytes 100000 | tf_op jit(solution)/shard_map/last_piece0/pallas_call | solution.py:352
  69.2 2.7 %early_edges0.1 = (bf16[800,256]{1,0:T(8,128)(2,1)S(1)}, f32[256,400]{1,0:T(8,128)}, bf16[256,2048]{1,0:T(8,128)(2,1)}, f32[400,256]{1,0:T(8,128)}) custom-call(f32[400,256]{1,0:T(8,128)S(1)} %get-tuple-element.87.refs_4_.refs_0_.refs_1_, f32[400,256]{1,0:T(8,128)S(1)} %get-tuple-element.88.refs_5_.refs_1_.refs_2_, ...), custom_call_target="tpu_custom_call" | custom-call | flops 1000000 | bytes 100000 | tf_op jit(solution)/shard_map/early_edges0/pallas_call | solution.py:352
  71.8 1.9 %early_right0.1 = (f32[400,2048]{1,0:T(8,128)}, f32[1,2048]{1,0:T(1,128)S(1)}) custom-call(f32[400,1280]{1,0:T(8,128)S(1)} %collective-permute-done.9.refs_0_, f32[1,2048]{1,0:T(1,128)S(1)} %collective-permute-done.6.refs_18_.refs_1_.refs_9_, f32[400,1280]{1,0:T(8,128)S(1)} %get-tuple-element.107.refs_2_, ...), custom_call_target="tpu_custom_call", output_to_operand_aliasing={{1}: (5, {}), {0}: (6, {})} | custom-call | flops 1000000 | bytes 100000 | tf_op jit(solution)/shard_map/early_right0/pallas_call | solution.py:352
  73.8 1.4 %collective-permute-done.8.refs_0_ = f32[400,512]{1,0:T(8,128)S(1)} collective-permute-done((f32[400,512]{1,0:T(8,128)S(1)}, f32[400,512]{1,0:T(8,128)S(1)}, u32[]{:S(2)}, u32[]{:S(2)}) %collective-permute-start.8) | collective-permute-done | bytes 819232 | tf_op jit(solution)/shard_map/ppermute | solution.py:646
  75.2 1.2 %last_piece1.1 = (f32[400,256]{1,0:T(8,128)S(1)}, f32[400,256]{1,0:T(8,128)S(1)}, f32[400,512]{1,0:T(8,128)S(1)}) custom-call(f32[400,512]{1,0:T(8,128)S(1)} %collective-permute-done.8.refs_0_, bf16[400,256]{1,0:T(8,128)(2,1)S(1)} %get-tuple-element.89.refs_6_.refs_1_.refs_3_, ...), custom_call_target="tpu_custom_call", output_to_operand_aliasing={{0}: (5, {}), {1}: (6, {})} | custom-call | flops 1000000 | bytes 100000 | tf_op jit(solution)/shard_map/last_piece1/pallas_call | solution.py:352
  76.4 1.4 %early_edges1.1 = (bf16[800,256]{1,0:T(8,128)(2,1)S(1)}, f32[256,400]{1,0:T(8,128)S(1)}, bf16[256,2048]{1,0:T(8,128)(2,1)S(1)}, f32[400,256]{1,0:T(8,128)S(1)}) custom-call(f32[400,256]{1,0:T(8,128)S(1)} %get-tuple-element.87.refs_4_.refs_0_.refs_1_, f32[400,256]{1,0:T(8,128)S(1)} %get-tuple-element.88.refs_5_.refs_1_.refs_2_, ...), custom_call_target="tpu_custom_call" | custom-call | flops 1000000 | bytes 100000 | tf_op jit(solution)/shard_map/early_edges1/pallas_call | solution.py:352
  77.8 1.5 %early_right1.1 = (f32[400,2048]{1,0:T(8,128)}, f32[1,2048]{1,0:T(1,128)S(1)}) custom-call(f32[400,512]{1,0:T(8,128)S(1)} %collective-permute-done.8.refs_0_, f32[1,2048]{1,0:T(1,128)S(1)} %collective-permute-done.6.refs_18_.refs_1_.refs_9_, f32[400,512]{1,0:T(8,128)S(1)} %get-tuple-element.117.refs_2_, ...), custom_call_target="tpu_custom_call", output_to_operand_aliasing={{1}: (5, {}), {0}: (6, {})} | custom-call | flops 1000000 | bytes 100000 | tf_op jit(solution)/shard_map/early_right1/pallas_call | solution.py:352
  79.3 0.2 collective-permute-done.7.refs_0_.refs_8_
  79.5 2.3 %late_edges.1 = (bf16[256,2048]{1,0:T(8,128)(2,1)S(1)}, f32[400,256]{1,0:T(8,128)S(1)}, f32[32,400]{1,0:T(8,128)S(1)}, f32[400,256]{1,0:T(8,128)S(1)}, bf16[800,...) custom-call(f32[400,256]{1,0:T(8,128)S(1)} %collective-permute-done., ...), custom_call_target="tpu_custom_call", output_to_operand_aliasing={{0}: (13, {}), {1}: (14, {}), {2}: (16, {})} | custom-call | flops 1000000 | bytes 100000 | tf_op jit(solution)/shard_map/late_edges/pallas_call | solution.py:352
  81.8 0.9 %ahead_left.1 = (f32[400,768]{1,0:T(8,128)S(1)}, f32[32,400]{1,0:T(8,128)S(1)}) custom-call(f32[400,2048]{1,0:T(8,128)S(1)} %get-tuple-element.84.left.refs_0_, f32[1,2048]{1,0:T(1,128)S(1)} %get-tuple-element.85.refs_1_, bf16[800,256]{1,0:T(8,128)(2,1)S(1)} %get-tuple-element.121.refs_2_, ...), custom_call_target="tpu_custom_call", output_to_operand_aliasing={{1}: (7, {})} | custom-call | flops 1000000 | bytes 100000 | tf_op jit(solution)/shard_map/ahead_left/pallas_call | solution.py:352
  82.7 1.8 %collective-permute-start.12 = (f32[32,400]{1,0:T(8,128)S(1)}, f32[32,400]{1,0:T(8,128)S(1)}, u32[]{:S(2)}, u32[]{:S(2)}) collective-permute-start(f32[32,400]{1,0:T(8,128)S(1)} %get-tuple-element.132.rest_0_), channel_id=1, source_target_pairs={{0,1},{1,0},{2,3},{3,2},{4,5},{5,4},{6,7},{7,6},{8,9},{9,8},{10,11... | collective-permute-start | bytes 153608 | tf_op jit(solution)/shard_map/ppermute | solution.py:670
  84.5 0.0 copy-start.8
  84.5 2.5 %late_slabs.1 = (f32[400,2048]{1,0:T(8,128)}, f32[400,2048]{1,0:T(8,128)}) custom-call(f32[400,2048]{1,0:T(8,128)S(1)} %get-tuple-element.84.left.refs_0_, f32[1,2048]{1,0:T(1,128)S(1)} %get-tuple-element.85.refs_1_, bf16[800,256]{1,0:T(8,128)(2,1)S(1)} %get-tuple-element.121.refs_2_, ...), custom_call_target="tpu_custom_call", output_to_operand_aliasing={{0}: (13, {}), {1}: (14, {})} | custom-call | flops 1000000 | bytes 100000 | tf_op jit(solution)/shard_map/late_slabs/pallas_call | solution.py:352
  87.0 0.1 collective-permute-done.12.rest_1_
  87.1 0.0 copy-done.8
  87.1 0.7 relation_update.1
  (1 shorter events, 0.0 us)
Async XLA Ops:
  0.6 11.1 %copy-start.9 = (f32[2048]{0:T(1024)S(1)}, f32[2048]{0:T(1024)}, u32[]{:S(2)}) copy-start(f32[2048]{0:T(1024)} %param.14) | copy-start | bytes 24580
  0.6 11.2 %copy-start = (f32[2048,400]{0,1:T(8,128)S(1)}, f32[2048,400]{0,1:T(8,128)}, u32[]{:S(2)}) copy-start(f32[2048,400]{0,1:T(8,128)} %param.11) | copy-start | bytes 9830404
  0.7 11.2 %copy-start.1 = (f32[32,400]{1,0:T(8,128)S(1)}, f32[32,400]{1,0:T(8,128)}, u32[]{:S(2)}) copy-start(f32[32,400]{1,0:T(8,128)} %relations.5) | copy-start | bytes 153604
  0.7 11.2 %copy-start.2 = (s32[2,1000]{1,0:T(2,128)S(1)}, s32[2,1000]{1,0:T(2,128)}, u32[]{:S(2)}) copy-start(s32[2,1000]{1,0:T(2,128)} %nsrc.3) | copy-start | bytes 24004
  0.7 11.2 %copy-start.3 = (s32[2,1000]{1,0:T(2,128)S(1)}, s32[2,1000]{1,0:T(2,128)}, u32[]{:S(2)}) copy-start(s32[2,1000]{1,0:T(2,128)} %ndst.3) | copy-start | bytes 24004
  0.7 11.2 %copy-start.5 = (s32[2,256]{1,0:T(2,128)S(1)}, s32[2,256]{1,0:T(2,128)}, u32[]{:S(2)}) copy-start(s32[2,256]{1,0:T(2,128)} %src.3) | copy-start | bytes 6148
  0.7 11.2 %copy-start.6 = (s32[2,256]{1,0:T(2,128)S(1)}, s32[2,256]{1,0:T(2,128)}, u32[]{:S(2)}) copy-start(s32[2,256]{1,0:T(2,128)} %dst.3) | copy-start | bytes 6148
  0.7 11.2 %copy-start.7 = (s32[2,256]{1,0:T(2,128)S(1)}, s32[2,256]{1,0:T(2,128)}, u32[]{:S(2)}) copy-start(s32[2,256]{1,0:T(2,128)} %rid.3) | copy-start | bytes 6148
  0.7 43.7 %collective-permute-start.4 = (f32[400,2048]{1,0:T(8,128)}, f32[400,2048]{1,0:T(8,128)S(1)}, u32[]{:S(2)}, u32[]{:S(2)}) collective-permute-start(f32[400,2048]{1,0:T(8,128)} %bitcast.18), channel_id=1, source_target_pairs={{2,4},{6,8},{10,12},{14,16},{18,20},{22,24},{26,28},{30,0},{3,5},{... | collective-permute-start | bytes 9830408 | tf_op jit(solution)/shard_map/ppermute | solution.py:638
  4.4 11.3 %copy-start.4 = (f32[2048]{0:T(1024)S(1)}, f32[2048]{0:T(1024)}, u32[]{:S(2)}) copy-start(f32[2048]{0:T(1024)} %param.12) | copy-start | bytes 24580
  4.5 11.3 %collective-permute-start.2 = (f32[400,1024]{1,0:T(8,128)S(1)}, f32[400,1024]{1,0:T(8,128)S(1)}, u32[]{:S(2)}, u32[]{:S(2)}) collective-permute-start(f32[400,1024]{1,0:T(8,128)S(1)} %get-tuple-element.133), channel_id=1, source_target_pairs={{0,2},{4,6},{8,10},{12,14},{16,18},{20,22},{24,26},{28,30},{1,3},{... | collective-permute-start | bytes 4915208 | tf_op jit(solution)/shard_map/ppermute | solution.py:639
  10.3 5.4 %collective-permute-start.1 = (f32[400,1024]{1,0:T(8,128)S(1)}, f32[400,1024]{1,0:T(8,128)S(1)}, u32[]{:S(2)}, u32[]{:S(2)}) collective-permute-start(f32[400,1024]{1,0:T(8,128)S(1)} %get-tuple-element.134), channel_id=1, source_target_pairs={{0,2},{4,6},{8,10},{12,14},{16,18},{20,22},{24,26},{28,30},{1,3},{... | collective-permute-start | bytes 4915208 | tf_op jit(solution)/shard_map/ppermute | solution.py:639
  11.8 4.0 %collective-permute-start = (f32[2048]{0:T(1024)S(1)}, f32[2048]{0:T(1024)S(1)}, u32[]{:S(2)}, u32[]{:S(2)}) collective-permute-start(f32[2048]{0:T(1024)S(1)} %copy-done.9), channel_id=1, source_target_pairs={{0,2},{4,6},{8,10},{12,14},{16,18},{20,22},{24,26},{28,30},{2,0},{... | collective-permute-start | bytes 24584 | tf_op jit(solution)/shard_map/ppermute | solution.py:640
  15.9 50.5 %collective-permute-start.9 = (f32[400,1280]{1,0:T(8,128)S(1)}, f32[400,1280]{1,0:T(8,128)S(1)}, u32[]{:S(2)}, u32[]{:S(2)}) collective-permute-start(f32[400,1280]{1,0:T(8,128)S(1)} %get-tuple-element.99), channel_id=1, source_target_pairs={{2,4},{6,8},{10,12},{14,16},{18,20},{22,24},{26,28},{30,0},{3,5},{... | collective-permute-start | bytes 6144008 | tf_op jit(solution)/shard_map/ppermute | solution.py:646
  17.2 15.4 %collective-permute-start.5 = (f32[1,2048]{1,0:T(1,128)S(1)}, f32[1,2048]{1,0:T(1,128)S(1)}, u32[]{:S(2)}, u32[]{:S(2)}) collective-permute-start(f32[1,2048]{1,0:T(1,128)S(1)} %get-tuple-element.83), channel_id=1, source_target_pairs={{2,0},{6,4},{10,8},{14,12},{18,16},{22,20},{26,24},{30,28},{3,1},{... | collective-permute-start | bytes 24584 | tf_op jit(solution)/shard_map/ppermute | solution.py:647
  18.5 17.5 %collective-permute-start.3 = (f32[2048]{0:T(1024)S(1)}, f32[2048]{0:T(1024)S(1)}, u32[]{:S(2)}, u32[]{:S(2)}) collective-permute-start(f32[2048]{0:T(1024)S(1)} %collective-permute-done), channel_id=1, source_target_pairs={{0,4},{4,8},{8,12},{12,16},{16,20},{20,24},{24,28},{28,0},{1,5},{5... | collective-permute-start | bytes 24584 | tf_op jit(solution)/shard_map/ppermute | solution.py:641
  32.6 8.4 %collective-permute-start.6 = (f32[1,2048]{1,0:T(1,128)S(1)}, f32[1,2048]{1,0:T(1,128)S(1)}, u32[]{:S(2)}, u32[]{:S(2)}) collective-permute-start(f32[1,2048]{1,0:T(1,128)S(1)} %collective-permute-done.5), channel_id=1, source_target_pairs={{0,4},{4,8},{8,12},{12,16},{16,20},{20,24},{24,28},{28,0},{1,5},{5... | collective-permute-start | bytes 24584 | tf_op jit(solution)/shard_map/ppermute | solution.py:647
  56.0 9.6 %collective-permute-start.10 = (f32[408,1024]{1,0:T(8,128)S(1)}, f32[408,1024]{1,0:T(8,128)S(1)}, u32[]{:S(2)}, u32[]{:S(2)}) collective-permute-start(f32[408,1024]{1,0:T(8,128)S(1)} %get-tuple-element.102), channel_id=1, source_target_pairs={{0,2},{4,6},{8,10},{12,14},{16,18},{20,22},{24,26},{28,30},{1,3},{... | collective-permute-start | bytes 5013512 | tf_op jit(solution)/shard_map/ppermute | solution.py:651
  57.4 8.2 %collective-permute-start.11 = (f32[400,1024]{1,0:T(8,128)}, f32[400,1024]{1,0:T(8,128)S(1)}, u32[]{:S(2)}, u32[]{:S(2)}) collective-permute-start(f32[400,1024]{1,0:T(8,128)} %get-tuple-element.103), channel_id=1, source_target_pairs={{0,2},{4,6},{8,10},{12,14},{16,18},{20,22},{24,26},{28,30},{1,3},{... | collective-permute-start | bytes 4915208 | tf_op jit(solution)/shard_map/ppermute | solution.py:651
  58.8 16.4 %collective-permute-start.8 = (f32[400,512]{1,0:T(8,128)S(1)}, f32[400,512]{1,0:T(8,128)S(1)}, u32[]{:S(2)}, u32[]{:S(2)}) collective-permute-start(f32[400,512]{1,0:T(8,128)S(1)} %get-tuple-element.98), channel_id=1, source_target_pairs={{2,4},{6,8},{10,12},{14,16},{18,20},{22,24},{26,28},{30,0},{3,5},{... | collective-permute-start | bytes 2457608 | tf_op jit(solution)/shard_map/ppermute | solution.py:646
  60.1 19.4 %collective-permute-start.7 = (f32[400,256]{1,0:T(8,128)S(1)}, f32[400,256]{1,0:T(8,128)S(1)}, u32[]{:S(2)}, u32[]{:S(2)}) collective-permute-start(f32[400,256]{1,0:T(8,128)S(1)} %get-tuple-element.86), channel_id=1, source_target_pairs={{2,4},{6,8},{10,12},{14,16},{18,20},{22,24},{26,28},{30,0},{3,5},{... | collective-permute-start | bytes 1228808 | tf_op jit(solution)/shard_map/ppermute | solution.py:646
  82.7 4.3 %collective-permute-start.12 = (f32[32,400]{1,0:T(8,128)S(1)}, f32[32,400]{1,0:T(8,128)S(1)}, u32[]{:S(2)}, u32[]{:S(2)}) collective-permute-start(f32[32,400]{1,0:T(8,128)S(1)} %get-tuple-element.132.rest_0_), channel_id=1, source_target_pairs={{0,1},{1,0},{2,3},{3,2},{4,5},{5,4},{6,7},{7,6},{8,9},{9,8},{10,11... | collective-permute-start | bytes 153608 | tf_op jit(solution)/shard_map/ppermute | solution.py:670
  84.5 2.6 %copy-start.8 = (f32[32]{0:T(128)S(1)}, f32[32]{0:T(128)}, u32[]{:S(2)}) copy-start(f32[32]{0:T(128)} %param.16) | copy-start | bytes 388

commit v5 on v3

--- a/solution.py
+++ b/solution.py
@@ -508,9 +508,7 @@
     def body(left, lstate, to_src, oh_src, probe, weights, count_l, _rel, result, _rel_out):
         @pl.when(first_along_rel())
         def _():
-            for i in range(ahead_rows(rows) // 256):
-                cut = slice(i * 256, (i + 1) * 256)
-                result[:, cut] = left_rows(cut, left, lstate, to_src, oh_src, probe, weights, count_l)
+            result[...] = left_rows(slice(0, ahead_rows(rows)), left, lstate, to_src, oh_src, probe, weights, count_l)
 
     return call(
         only_on(parity, body), "ahead_left", [left, lstate, to_src, oh_src, probe, weights, count_l, rel],
@@ -527,14 +525,6 @@
         def made_ahead():
             return pltpu.make_async_copy(ahead, left_out.at[:, 0 : ahead_rows(rows)], sems.at[0, 0])
 
-        def runs(start, stop):
-            out = []
-            while start < stop:
-                size = 512 if start % 512 == 0 and start + 512 < rows and start + 512 <= stop else 256
-                out.append(slice(start, start + size))
-                start += size
-            return out
-
         def copy(cut):
             return pltpu.make_async_copy(result.at[:, cut], left_out.at[:, cut], sems.at[0, cut.start // 256])
 
@@ -542,7 +532,8 @@
             result[:, cut] = left_rows(cut, left, lstate, to_src, oh_src, probe, weights, count_l)
             copy(cut).start()
 
-        first, others = runs(0, ahead_rows(rows)), runs(ahead_rows(rows), rows)
+        first = [slice(0, ahead_rows(rows))]
+        others = [slice(ahead_rows(rows), rows - 256), slice(rows - 256, rows)]
 
         @pl.when(first_along_rel())
         def _():

time: 88.1 us -> 88.4 us (level)
  no operation moved by 1% of the time
where the time goes in v5:
time: 88.4 us; the launch traced here: 88.1 us
  Pallas kernels  36.8 us (42%)
  starting transfers between devices  25.6 us (29%)
  waiting for transfers between devices  22.5 us (25%)
  local copies, waits for them, and re-layouts  2.21 us (2%)
  between operations  1.02 us (1%)
    pallas_call x15, Pallas kernels, call(): pl.pallas_call(kernel, out_shape=tuple(shapes), in_specs=[large if i in i...  36.8 us
    ppermute x2, waiting for transfers between devices, local(): state = lax.ppermute(lax.ppermute(state, 'blk', back), 'blk', skip)  16.1 us
    ppermute x2, starting transfers between devices, local(): lax.ppermute(right[:, at:at + size], 'blk', inside)  7.28 us
    ppermute x2, starting transfers between devices, local(): state = lax.ppermute(lax.ppermute(state, 'blk', back), 'blk', skip)  4.74 us
    ppermute x3, starting transfers between devices, local(): far = [lax.ppermute(piece, 'blk', across) for piece in far]  3.88 us
    ppermute x1, starting transfers between devices, local(): state_far = lax.ppermute(state_near, 'blk', skip).reshape(1, rows)  3.46 us
    ppermute x3, waiting for transfers between devices, local(): far = [lax.ppermute(piece, 'blk', across) for piece in far]  3.42 us
    ppermute x1, waiting for transfers between devices, local(): right_far = lax.ppermute(right, 'blk', across)  2.87 us
  transfers between devices with their start and end apart: 13, of which 7 were waited for; matrix products, arithmetic and copies ran while one was open for 2% of the time, Pallas kernels for 37%

profile of v5, /device:TPU:0, one launch (start us, length us, event | category | flops | bytes accessed | tf_op | source)
XLA Modules:
  0.0 88.1 jit_solution(9991648314554265354)
XLA Ops:
  0.6 0.0 copy-start.9
  0.6 0.0 copy-start
  0.7 0.0 copy-start.1
  0.7 0.0 copy-start.2
  0.7 0.0 copy-start.3
  0.7 0.0 copy-start.4
  0.7 0.0 copy-start.6
  0.7 0.0 copy-start.7
  0.7 1.6 %collective-permute-start.4 = (f32[400,2048]{1,0:T(8,128)}, f32[400,2048]{1,0:T(8,128)S(1)}, u32[]{:S(2)}, u32[]{:S(2)}) collective-permute-start(f32[400,2048]{1,0:T(8,128)} %bitcast.18), channel_id=1, source_target_pairs={{2,4},{6,8},{10,12},{14,16},{18,20},{22,24},{26,28},{30,0},{3,5},{... | collective-permute-start | bytes 9830408 | tf_op jit(solution)/shard_map/ppermute | solution.py:602
  2.3 2.2 %fusion = (f32[400,1024]{1,0:T(8,128)S(1)}, f32[400,1024]{1,0:T(8,128)S(1)}) fusion(f32[400,2048]{1,0:T(8,128)} %bitcast.19), kind=kLoop, calls=%fused_computation | loop fusion | bytes 6553600 | tf_op jit(solution)/shard_map/slice | solution.py:603
  4.4 0.0 copy-start.5
  4.4 5.9 %collective-permute-start.2 = (f32[400,1024]{1,0:T(8,128)S(1)}, f32[400,1024]{1,0:T(8,128)S(1)}, u32[]{:S(2)}, u32[]{:S(2)}) collective-permute-start(f32[400,1024]{1,0:T(8,128)S(1)} %get-tuple-element.125), channel_id=1, source_target_pairs={{0,2},{4,6},{8,10},{12,14},{16,18},{20,22},{24,26},{28,30},{1,3},{... | collective-permute-start | bytes 4915208 | tf_op jit(solution)/shard_map/ppermute | solution.py:603
  10.3 1.4 %collective-permute-start.1 = (f32[400,1024]{1,0:T(8,128)S(1)}, f32[400,1024]{1,0:T(8,128)S(1)}, u32[]{:S(2)}, u32[]{:S(2)}) collective-permute-start(f32[400,1024]{1,0:T(8,128)S(1)} %get-tuple-element.126), channel_id=1, source_target_pairs={{0,2},{4,6},{8,10},{12,14},{16,18},{20,22},{24,26},{28,30},{1,3},{... | collective-permute-start | bytes 4915208 | tf_op jit(solution)/shard_map/ppermute | solution.py:603
  11.7 0.0 copy-done.9
  11.8 0.1 collective-permute-start
  11.8 0.0 copy-done
  11.8 0.0 copy-done.1
  11.9 0.0 copy-done.2
  11.9 0.0 copy-done.3
  11.9 0.0 copy-done.4
  11.9 0.0 copy-done.6
  11.9 0.0 copy-done.7
  11.9 3.7 %prepare0.1 = (f32[400,256]{1,0:T(8,128)S(1)}, f32[400,256]{1,0:T(8,128)S(1)}, bf16[400,256]{1,0:T(8,128)(2,1)S(1)}, bf16[256,400]{1,0:T(8,128)(2,1)S(1)}, bf16[...) custom-call(f32[400,2048]{1,0:T(8,128)S(1)} %bitcast.9, ...), custom_call_target="tpu_custom_call" | custom-call | flops 1000000 | bytes 100000 | tf_op jit(solution)/shard_map/prepare0/pallas_call | solution.py:328
  15.6 0.1 collective-permute-done
  15.7 0.0 collective-permute-done.2.refs_16_
  15.7 0.0 collective-permute-done.1.refs_15_
  15.7 0.0 copy-done.5
  15.7 0.2 first_near.1
  15.9 1.3 %collective-permute-start.9 = (f32[400,1280]{1,0:T(8,128)S(1)}, f32[400,1280]{1,0:T(8,128)S(1)}, u32[]{:S(2)}, u32[]{:S(2)}) collective-permute-start(f32[400,1280]{1,0:T(8,128)S(1)} %get-tuple-element.93), channel_id=1, source_target_pairs={{2,4},{6,8},{10,12},{14,16},{18,20},{22,24},{26,28},{30,0},{3,5},{... | collective-permute-start | bytes 6144008 | tf_op jit(solution)/shard_map/ppermute | solution.py:610
  17.2 1.3 %collective-permute-start.5 = (f32[1,2048]{1,0:T(1,128)S(1)}, f32[1,2048]{1,0:T(1,128)S(1)}, u32[]{:S(2)}, u32[]{:S(2)}) collective-permute-start(f32[1,2048]{1,0:T(1,128)S(1)} %get-tuple-element.78), channel_id=1, source_target_pairs={{2,0},{6,4},{10,8},{14,12},{18,16},{22,20},{26,24},{30,28},{3,1},{... | collective-permute-start | bytes 24584 | tf_op jit(solution)/shard_map/ppermute | solution.py:611
  18.5 3.5 %collective-permute-start.3 = (f32[2048]{0:T(1024)S(1)}, f32[2048]{0:T(1024)S(1)}, u32[]{:S(2)}, u32[]{:S(2)}) collective-permute-start(f32[2048]{0:T(1024)S(1)} %collective-permute-done), channel_id=1, source_target_pairs={{0,4},{4,8},{8,12},{12,16},{16,20},{20,24},{24,28},{28,0},{1,5},{5... | collective-permute-start | bytes 24584 | tf_op jit(solution)/shard_map/ppermute | solution.py:605
  22.0 11.2 %collective-permute-done.5 = f32[1,2048]{1,0:T(1,128)S(1)} collective-permute-done((f32[1,2048]{1,0:T(1,128)S(1)}, f32[1,2048]{1,0:T(1,128)S(1)}, u32[]{:S(2)}, u32[]{:S(2)}) %collective-permute-start.5) | collective-permute-done | bytes 8224 | tf_op jit(solution)/shard_map/ppermute | solution.py:611
  33.2 3.4 %collective-permute-start.6 = (f32[1,2048]{1,0:T(1,128)S(1)}, f32[1,2048]{1,0:T(1,128)S(1)}, u32[]{:S(2)}, u32[]{:S(2)}) collective-permute-start(f32[1,2048]{1,0:T(1,128)S(1)} %collective-permute-done.5), channel_id=1, source_target_pairs={{0,4},{4,8},{8,12},{12,16},{16,20},{20,24},{24,28},{28,0},{1,5},{5... | collective-permute-start | bytes 24584 | tf_op jit(solution)/shard_map/ppermute | solution.py:611
  36.6 0.0 collective-permute-done.3
  36.6 4.9 %collective-permute-done.6.refs_17_.refs_1_.refs_9_ = f32[1,2048]{1,0:T(1,128)S(1)} collective-permute-done((f32[1,2048]{1,0:T(1,128)S(1)}, f32[1,2048]{1,0:T(1,128)S(1)}, u32[]{:S(2)}, u32[]{:S(2)}) %collective-permute-start.6) | collective-permute-done | bytes 8224 | tf_op jit(solution)/shard_map/ppermute | solution.py:611
  41.5 2.9 %collective-permute-done.4.refs_15_ = f32[400,2048]{1,0:T(8,128)S(1)} collective-permute-done((f32[400,2048]{1,0:T(8,128)}, f32[400,2048]{1,0:T(8,128)S(1)}, u32[]{:S(2)}, u32[]{:S(2)}) %collective-permute-start.4) | collective-permute-done | bytes 3276832 | tf_op jit(solution)/shard_map/ppermute | solution.py:602
  44.4 10.9 %first_far.1 = (f32[400,2048]{1,0:T(8,128)S(1)}, f32[1,2048]{1,0:T(1,128)S(1)}, f32[32,400]{1,0:T(8,128)S(1)}, f32[408,1024]{1,0:T(8,128)S(1)}, f32[400,1024]{1,0:T(8,128)S(1)}, /*index=5*/f32[1,2048]{1,0:T(1,128)}) custom-call(f32[400,2048]{1,0:T(8,128)S(1)} %bitcast.11, f32[1,2048]{1,0:T(1,128)S(1)} %get-tuple-element.75.refs_1_, ...), custom_call_target="tpu_custom_call", output_to_operand_aliasing={{0}: (16, {})} | custom-call | flops 1000000 | bytes 100000 | tf_op jit(solution)/shard_map/first_far/pallas_call | solution.py:328
  55.3 1.4 %collective-permute-start.10 = (f32[408,1024]{1,0:T(8,128)S(1)}, f32[408,1024]{1,0:T(8,128)S(1)}, u32[]{:S(2)}, u32[]{:S(2)}) collective-permute-start(f32[408,1024]{1,0:T(8,128)S(1)} %get-tuple-element.96), channel_id=1, source_target_pairs={{0,2},{4,6},{8,10},{12,14},{16,18},{20,22},{24,26},{28,30},{1,3},{... | collective-permute-start | bytes 5013512 | tf_op jit(solution)/shard_map/ppermute | solution.py:615
  56.7 1.4 %collective-permute-start.11 = (f32[400,1024]{1,0:T(8,128)S(1)}, f32[400,1024]{1,0:T(8,128)S(1)}, u32[]{:S(2)}, u32[]{:S(2)}) collective-permute-start(f32[400,1024]{1,0:T(8,128)S(1)} %get-tuple-element.97), channel_id=1, source_target_pairs={{0,2},{4,6},{8,10},{12,14},{16,18},{20,22},{24,26},{28,30},{1,3},{... | collective-permute-start | bytes 4915208 | tf_op jit(solution)/shard_map/ppermute | solution.py:615
  58.1 1.3 %collective-permute-start.8 = (f32[400,512]{1,0:T(8,128)S(1)}, f32[400,512]{1,0:T(8,128)S(1)}, u32[]{:S(2)}, u32[]{:S(2)}) collective-permute-start(f32[400,512]{1,0:T(8,128)S(1)} %get-tuple-element.92), channel_id=1, source_target_pairs={{2,4},{6,8},{10,12},{14,16},{18,20},{22,24},{26,28},{30,0},{3,5},{... | collective-permute-start | bytes 2457608 | tf_op jit(solution)/shard_map/ppermute | solution.py:610
  59.4 1.3 %collective-permute-start.7 = (f32[400,256]{1,0:T(8,128)S(1)}, f32[400,256]{1,0:T(8,128)S(1)}, u32[]{:S(2)}, u32[]{:S(2)}) collective-permute-start(f32[400,256]{1,0:T(8,128)S(1)} %get-tuple-element.81), channel_id=1, source_target_pairs={{2,4},{6,8},{10,12},{14,16},{18,20},{22,24},{26,28},{30,0},{3,5},{... | collective-permute-start | bytes 1228808 | tf_op jit(solution)/shard_map/ppermute | solution.py:610
  60.7 3.7 %prepare1.1 = (f32[400,256]{1,0:T(8,128)S(1)}, f32[400,256]{1,0:T(8,128)S(1)}, bf16[400,256]{1,0:T(8,128)(2,1)S(1)}, bf16[256,400]{1,0:T(8,128)(2,1)S(1)}, bf16[...) custom-call(f32[400,2048]{1,0:T(8,128)S(1)} %get-tuple-element.79.le, ...), custom_call_target="tpu_custom_call" | custom-call | flops 1000000 | bytes 100000 | tf_op jit(solution)/shard_map/prepare1/pallas_call | solution.py:328
  64.5 0.0 collective-permute-done.11.refs_16_
  64.5 0.0 collective-permute-done.10.refs_15_
  64.5 1.0 %last_near.1 = (f32[400,2048]{1,0:T(8,128)}, f32[1,2048]{1,0:T(1,128)S(1)}, f32[32,400]{1,0:T(8,128)S(1)}, f32[400,2048]{1,0:T(8,128)}, f32[1,2048]{1,0:T(1,128)}) custom-call(f32[400,2048]{1,0:T(8,128)S(1)} %get-tuple-element.79.left.refs_0_, f32[1,2048]{1,0:T(1,128)S(1)} %get-tuple-element.80.refs_1_, f32[1,2048]{1,0:T(1,128)S(1)} %bitcast.13, ...), custom_call_target="tpu_custom_call" | custom-call | flops 1000000 | bytes 100000 | tf_op jit(solution)/shard_map/last_near/pallas_call | solution.py:328
  65.5 0.9 collective-permute-done.9.refs_0_
  66.4 2.5 %last_piece0.1 = (f32[400,256]{1,0:T(8,128)S(1)}, f32[400,256]{1,0:T(8,128)S(1)}, f32[400,1280]{1,0:T(8,128)S(1)}) custom-call(f32[400,1280]{1,0:T(8,128)S(1)} %collective-permute-done.9.refs_0_, bf16[400,256]{1,0:T(8,128)(2,1)S(1)} %get-tuple-element.84.refs_6_.refs_1_.refs_3_, bf16[256,400]{1,0:T(8,128)(2,1)S(1)} %get-tuple-element.85.refs_7_.refs_2_.refs_4_, ...), custom_call_target="tpu_custom_call" | custom-call | flops 1000000 | bytes 100000 | tf_op jit(solution)/shard_map/last_piece0/pallas_call | solution.py:328
  68.9 2.1 %early_edges0.1 = (bf16[800,256]{1,0:T(8,128)(2,1)S(1)}, f32[256,400]{1,0:T(8,128)}) custom-call(f32[400,256]{1,0:T(8,128)S(1)} %get-tuple-element.82.refs_4_.refs_0_.refs_1_, f32[400,256]{1,0:T(8,128)S(1)} %get-tuple-element.83.refs_5_.refs_1_.refs_2_, f32[400,256]{1,0:T(8,128)S(1)} %get-tuple-element.99.refs_2_.refs_5_, ...), custom_call_target="tpu_custom_call" | custom-call | flops 1000000 | bytes 100000 | tf_op jit(solution)/shard_map/early_edges0/pallas_call | solution.py:328
  71.0 1.9 %early_right0.1 = (f32[400,2048]{1,0:T(8,128)}, f32[1,2048]{1,0:T(1,128)S(1)}) custom-call(f32[400,1280]{1,0:T(8,128)S(1)} %collective-permute-done.9.refs_0_, f32[1,2048]{1,0:T(1,128)S(1)} %collective-permute-done.6.refs_17_.refs_1_.refs_9_, f32[400,1280]{1,0:T(8,128)S(1)} %get-tuple-element.101.refs_2_, ...), custom_call_target="tpu_custom_call", output_to_operand_aliasing={{1}: (5, {}), {0}: (6, {})} | custom-call | flops 1000000 | bytes 100000 | tf_op jit(solution)/shard_map/early_right0/pallas_call | solution.py:328
  72.9 2.3 %collective-permute-done.8.refs_0_ = f32[400,512]{1,0:T(8,128)S(1)} collective-permute-done((f32[400,512]{1,0:T(8,128)S(1)}, f32[400,512]{1,0:T(8,128)S(1)}, u32[]{:S(2)}, u32[]{:S(2)}) %collective-permute-start.8) | collective-permute-done | bytes 819232 | tf_op jit(solution)/shard_map/ppermute | solution.py:610
  75.1 1.2 %last_piece1.1 = (f32[400,256]{1,0:T(8,128)S(1)}, f32[400,256]{1,0:T(8,128)S(1)}, f32[400,512]{1,0:T(8,128)S(1)}) custom-call(f32[400,512]{1,0:T(8,128)S(1)} %collective-permute-done.8.refs_0_, bf16[400,256]{1,0:T(8,128)(2,1)S(1)} %get-tuple-element.84.refs_6_.refs_1_.refs_3_, ...), custom_call_target="tpu_custom_call", output_to_operand_aliasing={{0}: (5, {}), {1}: (6, {})} | custom-call | flops 1000000 | bytes 100000 | tf_op jit(solution)/shard_map/last_piece1/pallas_call | solution.py:328
  76.4 1.3 %early_edges1.1 = (bf16[800,256]{1,0:T(8,128)(2,1)S(1)}, f32[256,400]{1,0:T(8,128)S(1)}) custom-call(f32[400,256]{1,0:T(8,128)S(1)} %get-tuple-element.82.refs_4_.refs_0_.refs_1_, f32[400,256]{1,0:T(8,128)S(1)} %get-tuple-element.83.refs_5_.refs_1_.refs_2_, f32[400,256]{1,0:T(8,128)S(1)} %get-tuple-element.105.refs_2_, ...), custom_call_target="tpu_custom_call" | custom-call | flops 1000000 | bytes 100000 | tf_op jit(solution)/shard_map/early_edges1/pallas_call | solution.py:328
  77.7 1.5 %early_right1.1 = (f32[400,2048]{1,0:T(8,128)}, f32[1,2048]{1,0:T(1,128)S(1)}) custom-call(f32[400,512]{1,0:T(8,128)S(1)} %collective-permute-done.8.refs_0_, f32[1,2048]{1,0:T(1,128)S(1)} %collective-permute-done.6.refs_17_.refs_1_.refs_9_, f32[400,512]{1,0:T(8,128)S(1)} %get-tuple-element.109.refs_2_, ...), custom_call_target="tpu_custom_call", output_to_operand_aliasing={{1}: (5, {}), {0}: (6, {})} | custom-call | flops 1000000 | bytes 100000 | tf_op jit(solution)/shard_map/early_right1/pallas_call | solution.py:328
  79.2 0.3 collective-permute-done.7.refs_0_.refs_8_
  79.5 2.3 %late_edges.1 = (f32[400,256]{1,0:T(8,128)S(1)}, bf16[800,256]{1,0:T(8,128)(2,1)S(1)}, bf16[800,256]{1,0:T(8,128)(2,1)S(1)}, f32[32,400]{1,0:T(8,128)S(1)}, bf16...) custom-call(f32[400,256]{1,0:T(8,128)S(1)} %collective-permute-done.7.refs_0_.refs_8_, ...), custom_call_target="tpu_custom_call", output_to_operand_aliasing={{3}: (14, {})} | custom-call | flops 1000000 | bytes 100000 | tf_op jit(solution)/shard_map/late_edges/pallas_call | solution.py:328
  81.8 0.9 %ahead_left.1 = (f32[400,768]{1,0:T(8,128)S(1)}, f32[32,400]{1,0:T(8,128)S(1)}) custom-call(f32[400,2048]{1,0:T(8,128)S(1)} %get-tuple-element.79.left.refs_0_, f32[1,2048]{1,0:T(1,128)S(1)} %get-tuple-element.80.refs_1_, bf16[800,256]{1,0:T(8,128)(2,1)S(1)} %get-tuple-element.113.refs_2_, ...), custom_call_target="tpu_custom_call", output_to_operand_aliasing={{1}: (7, {})} | custom-call | flops 1000000 | bytes 100000 | tf_op jit(solution)/shard_map/ahead_left/pallas_call | solution.py:328
  82.7 1.8 %collective-permute-start.12 = (f32[32,400]{1,0:T(8,128)S(1)}, f32[32,400]{1,0:T(8,128)S(1)}, u32[]{:S(2)}, u32[]{:S(2)}) collective-permute-start(f32[32,400]{1,0:T(8,128)S(1)} %get-tuple-element.124.rest_0_), channel_id=1, source_target_pairs={{0,1},{1,0},{2,3},{3,2},{4,5},{5,4},{6,7},{7,6},{8,9},{9,8},{10,11... | collective-permute-start | bytes 153608 | tf_op jit(solution)/shard_map/ppermute | solution.py:632
  84.5 0.0 copy-start.8
  84.5 2.8 %late_slabs.1 = (f32[400,2048]{1,0:T(8,128)}, f32[400,2048]{1,0:T(8,128)}) custom-call(f32[400,2048]{1,0:T(8,128)S(1)} %get-tuple-element.79.left.refs_0_, f32[1,2048]{1,0:T(1,128)S(1)} %get-tuple-element.80.refs_1_, bf16[800,256]{1,0:T(8,128)(2,1)S(1)} %get-tuple-element.113.refs_2_, ...), custom_call_target="tpu_custom_call", output_to_operand_aliasing={{0}: (13, {}), {1}: (14, {})} | custom-call | flops 1000000 | bytes 100000 | tf_op jit(solution)/shard_map/late_slabs/pallas_call | solution.py:328
  87.3 0.0 collective-permute-done.12.rest_1_
  87.4 0.0 copy-done.8
  87.4 0.7 relation_update.1
  (1 shorter events, 0.0 us)
Async XLA Ops:
  0.6 11.1 %copy-start.9 = (f32[2048]{0:T(1024)S(1)}, f32[2048]{0:T(1024)}, u32[]{:S(2)}) copy-start(f32[2048]{0:T(1024)} %param.14) | copy-start | bytes 24580
  0.6 11.2 %copy-start = (f32[2048,400]{0,1:T(8,128)S(1)}, f32[2048,400]{0,1:T(8,128)}, u32[]{:S(2)}) copy-start(f32[2048,400]{0,1:T(8,128)} %param.11) | copy-start | bytes 9830404
  0.7 11.2 %copy-start.1 = (f32[32,400]{1,0:T(8,128)S(1)}, f32[32,400]{1,0:T(8,128)}, u32[]{:S(2)}) copy-start(f32[32,400]{1,0:T(8,128)} %relations.5) | copy-start | bytes 153604
  0.7 11.2 %copy-start.2 = (s32[2,256]{1,0:T(2,128)S(1)}, s32[2,256]{1,0:T(2,128)}, u32[]{:S(2)}) copy-start(s32[2,256]{1,0:T(2,128)} %refs_10_.1) | copy-start | bytes 6148
  0.7 11.2 %copy-start.3 = (s32[2,1000]{1,0:T(2,128)S(1)}, s32[2,1000]{1,0:T(2,128)}, u32[]{:S(2)}) copy-start(s32[2,1000]{1,0:T(2,128)} %nsrc.3) | copy-start | bytes 24004
  0.7 11.2 %copy-start.4 = (s32[2,1000]{1,0:T(2,128)S(1)}, s32[2,1000]{1,0:T(2,128)}, u32[]{:S(2)}) copy-start(s32[2,1000]{1,0:T(2,128)} %ndst.3) | copy-start | bytes 24004
  0.7 11.2 %copy-start.6 = (s32[2,256]{1,0:T(2,128)S(1)}, s32[2,256]{1,0:T(2,128)}, u32[]{:S(2)}) copy-start(s32[2,256]{1,0:T(2,128)} %src.3) | copy-start | bytes 6148
  0.7 11.2 %copy-start.7 = (s32[2,256]{1,0:T(2,128)S(1)}, s32[2,256]{1,0:T(2,128)}, u32[]{:S(2)}) copy-start(s32[2,256]{1,0:T(2,128)} %rid.3) | copy-start | bytes 6148
  0.7 43.7 %collective-permute-start.4 = (f32[400,2048]{1,0:T(8,128)}, f32[400,2048]{1,0:T(8,128)S(1)}, u32[]{:S(2)}, u32[]{:S(2)}) collective-permute-start(f32[400,2048]{1,0:T(8,128)} %bitcast.18), channel_id=1, source_target_pairs={{2,4},{6,8},{10,12},{14,16},{18,20},{22,24},{26,28},{30,0},{3,5},{... | collective-permute-start | bytes 9830408 | tf_op jit(solution)/shard_map/ppermute | solution.py:602
  4.4 11.3 %copy-start.5 = (f32[2048]{0:T(1024)S(1)}, f32[2048]{0:T(1024)}, u32[]{:S(2)}) copy-start(f32[2048]{0:T(1024)} %param.12) | copy-start | bytes 24580
  4.4 11.3 %collective-permute-start.2 = (f32[400,1024]{1,0:T(8,128)S(1)}, f32[400,1024]{1,0:T(8,128)S(1)}, u32[]{:S(2)}, u32[]{:S(2)}) collective-permute-start(f32[400,1024]{1,0:T(8,128)S(1)} %get-tuple-element.125), channel_id=1, source_target_pairs={{0,2},{4,6},{8,10},{12,14},{16,18},{20,22},{24,26},{28,30},{1,3},{... | collective-permute-start | bytes 4915208 | tf_op jit(solution)/shard_map/ppermute | solution.py:603
  10.3 5.4 %collective-permute-start.1 = (f32[400,1024]{1,0:T(8,128)S(1)}, f32[400,1024]{1,0:T(8,128)S(1)}, u32[]{:S(2)}, u32[]{:S(2)}) collective-permute-start(f32[400,1024]{1,0:T(8,128)S(1)} %get-tuple-element.126), channel_id=1, source_target_pairs={{0,2},{4,6},{8,10},{12,14},{16,18},{20,22},{24,26},{28,30},{1,3},{... | collective-permute-start | bytes 4915208 | tf_op jit(solution)/shard_map/ppermute | solution.py:603
  11.8 4.0 %collective-permute-start = (f32[2048]{0:T(1024)S(1)}, f32[2048]{0:T(1024)S(1)}, u32[]{:S(2)}, u32[]{:S(2)}) collective-permute-start(f32[2048]{0:T(1024)S(1)} %copy-done.9), channel_id=1, source_target_pairs={{0,2},{4,6},{8,10},{12,14},{16,18},{20,22},{24,26},{28,30},{2,0},{... | collective-permute-start | bytes 24584 | tf_op jit(solution)/shard_map/ppermute | solution.py:604
  15.9 50.4 %collective-permute-start.9 = (f32[400,1280]{1,0:T(8,128)S(1)}, f32[400,1280]{1,0:T(8,128)S(1)}, u32[]{:S(2)}, u32[]{:S(2)}) collective-permute-start(f32[400,1280]{1,0:T(8,128)S(1)} %get-tuple-element.93), channel_id=1, source_target_pairs={{2,4},{6,8},{10,12},{14,16},{18,20},{22,24},{26,28},{30,0},{3,5},{... | collective-permute-start | bytes 6144008 | tf_op jit(solution)/shard_map/ppermute | solution.py:610
  17.2 15.9 %collective-permute-start.5 = (f32[1,2048]{1,0:T(1,128)S(1)}, f32[1,2048]{1,0:T(1,128)S(1)}, u32[]{:S(2)}, u32[]{:S(2)}) collective-permute-start(f32[1,2048]{1,0:T(1,128)S(1)} %get-tuple-element.78), channel_id=1, source_target_pairs={{2,0},{6,4},{10,8},{14,12},{18,16},{22,20},{26,24},{30,28},{3,1},{... | collective-permute-start | bytes 24584 | tf_op jit(solution)/shard_map/ppermute | solution.py:611
  18.5 18.1 %collective-permute-start.3 = (f32[2048]{0:T(1024)S(1)}, f32[2048]{0:T(1024)S(1)}, u32[]{:S(2)}, u32[]{:S(2)}) collective-permute-start(f32[2048]{0:T(1024)S(1)} %collective-permute-done), channel_id=1, source_target_pairs={{0,4},{4,8},{8,12},{12,16},{16,20},{20,24},{24,28},{28,0},{1,5},{5... | collective-permute-start | bytes 24584 | tf_op jit(solution)/shard_map/ppermute | solution.py:605
  33.2 8.4 %collective-permute-start.6 = (f32[1,2048]{1,0:T(1,128)S(1)}, f32[1,2048]{1,0:T(1,128)S(1)}, u32[]{:S(2)}, u32[]{:S(2)}) collective-permute-start(f32[1,2048]{1,0:T(1,128)S(1)} %collective-permute-done.5), channel_id=1, source_target_pairs={{0,4},{4,8},{8,12},{12,16},{16,20},{20,24},{24,28},{28,0},{1,5},{5... | collective-permute-start | bytes 24584 | tf_op jit(solution)/shard_map/ppermute | solution.py:611
  55.3 9.2 %collective-permute-start.10 = (f32[408,1024]{1,0:T(8,128)S(1)}, f32[408,1024]{1,0:T(8,128)S(1)}, u32[]{:S(2)}, u32[]{:S(2)}) collective-permute-start(f32[408,1024]{1,0:T(8,128)S(1)} %get-tuple-element.96), channel_id=1, source_target_pairs={{0,2},{4,6},{8,10},{12,14},{16,18},{20,22},{24,26},{28,30},{1,3},{... | collective-permute-start | bytes 5013512 | tf_op jit(solution)/shard_map/ppermute | solution.py:615
  56.7 7.7 %collective-permute-start.11 = (f32[400,1024]{1,0:T(8,128)S(1)}, f32[400,1024]{1,0:T(8,128)S(1)}, u32[]{:S(2)}, u32[]{:S(2)}) collective-permute-start(f32[400,1024]{1,0:T(8,128)S(1)} %get-tuple-element.97), channel_id=1, source_target_pairs={{0,2},{4,6},{8,10},{12,14},{16,18},{20,22},{24,26},{28,30},{1,3},{... | collective-permute-start | bytes 4915208 | tf_op jit(solution)/shard_map/ppermute | solution.py:615
  58.1 17.0 %collective-permute-start.8 = (f32[400,512]{1,0:T(8,128)S(1)}, f32[400,512]{1,0:T(8,128)S(1)}, u32[]{:S(2)}, u32[]{:S(2)}) collective-permute-start(f32[400,512]{1,0:T(8,128)S(1)} %get-tuple-element.92), channel_id=1, source_target_pairs={{2,4},{6,8},{10,12},{14,16},{18,20},{22,24},{26,28},{30,0},{3,5},{... | collective-permute-start | bytes 2457608 | tf_op jit(solution)/shard_map/ppermute | solution.py:610
  59.4 20.1 %collective-permute-start.7 = (f32[400,256]{1,0:T(8,128)S(1)}, f32[400,256]{1,0:T(8,128)S(1)}, u32[]{:S(2)}, u32[]{:S(2)}) collective-permute-start(f32[400,256]{1,0:T(8,128)S(1)} %get-tuple-element.81), channel_id=1, source_target_pairs={{2,4},{6,8},{10,12},{14,16},{18,20},{22,24},{26,28},{30,0},{3,5},{... | collective-permute-start | bytes 1228808 | tf_op jit(solution)/shard_map/ppermute | solution.py:610
  82.7 4.6 %collective-permute-start.12 = (f32[32,400]{1,0:T(8,128)S(1)}, f32[32,400]{1,0:T(8,128)S(1)}, u32[]{:S(2)}, u32[]{:S(2)}) collective-permute-start(f32[32,400]{1,0:T(8,128)S(1)} %get-tuple-element.124.rest_0_), channel_id=1, source_target_pairs={{0,1},{1,0},{2,3},{3,2},{4,5},{5,4},{6,7},{7,6},{8,9},{9,8},{10,11... | collective-permute-start | bytes 153608 | tf_op jit(solution)/shard_map/ppermute | solution.py:632
  84.5 2.8 %copy-start.8 = (f32[32]{0:T(128)S(1)}, f32[32]{0:T(128)}, u32[]{:S(2)}) copy-start(f32[32]{0:T(128)} %param.16) | copy-start | bytes 388

commit v6 on v3

--- a/solution.py
+++ b/solution.py
@@ -145,7 +145,7 @@
         target[...] = jnp.zeros_like(target)
         gq[...] = jnp.zeros_like(gq)
 
-    size = step_of(piece.shape[1], 256 if fixed else 512)
+    size = step_of(piece.shape[1], 256)
 
     def part(i):
         cut = lanes_at(i, size)
@@ -160,14 +160,14 @@
 
 
 def join(number, weight, source, target, gq, left16, count_l, kind, rel_in,
-         probe, probe_rows, gp, lgrad, to_src, to_dst, rel_out, fixed=False):
+         probe, probe_rows, gp, lgrad, to_src, to_dst, rel_out, fixed=False, most=512):
     rows = left16.shape[1]
     product = weight[...] * target[...]
     probe[...] = product.astype(BF16)
     probe_rows[...] = half_rows(product.astype(BF16).astype(F32))
     gp[...] = jnp.zeros_like(gp)
 
-    size = step_of(rows)
+    size = step_of(rows, most)
 
     def part(i):
         cut = lanes_at(i, size)
@@ -286,7 +286,7 @@
             take_piece(number, at, piece, query, query_rows, oh_dst, count_r, target, gq, grads[-1], fixed)
             at += piece.shape[1]
         join(number, weight, source, target, gq, left16, count_l, kind, rel_in,
-             probe, probe_rows, gp, lgrad, to_src, to_dst, rel_out, fixed)
+             probe, probe_rows, gp, lgrad, to_src, to_dst, rel_out, fixed, 1024 if last else 512)
         if last:
             unpack_state(right[STATE], depth, rstate)
             wait_right = update_and_send(right, rstate, grads, to_dst, oh_dst, spare, right_out[0], sems.at[0], fixed)
@@ -298,12 +298,12 @@
                 for old, begin, length in rows_of(right, at, size):
                     cut = slice(begin, begin + length)
                     here = slice(begin - at, begin - at + length)
-                    adagrad(old, rstate_in.at[:, cut], rgrad.at[:, cut], to_dst, oh_dst, begin, out.at[:, here], spare.at[:, cut])
+                    adagrad(old, rstate_in.at[:, cut], rgrad.at[:, cut], to_dst, oh_dst, begin, out.at[:, here], spare.at[:, cut], None, fixed)
             if packs:
                 pack_state(spare, right_out[STATE], depth)
             else:
                 state_out[...] = spare[...]
-            adagrad(left, lstate, lgrad, to_src, oh_src, 0, left_out, lstate_out)
+            adagrad(left, lstate, lgrad, to_src, oh_src, 0, left_out, lstate_out, None, fixed)
 
 
 def shape(*dims, dtype=F32):
@@ -470,7 +470,9 @@
         p = gp[...]
         coef = -jax.nn.sigmoid(-jnp.sum(s * w * t, axis=0, keepdims=True))
         g_weight = coef * s * t + q * s + p * t
-        rel_out[...] = rel_in[...] + sum(mul(kind[...], part, NT) for part in split(g_weight, 2))
+        rel_out[...] = rel_in[...] + mul(
+            jnp.concatenate([kind[...]] * 2, axis=1), jnp.concatenate(split(g_weight, 2), axis=1), NT
+        )
         to_src[0:depth, :], to_src[depth:, :] = split(coef * w * t + q * w, 2)
         here = dst[step : step + 1, :] >= at
         to_dst[0:depth, :], to_dst[depth:, :] = split(jnp.where(here, coef * w * s + p * w, 0.0), 2)

time: 88.1 us -> 88.1 us (level)
  waiting for transfers between devices: 22.5 us -> 24.3 us
  Pallas kernels: 36.4 us -> 34.7 us
    pallas_call x15, Pallas kernels: 36.4 us -> 34.7 us  [call(): pl.pallas_call(kernel, out_shape=tuple(shapes), in_specs=[large if i in i...]
    ppermute x3, waiting for transfers between devices: 3.42 us -> 5.13 us  [local(): far = [lax.ppermute(piece, 'blk', across) for piece in far]]
  transfers between devices with their start and end apart: 13 -> 13, of which waited for: 7 -> 8; matrix products, arithmetic and copies ran while one was open for 2% -> 2% of each run, Pallas kernels for 37% -> 35%
where the time goes in v6:
time: 88.1 us; the launch traced here: 87.7 us
  Pallas kernels  34.7 us (39%)
  starting transfers between devices  25.6 us (29%)
  waiting for transfers between devices  24.3 us (28%)
  local copies, waits for them, and re-layouts  2.21 us (3%)
  between operations  0.99 us (1%)
    pallas_call x15, Pallas kernels, call(): pl.pallas_call(kernel, out_shape=tuple(shapes), in_specs=[large if i in i...  34.7 us
    ppermute x2, waiting for transfers between devices, local(): state = lax.ppermute(lax.ppermute(state, 'blk', back), 'blk', skip)  15.4 us
    ppermute x2, starting transfers between devices, local(): lax.ppermute(right[:, at:at + size], 'blk', inside)  7.28 us
    ppermute x3, waiting for transfers between devices, local(): far = [lax.ppermute(piece, 'blk', across) for piece in far]  5.13 us
    ppermute x2, starting transfers between devices, local(): state = lax.ppermute(lax.ppermute(state, 'blk', back), 'blk', skip)  4.74 us
    ppermute x3, starting transfers between devices, local(): far = [lax.ppermute(piece, 'blk', across) for piece in far]  3.88 us
    ppermute x1, waiting for transfers between devices, local(): right_far = lax.ppermute(right, 'blk', across)  3.54 us
    ppermute x1, starting transfers between devices, local(): state_far = lax.ppermute(state_near, 'blk', skip).reshape(1, rows)  3.46 us
  transfers between devices with their start and end apart: 13, of which 8 were waited for; matrix products, arithmetic and copies ran while one was open for 2% of the time, Pallas kernels for 35%

profile of v6, /device:TPU:0, one launch (start us, length us, event | category | flops | bytes accessed | tf_op | source)
XLA Modules:
  0.0 87.7 jit_solution(8183287386462729372)
XLA Ops:
  0.6 0.0 copy-start.9
  0.6 0.0 copy-start
  0.7 0.0 copy-start.1
  0.7 0.0 copy-start.2
  0.7 0.0 copy-start.3
  0.7 0.0 copy-start.4
  0.7 0.0 copy-start.6
  0.7 0.0 copy-start.7
  0.7 1.6 %collective-permute-start.4 = (f32[400,2048]{1,0:T(8,128)}, f32[400,2048]{1,0:T(8,128)S(1)}, u32[]{:S(2)}, u32[]{:S(2)}) collective-permute-start(f32[400,2048]{1,0:T(8,128)} %bitcast.18), channel_id=1, source_target_pairs={{2,4},{6,8},{10,12},{14,16},{18,20},{22,24},{26,28},{30,0},{3,5},{... | collective-permute-start | bytes 9830408 | tf_op jit(solution)/shard_map/ppermute | solution.py:613
  2.3 2.2 %fusion = (f32[400,1024]{1,0:T(8,128)S(1)}, f32[400,1024]{1,0:T(8,128)S(1)}) fusion(f32[400,2048]{1,0:T(8,128)} %bitcast.19), kind=kLoop, calls=%fused_computation | loop fusion | bytes 6553600 | tf_op jit(solution)/shard_map/slice | solution.py:614
  4.4 0.0 copy-start.5
  4.4 5.9 %collective-permute-start.2 = (f32[400,1024]{1,0:T(8,128)S(1)}, f32[400,1024]{1,0:T(8,128)S(1)}, u32[]{:S(2)}, u32[]{:S(2)}) collective-permute-start(f32[400,1024]{1,0:T(8,128)S(1)} %get-tuple-element.125), channel_id=1, source_target_pairs={{0,2},{4,6},{8,10},{12,14},{16,18},{20,22},{24,26},{28,30},{1,3},{... | collective-permute-start | bytes 4915208 | tf_op jit(solution)/shard_map/ppermute | solution.py:614
  10.3 1.4 %collective-permute-start.1 = (f32[400,1024]{1,0:T(8,128)S(1)}, f32[400,1024]{1,0:T(8,128)S(1)}, u32[]{:S(2)}, u32[]{:S(2)}) collective-permute-start(f32[400,1024]{1,0:T(8,128)S(1)} %get-tuple-element.126), channel_id=1, source_target_pairs={{0,2},{4,6},{8,10},{12,14},{16,18},{20,22},{24,26},{28,30},{1,3},{... | collective-permute-start | bytes 4915208 | tf_op jit(solution)/shard_map/ppermute | solution.py:614
  11.7 0.0 copy-done.9
  11.8 0.1 collective-permute-start
  11.8 0.0 copy-done
  11.8 0.0 copy-done.1
  11.9 0.0 copy-done.2
  11.9 0.0 copy-done.3
  11.9 0.0 copy-done.4
  11.9 0.0 copy-done.6
  11.9 0.0 copy-done.7
  11.9 3.7 %prepare0.1 = (f32[400,256]{1,0:T(8,128)S(1)}, f32[400,256]{1,0:T(8,128)S(1)}, bf16[400,256]{1,0:T(8,128)(2,1)S(1)}, bf16[256,400]{1,0:T(8,128)(2,1)S(1)}, bf16[...) custom-call(f32[400,2048]{1,0:T(8,128)S(1)} %bitcast.9, ...), custom_call_target="tpu_custom_call" | custom-call | flops 1000000 | bytes 100000 | tf_op jit(solution)/shard_map/prepare0/pallas_call | solution.py:328
  15.6 0.1 collective-permute-done
  15.7 0.0 collective-permute-done.2.refs_16_
  15.7 0.0 collective-permute-done.1.refs_15_
  15.7 0.0 copy-done.5
  15.7 0.2 first_near.1
  15.9 1.3 %collective-permute-start.9 = (f32[400,1280]{1,0:T(8,128)S(1)}, f32[400,1280]{1,0:T(8,128)S(1)}, u32[]{:S(2)}, u32[]{:S(2)}) collective-permute-start(f32[400,1280]{1,0:T(8,128)S(1)} %get-tuple-element.93), channel_id=1, source_target_pairs={{2,4},{6,8},{10,12},{14,16},{18,20},{22,24},{26,28},{30,0},{3,5},{... | collective-permute-start | bytes 6144008 | tf_op jit(solution)/shard_map/ppermute | solution.py:621
  17.2 1.3 %collective-permute-start.5 = (f32[1,2048]{1,0:T(1,128)S(1)}, f32[1,2048]{1,0:T(1,128)S(1)}, u32[]{:S(2)}, u32[]{:S(2)}) collective-permute-start(f32[1,2048]{1,0:T(1,128)S(1)} %get-tuple-element.78), channel_id=1, source_target_pairs={{2,0},{6,4},{10,8},{14,12},{18,16},{22,20},{26,24},{30,28},{3,1},{... | collective-permute-start | bytes 24584 | tf_op jit(solution)/shard_map/ppermute | solution.py:622
  18.5 3.5 %collective-permute-start.3 = (f32[2048]{0:T(1024)S(1)}, f32[2048]{0:T(1024)S(1)}, u32[]{:S(2)}, u32[]{:S(2)}) collective-permute-start(f32[2048]{0:T(1024)S(1)} %collective-permute-done), channel_id=1, source_target_pairs={{0,4},{4,8},{8,12},{12,16},{16,20},{20,24},{24,28},{28,0},{1,5},{5... | collective-permute-start | bytes 24584 | tf_op jit(solution)/shard_map/ppermute | solution.py:616
  22.0 10.5 %collective-permute-done.5 = f32[1,2048]{1,0:T(1,128)S(1)} collective-permute-done((f32[1,2048]{1,0:T(1,128)S(1)}, f32[1,2048]{1,0:T(1,128)S(1)}, u32[]{:S(2)}, u32[]{:S(2)}) %collective-permute-start.5) | collective-permute-done | bytes 8224 | tf_op jit(solution)/shard_map/ppermute | solution.py:622
  32.5 3.4 %collective-permute-start.6 = (f32[1,2048]{1,0:T(1,128)S(1)}, f32[1,2048]{1,0:T(1,128)S(1)}, u32[]{:S(2)}, u32[]{:S(2)}) collective-permute-start(f32[1,2048]{1,0:T(1,128)S(1)} %collective-permute-done.5), channel_id=1, source_target_pairs={{0,4},{4,8},{8,12},{12,16},{16,20},{20,24},{24,28},{28,0},{1,5},{5... | collective-permute-start | bytes 24584 | tf_op jit(solution)/shard_map/ppermute | solution.py:622
  35.9 0.0 collective-permute-done.3
  36.0 4.9 %collective-permute-done.6.refs_17_.refs_1_.refs_9_ = f32[1,2048]{1,0:T(1,128)S(1)} collective-permute-done((f32[1,2048]{1,0:T(1,128)S(1)}, f32[1,2048]{1,0:T(1,128)S(1)}, u32[]{:S(2)}, u32[]{:S(2)}) %collective-permute-start.6) | collective-permute-done | bytes 8224 | tf_op jit(solution)/shard_map/ppermute | solution.py:622
  40.9 3.5 %collective-permute-done.4.refs_15_ = f32[400,2048]{1,0:T(8,128)S(1)} collective-permute-done((f32[400,2048]{1,0:T(8,128)}, f32[400,2048]{1,0:T(8,128)S(1)}, u32[]{:S(2)}, u32[]{:S(2)}) %collective-permute-start.4) | collective-permute-done | bytes 3276832 | tf_op jit(solution)/shard_map/ppermute | solution.py:613
  44.4 9.2 %first_far.1 = (f32[400,2048]{1,0:T(8,128)S(1)}, f32[1,2048]{1,0:T(1,128)S(1)}, f32[32,400]{1,0:T(8,128)S(1)}, f32[408,1024]{1,0:T(8,128)S(1)}, f32[400,1024]{1,0:T(8,128)S(1)}, /*index=5*/f32[1,2048]{1,0:T(1,128)}) custom-call(f32[400,2048]{1,0:T(8,128)S(1)} %bitcast.11, f32[1,2048]{1,0:T(1,128)S(1)} %get-tuple-element.75.refs_1_, ...), custom_call_target="tpu_custom_call", output_to_operand_aliasing={{0}: (16, {})} | custom-call | flops 1000000 | bytes 100000 | tf_op jit(solution)/shard_map/first_far/pallas_call | solution.py:328
  53.6 1.4 %collective-permute-start.10 = (f32[408,1024]{1,0:T(8,128)S(1)}, f32[408,1024]{1,0:T(8,128)S(1)}, u32[]{:S(2)}, u32[]{:S(2)}) collective-permute-start(f32[408,1024]{1,0:T(8,128)S(1)} %get-tuple-element.96), channel_id=1, source_target_pairs={{0,2},{4,6},{8,10},{12,14},{16,18},{20,22},{24,26},{28,30},{1,3},{... | collective-permute-start | bytes 5013512 | tf_op jit(solution)/shard_map/ppermute | solution.py:626
  55.0 1.4 %collective-permute-start.11 = (f32[400,1024]{1,0:T(8,128)S(1)}, f32[400,1024]{1,0:T(8,128)S(1)}, u32[]{:S(2)}, u32[]{:S(2)}) collective-permute-start(f32[400,1024]{1,0:T(8,128)S(1)} %get-tuple-element.97), channel_id=1, source_target_pairs={{0,2},{4,6},{8,10},{12,14},{16,18},{20,22},{24,26},{28,30},{1,3},{... | collective-permute-start | bytes 4915208 | tf_op jit(solution)/shard_map/ppermute | solution.py:626
  56.4 1.3 %collective-permute-start.8 = (f32[400,512]{1,0:T(8,128)S(1)}, f32[400,512]{1,0:T(8,128)S(1)}, u32[]{:S(2)}, u32[]{:S(2)}) collective-permute-start(f32[400,512]{1,0:T(8,128)S(1)} %get-tuple-element.92), channel_id=1, source_target_pairs={{2,4},{6,8},{10,12},{14,16},{18,20},{22,24},{26,28},{30,0},{3,5},{... | collective-permute-start | bytes 2457608 | tf_op jit(solution)/shard_map/ppermute | solution.py:621
  57.7 1.3 %collective-permute-start.7 = (f32[400,256]{1,0:T(8,128)S(1)}, f32[400,256]{1,0:T(8,128)S(1)}, u32[]{:S(2)}, u32[]{:S(2)}) collective-permute-start(f32[400,256]{1,0:T(8,128)S(1)} %get-tuple-element.81), channel_id=1, source_target_pairs={{2,4},{6,8},{10,12},{14,16},{18,20},{22,24},{26,28},{30,0},{3,5},{... | collective-permute-start | bytes 1228808 | tf_op jit(solution)/shard_map/ppermute | solution.py:621
  59.0 3.7 %prepare1.1 = (f32[400,256]{1,0:T(8,128)S(1)}, f32[400,256]{1,0:T(8,128)S(1)}, bf16[400,256]{1,0:T(8,128)(2,1)S(1)}, bf16[256,400]{1,0:T(8,128)(2,1)S(1)}, bf16[...) custom-call(f32[400,2048]{1,0:T(8,128)S(1)} %get-tuple-element.79.le, ...), custom_call_target="tpu_custom_call" | custom-call | flops 1000000 | bytes 100000 | tf_op jit(solution)/shard_map/prepare1/pallas_call | solution.py:328
  62.8 0.0 collective-permute-done.11.refs_16_
  62.8 0.0 collective-permute-done.10.refs_15_
  62.8 1.0 %last_near.1 = (f32[400,2048]{1,0:T(8,128)}, f32[1,2048]{1,0:T(1,128)S(1)}, f32[32,400]{1,0:T(8,128)S(1)}, f32[400,2048]{1,0:T(8,128)}, f32[1,2048]{1,0:T(1,128)}) custom-call(f32[400,2048]{1,0:T(8,128)S(1)} %get-tuple-element.79.left.refs_0_, f32[1,2048]{1,0:T(1,128)S(1)} %get-tuple-element.80.refs_1_, f32[1,2048]{1,0:T(1,128)S(1)} %bitcast.13, ...), custom_call_target="tpu_custom_call" | custom-call | flops 1000000 | bytes 100000 | tf_op jit(solution)/shard_map/last_near/pallas_call | solution.py:328
  63.8 2.6 %collective-permute-done.9.refs_0_ = f32[400,1280]{1,0:T(8,128)S(1)} collective-permute-done((f32[400,1280]{1,0:T(8,128)S(1)}, f32[400,1280]{1,0:T(8,128)S(1)}, u32[]{:S(2)}, u32[]{:S(2)}) %collective-permute-start.9) | collective-permute-done | bytes 2048032 | tf_op jit(solution)/shard_map/ppermute | solution.py:621
  66.4 2.5 %last_piece0.1 = (f32[400,256]{1,0:T(8,128)S(1)}, f32[400,256]{1,0:T(8,128)S(1)}, f32[400,1280]{1,0:T(8,128)S(1)}) custom-call(f32[400,1280]{1,0:T(8,128)S(1)} %collective-permute-done.9.refs_0_, bf16[400,256]{1,0:T(8,128)(2,1)S(1)} %get-tuple-element.84.refs_6_.refs_1_.refs_3_, bf16[256,400]{1,0:T(8,128)(2,1)S(1)} %get-tuple-element.85.refs_7_.refs_2_.refs_4_, ...), custom_call_target="tpu_custom_call" | custom-call | flops 1000000 | bytes 100000 | tf_op jit(solution)/shard_map/last_piece0/pallas_call | solution.py:328
  68.9 2.1 %early_edges0.1 = (bf16[800,256]{1,0:T(8,128)(2,1)S(1)}, f32[256,400]{1,0:T(8,128)}) custom-call(f32[400,256]{1,0:T(8,128)S(1)} %get-tuple-element.82.refs_4_.refs_0_.refs_1_, f32[400,256]{1,0:T(8,128)S(1)} %get-tuple-element.83.refs_5_.refs_1_.refs_2_, f32[400,256]{1,0:T(8,128)S(1)} %get-tuple-element.99.refs_2_.refs_5_, ...), custom_call_target="tpu_custom_call" | custom-call | flops 1000000 | bytes 100000 | tf_op jit(solution)/shard_map/early_edges0/pallas_call | solution.py:328
  71.0 1.9 %early_right0.1 = (f32[400,2048]{1,0:T(8,128)}, f32[1,2048]{1,0:T(1,128)S(1)}) custom-call(f32[400,1280]{1,0:T(8,128)S(1)} %collective-permute-done.9.refs_0_, f32[1,2048]{1,0:T(1,128)S(1)} %collective-permute-done.6.refs_17_.refs_1_.refs_9_, f32[400,1280]{1,0:T(8,128)S(1)} %get-tuple-element.101.refs_2_, ...), custom_call_target="tpu_custom_call", output_to_operand_aliasing={{1}: (5, {}), {0}: (6, {})} | custom-call | flops 1000000 | bytes 100000 | tf_op jit(solution)/shard_map/early_right0/pallas_call | solution.py:328
  72.9 2.3 %collective-permute-done.8.refs_0_ = f32[400,512]{1,0:T(8,128)S(1)} collective-permute-done((f32[400,512]{1,0:T(8,128)S(1)}, f32[400,512]{1,0:T(8,128)S(1)}, u32[]{:S(2)}, u32[]{:S(2)}) %collective-permute-start.8) | collective-permute-done | bytes 819232 | tf_op jit(solution)/shard_map/ppermute | solution.py:621
  75.1 1.2 %last_piece1.1 = (f32[400,256]{1,0:T(8,128)S(1)}, f32[400,256]{1,0:T(8,128)S(1)}, f32[400,512]{1,0:T(8,128)S(1)}) custom-call(f32[400,512]{1,0:T(8,128)S(1)} %collective-permute-done.8.refs_0_, bf16[400,256]{1,0:T(8,128)(2,1)S(1)} %get-tuple-element.84.refs_6_.refs_1_.refs_3_, ...), custom_call_target="tpu_custom_call", output_to_operand_aliasing={{0}: (5, {}), {1}: (6, {})} | custom-call | flops 1000000 | bytes 100000 | tf_op jit(solution)/shard_map/last_piece1/pallas_call | solution.py:328
  76.4 1.3 %early_edges1.1 = (bf16[800,256]{1,0:T(8,128)(2,1)S(1)}, f32[256,400]{1,0:T(8,128)S(1)}) custom-call(f32[400,256]{1,0:T(8,128)S(1)} %get-tuple-element.82.refs_4_.refs_0_.refs_1_, f32[400,256]{1,0:T(8,128)S(1)} %get-tuple-element.83.refs_5_.refs_1_.refs_2_, f32[400,256]{1,0:T(8,128)S(1)} %get-tuple-element.105.refs_2_, ...), custom_call_target="tpu_custom_call" | custom-call | flops 1000000 | bytes 100000 | tf_op jit(solution)/shard_map/early_edges1/pallas_call | solution.py:328
  77.7 1.5 %early_right1.1 = (f32[400,2048]{1,0:T(8,128)}, f32[1,2048]{1,0:T(1,128)S(1)}) custom-call(f32[400,512]{1,0:T(8,128)S(1)} %collective-permute-done.8.refs_0_, f32[1,2048]{1,0:T(1,128)S(1)} %collective-permute-done.6.refs_17_.refs_1_.refs_9_, f32[400,512]{1,0:T(8,128)S(1)} %get-tuple-element.109.refs_2_, ...), custom_call_target="tpu_custom_call", output_to_operand_aliasing={{1}: (5, {}), {0}: (6, {})} | custom-call | flops 1000000 | bytes 100000 | tf_op jit(solution)/shard_map/early_right1/pallas_call | solution.py:328
  79.2 0.3 collective-permute-done.7.refs_0_.refs_8_
  79.5 2.3 %late_edges.1 = (f32[400,256]{1,0:T(8,128)S(1)}, bf16[800,256]{1,0:T(8,128)(2,1)S(1)}, bf16[800,256]{1,0:T(8,128)(2,1)S(1)}, f32[32,400]{1,0:T(8,128)S(1)}, bf16...) custom-call(f32[400,256]{1,0:T(8,128)S(1)} %collective-permute-done.7.refs_0_.refs_8_, ...), custom_call_target="tpu_custom_call", output_to_operand_aliasing={{3}: (14, {})} | custom-call | flops 1000000 | bytes 100000 | tf_op jit(solution)/shard_map/late_edges/pallas_call | solution.py:328
  81.8 0.9 %ahead_left.1 = (f32[400,768]{1,0:T(8,128)S(1)}, f32[32,400]{1,0:T(8,128)S(1)}) custom-call(f32[400,2048]{1,0:T(8,128)S(1)} %get-tuple-element.79.left.refs_0_, f32[1,2048]{1,0:T(1,128)S(1)} %get-tuple-element.80.refs_1_, bf16[800,256]{1,0:T(8,128)(2,1)S(1)} %get-tuple-element.113.refs_2_, ...), custom_call_target="tpu_custom_call", output_to_operand_aliasing={{1}: (7, {})} | custom-call | flops 1000000 | bytes 100000 | tf_op jit(solution)/shard_map/ahead_left/pallas_call | solution.py:328
  82.7 1.8 %collective-permute-start.12 = (f32[32,400]{1,0:T(8,128)S(1)}, f32[32,400]{1,0:T(8,128)S(1)}, u32[]{:S(2)}, u32[]{:S(2)}) collective-permute-start(f32[32,400]{1,0:T(8,128)S(1)} %get-tuple-element.124.rest_0_), channel_id=1, source_target_pairs={{0,1},{1,0},{2,3},{3,2},{4,5},{5,4},{6,7},{7,6},{8,9},{9,8},{10,11... | collective-permute-start | bytes 153608 | tf_op jit(solution)/shard_map/ppermute | solution.py:643
  84.5 0.0 copy-start.8
  84.5 2.4 %late_slabs.1 = (f32[400,2048]{1,0:T(8,128)}, f32[400,2048]{1,0:T(8,128)}) custom-call(f32[400,2048]{1,0:T(8,128)S(1)} %get-tuple-element.79.left.refs_0_, f32[1,2048]{1,0:T(1,128)S(1)} %get-tuple-element.80.refs_1_, bf16[800,256]{1,0:T(8,128)(2,1)S(1)} %get-tuple-element.113.refs_2_, ...), custom_call_target="tpu_custom_call", output_to_operand_aliasing={{0}: (13, {}), {1}: (14, {})} | custom-call | flops 1000000 | bytes 100000 | tf_op jit(solution)/shard_map/late_slabs/pallas_call | solution.py:328
  86.9 0.1 collective-permute-done.12.rest_1_
  87.0 0.0 copy-done.8
  87.0 0.7 relation_update.1
  (1 shorter events, 0.0 us)
Async XLA Ops:
  0.6 11.1 %copy-start.9 = (f32[2048]{0:T(1024)S(1)}, f32[2048]{0:T(1024)}, u32[]{:S(2)}) copy-start(f32[2048]{0:T(1024)} %param.14) | copy-start | bytes 24580
  0.6 11.2 %copy-start = (f32[2048,400]{0,1:T(8,128)S(1)}, f32[2048,400]{0,1:T(8,128)}, u32[]{:S(2)}) copy-start(f32[2048,400]{0,1:T(8,128)} %param.11) | copy-start | bytes 9830404
  0.7 11.2 %copy-start.1 = (f32[32,400]{1,0:T(8,128)S(1)}, f32[32,400]{1,0:T(8,128)}, u32[]{:S(2)}) copy-start(f32[32,400]{1,0:T(8,128)} %relations.5) | copy-start | bytes 153604
  0.7 11.2 %copy-start.2 = (s32[2,256]{1,0:T(2,128)S(1)}, s32[2,256]{1,0:T(2,128)}, u32[]{:S(2)}) copy-start(s32[2,256]{1,0:T(2,128)} %refs_10_.1) | copy-start | bytes 6148
  0.7 11.2 %copy-start.3 = (s32[2,1000]{1,0:T(2,128)S(1)}, s32[2,1000]{1,0:T(2,128)}, u32[]{:S(2)}) copy-start(s32[2,1000]{1,0:T(2,128)} %nsrc.3) | copy-start | bytes 24004
  0.7 11.2 %copy-start.4 = (s32[2,1000]{1,0:T(2,128)S(1)}, s32[2,1000]{1,0:T(2,128)}, u32[]{:S(2)}) copy-start(s32[2,1000]{1,0:T(2,128)} %ndst.3) | copy-start | bytes 24004
  0.7 11.2 %copy-start.6 = (s32[2,256]{1,0:T(2,128)S(1)}, s32[2,256]{1,0:T(2,128)}, u32[]{:S(2)}) copy-start(s32[2,256]{1,0:T(2,128)} %src.3) | copy-start | bytes 6148
  0.7 11.2 %copy-start.7 = (s32[2,256]{1,0:T(2,128)S(1)}, s32[2,256]{1,0:T(2,128)}, u32[]{:S(2)}) copy-start(s32[2,256]{1,0:T(2,128)} %rid.3) | copy-start | bytes 6148
  0.7 43.7 %collective-permute-start.4 = (f32[400,2048]{1,0:T(8,128)}, f32[400,2048]{1,0:T(8,128)S(1)}, u32[]{:S(2)}, u32[]{:S(2)}) collective-permute-start(f32[400,2048]{1,0:T(8,128)} %bitcast.18), channel_id=1, source_target_pairs={{2,4},{6,8},{10,12},{14,16},{18,20},{22,24},{26,28},{30,0},{3,5},{... | collective-permute-start | bytes 9830408 | tf_op jit(solution)/shard_map/ppermute | solution.py:613
  4.4 11.3 %copy-start.5 = (f32[2048]{0:T(1024)S(1)}, f32[2048]{0:T(1024)}, u32[]{:S(2)}) copy-start(f32[2048]{0:T(1024)} %param.12) | copy-start | bytes 24580
  4.4 11.3 %collective-permute-start.2 = (f32[400,1024]{1,0:T(8,128)S(1)}, f32[400,1024]{1,0:T(8,128)S(1)}, u32[]{:S(2)}, u32[]{:S(2)}) collective-permute-start(f32[400,1024]{1,0:T(8,128)S(1)} %get-tuple-element.125), channel_id=1, source_target_pairs={{0,2},{4,6},{8,10},{12,14},{16,18},{20,22},{24,26},{28,30},{1,3},{... | collective-permute-start | bytes 4915208 | tf_op jit(solution)/shard_map/ppermute | solution.py:614
  10.3 5.4 %collective-permute-start.1 = (f32[400,1024]{1,0:T(8,128)S(1)}, f32[400,1024]{1,0:T(8,128)S(1)}, u32[]{:S(2)}, u32[]{:S(2)}) collective-permute-start(f32[400,1024]{1,0:T(8,128)S(1)} %get-tuple-element.126), channel_id=1, source_target_pairs={{0,2},{4,6},{8,10},{12,14},{16,18},{20,22},{24,26},{28,30},{1,3},{... | collective-permute-start | bytes 4915208 | tf_op jit(solution)/shard_map/ppermute | solution.py:614
  11.8 4.0 %collective-permute-start = (f32[2048]{0:T(1024)S(1)}, f32[2048]{0:T(1024)S(1)}, u32[]{:S(2)}, u32[]{:S(2)}) collective-permute-start(f32[2048]{0:T(1024)S(1)} %copy-done.9), channel_id=1, source_target_pairs={{0,2},{4,6},{8,10},{12,14},{16,18},{20,22},{24,26},{28,30},{2,0},{... | collective-permute-start | bytes 24584 | tf_op jit(solution)/shard_map/ppermute | solution.py:615
  15.9 50.4 %collective-permute-start.9 = (f32[400,1280]{1,0:T(8,128)S(1)}, f32[400,1280]{1,0:T(8,128)S(1)}, u32[]{:S(2)}, u32[]{:S(2)}) collective-permute-start(f32[400,1280]{1,0:T(8,128)S(1)} %get-tuple-element.93), channel_id=1, source_target_pairs={{2,4},{6,8},{10,12},{14,16},{18,20},{22,24},{26,28},{30,0},{3,5},{... | collective-permute-start | bytes 6144008 | tf_op jit(solution)/shard_map/ppermute | solution.py:621
  17.2 15.3 %collective-permute-start.5 = (f32[1,2048]{1,0:T(1,128)S(1)}, f32[1,2048]{1,0:T(1,128)S(1)}, u32[]{:S(2)}, u32[]{:S(2)}) collective-permute-start(f32[1,2048]{1,0:T(1,128)S(1)} %get-tuple-element.78), channel_id=1, source_target_pairs={{2,0},{6,4},{10,8},{14,12},{18,16},{22,20},{26,24},{30,28},{3,1},{... | collective-permute-start | bytes 24584 | tf_op jit(solution)/shard_map/ppermute | solution.py:622
  18.5 17.4 %collective-permute-start.3 = (f32[2048]{0:T(1024)S(1)}, f32[2048]{0:T(1024)S(1)}, u32[]{:S(2)}, u32[]{:S(2)}) collective-permute-start(f32[2048]{0:T(1024)S(1)} %collective-permute-done), channel_id=1, source_target_pairs={{0,4},{4,8},{8,12},{12,16},{16,20},{20,24},{24,28},{28,0},{1,5},{5... | collective-permute-start | bytes 24584 | tf_op jit(solution)/shard_map/ppermute | solution.py:616
  32.5 8.4 %collective-permute-start.6 = (f32[1,2048]{1,0:T(1,128)S(1)}, f32[1,2048]{1,0:T(1,128)S(1)}, u32[]{:S(2)}, u32[]{:S(2)}) collective-permute-start(f32[1,2048]{1,0:T(1,128)S(1)} %collective-permute-done.5), channel_id=1, source_target_pairs={{0,4},{4,8},{8,12},{12,16},{16,20},{20,24},{24,28},{28,0},{1,5},{5... | collective-permute-start | bytes 24584 | tf_op jit(solution)/shard_map/ppermute | solution.py:622
  53.6 9.2 %collective-permute-start.10 = (f32[408,1024]{1,0:T(8,128)S(1)}, f32[408,1024]{1,0:T(8,128)S(1)}, u32[]{:S(2)}, u32[]{:S(2)}) collective-permute-start(f32[408,1024]{1,0:T(8,128)S(1)} %get-tuple-element.96), channel_id=1, source_target_pairs={{0,2},{4,6},{8,10},{12,14},{16,18},{20,22},{24,26},{28,30},{1,3},{... | collective-permute-start | bytes 5013512 | tf_op jit(solution)/shard_map/ppermute | solution.py:626
  55.0 7.7 %collective-permute-start.11 = (f32[400,1024]{1,0:T(8,128)S(1)}, f32[400,1024]{1,0:T(8,128)S(1)}, u32[]{:S(2)}, u32[]{:S(2)}) collective-permute-start(f32[400,1024]{1,0:T(8,128)S(1)} %get-tuple-element.97), channel_id=1, source_target_pairs={{0,2},{4,6},{8,10},{12,14},{16,18},{20,22},{24,26},{28,30},{1,3},{... | collective-permute-start | bytes 4915208 | tf_op jit(solution)/shard_map/ppermute | solution.py:626
  56.4 18.7 %collective-permute-start.8 = (f32[400,512]{1,0:T(8,128)S(1)}, f32[400,512]{1,0:T(8,128)S(1)}, u32[]{:S(2)}, u32[]{:S(2)}) collective-permute-start(f32[400,512]{1,0:T(8,128)S(1)} %get-tuple-element.92), channel_id=1, source_target_pairs={{2,4},{6,8},{10,12},{14,16},{18,20},{22,24},{26,28},{30,0},{3,5},{... | collective-permute-start | bytes 2457608 | tf_op jit(solution)/shard_map/ppermute | solution.py:621
  57.7 21.8 %collective-permute-start.7 = (f32[400,256]{1,0:T(8,128)S(1)}, f32[400,256]{1,0:T(8,128)S(1)}, u32[]{:S(2)}, u32[]{:S(2)}) collective-permute-start(f32[400,256]{1,0:T(8,128)S(1)} %get-tuple-element.81), channel_id=1, source_target_pairs={{2,4},{6,8},{10,12},{14,16},{18,20},{22,24},{26,28},{30,0},{3,5},{... | collective-permute-start | bytes 1228808 | tf_op jit(solution)/shard_map/ppermute | solution.py:621
  82.7 4.3 %collective-permute-start.12 = (f32[32,400]{1,0:T(8,128)S(1)}, f32[32,400]{1,0:T(8,128)S(1)}, u32[]{:S(2)}, u32[]{:S(2)}) collective-permute-start(f32[32,400]{1,0:T(8,128)S(1)} %get-tuple-element.124.rest_0_), channel_id=1, source_target_pairs={{0,1},{1,0},{2,3},{3,2},{4,5},{5,4},{6,7},{7,6},{8,9},{9,8},{10,11... | collective-permute-start | bytes 153608 | tf_op jit(solution)/shard_map/ppermute | solution.py:643
  84.5 2.5 %copy-start.8 = (f32[32]{0:T(128)S(1)}, f32[32]{0:T(128)}, u32[]{:S(2)}) copy-start(f32[32]{0:T(128)} %param.16) | copy-start | bytes 388

commit v7 on v3

--- a/solution.py
+++ b/solution.py
@@ -103,7 +103,7 @@
 
 
 def often(weight, times):
-    return (weight.astype(F32) * times).astype(BF16)
+    return weight * times.astype(BF16)
 
 
 def negatives(rows16, query, query_rows, times, number):

time: 88.1 us -> 88.2 us (level)
  transfers between devices with their start and end apart: 13 -> 13, of which waited for: 7 -> 8; matrix products, arithmetic and copies ran while one was open for 2% -> 2% of each run, Pallas kernels for 37% -> 37%
where the time goes in v7:
time: 88.2 us; the launch traced here: 87.8 us
  Pallas kernels  36.4 us (41%)
  starting transfers between devices  25.6 us (29%)
  waiting for transfers between devices  22.6 us (26%)
  local copies, waits for them, and re-layouts  2.21 us (3%)
  between operations  1 us (1%)
    pallas_call x15, Pallas kernels, call(): pl.pallas_call(kernel, out_shape=tuple(shapes), in_specs=[large if i in i...  36.4 us
    ppermute x2, waiting for transfers between devices, local(): state = lax.ppermute(lax.ppermute(state, 'blk', back), 'blk', skip)  16 us
    ppermute x2, starting transfers between devices, local(): lax.ppermute(right[:, at:at + size], 'blk', inside)  7.28 us
    ppermute x2, starting transfers between devices, local(): state = lax.ppermute(lax.ppermute(state, 'blk', back), 'blk', skip)  4.74 us
    ppermute x3, starting transfers between devices, local(): far = [lax.ppermute(piece, 'blk', across) for piece in far]  3.88 us
    ppermute x3, waiting for transfers between devices, local(): far = [lax.ppermute(piece, 'blk', across) for piece in far]  3.48 us
    ppermute x1, starting transfers between devices, local(): state_far = lax.ppermute(state_near, 'blk', skip).reshape(1, rows)  3.46 us
    ppermute x1, waiting for transfers between devices, local(): right_far = lax.ppermute(right, 'blk', across)  2.95 us
  transfers between devices with their start and end apart: 13, of which 8 were waited for; matrix products, arithmetic and copies ran while one was open for 2% of the time, Pallas kernels for 37%

profile of v7, /device:TPU:0, one launch (start us, length us, event | category | flops | bytes accessed | tf_op | source)
XLA Modules:
  0.0 87.8 jit_solution(13492062212185963801)
XLA Ops:
  0.6 0.0 copy-start.9
  0.6 0.0 copy-start
  0.7 0.0 copy-start.1
  0.7 0.0 copy-start.2
  0.7 0.0 copy-start.3
  0.7 0.0 copy-start.4
  0.7 0.0 copy-start.6
  0.7 0.0 copy-start.7
  0.7 1.6 %collective-permute-start.4 = (f32[400,2048]{1,0:T(8,128)}, f32[400,2048]{1,0:T(8,128)S(1)}, u32[]{:S(2)}, u32[]{:S(2)}) collective-permute-start(f32[400,2048]{1,0:T(8,128)} %bitcast.18), channel_id=1, source_target_pairs={{2,4},{6,8},{10,12},{14,16},{18,20},{22,24},{26,28},{30,0},{3,5},{... | collective-permute-start | bytes 9830408 | tf_op jit(solution)/shard_map/ppermute | solution.py:611
  2.3 2.2 %fusion = (f32[400,1024]{1,0:T(8,128)S(1)}, f32[400,1024]{1,0:T(8,128)S(1)}) fusion(f32[400,2048]{1,0:T(8,128)} %bitcast.19), kind=kLoop, calls=%fused_computation | loop fusion | bytes 6553600 | tf_op jit(solution)/shard_map/slice | solution.py:612
  4.4 0.0 copy-start.5
  4.4 5.9 %collective-permute-start.2 = (f32[400,1024]{1,0:T(8,128)S(1)}, f32[400,1024]{1,0:T(8,128)S(1)}, u32[]{:S(2)}, u32[]{:S(2)}) collective-permute-start(f32[400,1024]{1,0:T(8,128)S(1)} %get-tuple-element.125), channel_id=1, source_target_pairs={{0,2},{4,6},{8,10},{12,14},{16,18},{20,22},{24,26},{28,30},{1,3},{... | collective-permute-start | bytes 4915208 | tf_op jit(solution)/shard_map/ppermute | solution.py:612
  10.3 1.4 %collective-permute-start.1 = (f32[400,1024]{1,0:T(8,128)S(1)}, f32[400,1024]{1,0:T(8,128)S(1)}, u32[]{:S(2)}, u32[]{:S(2)}) collective-permute-start(f32[400,1024]{1,0:T(8,128)S(1)} %get-tuple-element.126), channel_id=1, source_target_pairs={{0,2},{4,6},{8,10},{12,14},{16,18},{20,22},{24,26},{28,30},{1,3},{... | collective-permute-start | bytes 4915208 | tf_op jit(solution)/shard_map/ppermute | solution.py:612
  11.7 0.0 copy-done.9
  11.8 0.1 collective-permute-start
  11.8 0.0 copy-done
  11.8 0.0 copy-done.1
  11.9 0.0 copy-done.2
  11.9 0.0 copy-done.3
  11.9 0.0 copy-done.4
  11.9 0.0 copy-done.6
  11.9 0.0 copy-done.7
  11.9 3.7 %prepare0.1 = (f32[400,256]{1,0:T(8,128)S(1)}, f32[400,256]{1,0:T(8,128)S(1)}, bf16[400,256]{1,0:T(8,128)(2,1)S(1)}, bf16[256,400]{1,0:T(8,128)(2,1)S(1)}, bf16[...) custom-call(f32[400,2048]{1,0:T(8,128)S(1)} %bitcast.9, ...), custom_call_target="tpu_custom_call" | custom-call | flops 1000000 | bytes 100000 | tf_op jit(solution)/shard_map/prepare0/pallas_call | solution.py:328
  15.6 0.1 collective-permute-done
  15.7 0.0 collective-permute-done.2.refs_16_
  15.7 0.0 collective-permute-done.1.refs_15_
  15.7 0.0 copy-done.5
  15.7 0.2 first_near.1
  15.9 1.3 %collective-permute-start.9 = (f32[400,1280]{1,0:T(8,128)S(1)}, f32[400,1280]{1,0:T(8,128)S(1)}, u32[]{:S(2)}, u32[]{:S(2)}) collective-permute-start(f32[400,1280]{1,0:T(8,128)S(1)} %get-tuple-element.93), channel_id=1, source_target_pairs={{2,4},{6,8},{10,12},{14,16},{18,20},{22,24},{26,28},{30,0},{3,5},{... | collective-permute-start | bytes 6144008 | tf_op jit(solution)/shard_map/ppermute | solution.py:619
  17.2 1.3 %collective-permute-start.5 = (f32[1,2048]{1,0:T(1,128)S(1)}, f32[1,2048]{1,0:T(1,128)S(1)}, u32[]{:S(2)}, u32[]{:S(2)}) collective-permute-start(f32[1,2048]{1,0:T(1,128)S(1)} %get-tuple-element.78), channel_id=1, source_target_pairs={{2,0},{6,4},{10,8},{14,12},{18,16},{22,20},{26,24},{30,28},{3,1},{... | collective-permute-start | bytes 24584 | tf_op jit(solution)/shard_map/ppermute | solution.py:620
  18.5 3.5 %collective-permute-start.3 = (f32[2048]{0:T(1024)S(1)}, f32[2048]{0:T(1024)S(1)}, u32[]{:S(2)}, u32[]{:S(2)}) collective-permute-start(f32[2048]{0:T(1024)S(1)} %collective-permute-done), channel_id=1, source_target_pairs={{0,4},{4,8},{8,12},{12,16},{16,20},{20,24},{24,28},{28,0},{1,5},{5... | collective-permute-start | bytes 24584 | tf_op jit(solution)/shard_map/ppermute | solution.py:614
  22.0 11.1 %collective-permute-done.5 = f32[1,2048]{1,0:T(1,128)S(1)} collective-permute-done((f32[1,2048]{1,0:T(1,128)S(1)}, f32[1,2048]{1,0:T(1,128)S(1)}, u32[]{:S(2)}, u32[]{:S(2)}) %collective-permute-start.5) | collective-permute-done | bytes 8224 | tf_op jit(solution)/shard_map/ppermute | solution.py:620
  33.1 3.4 %collective-permute-start.6 = (f32[1,2048]{1,0:T(1,128)S(1)}, f32[1,2048]{1,0:T(1,128)S(1)}, u32[]{:S(2)}, u32[]{:S(2)}) collective-permute-start(f32[1,2048]{1,0:T(1,128)S(1)} %collective-permute-done.5), channel_id=1, source_target_pairs={{0,4},{4,8},{8,12},{12,16},{16,20},{20,24},{24,28},{28,0},{1,5},{5... | collective-permute-start | bytes 24584 | tf_op jit(solution)/shard_map/ppermute | solution.py:620
  36.5 0.0 collective-permute-done.3
  36.5 4.9 %collective-permute-done.6.refs_17_.refs_1_.refs_9_ = f32[1,2048]{1,0:T(1,128)S(1)} collective-permute-done((f32[1,2048]{1,0:T(1,128)S(1)}, f32[1,2048]{1,0:T(1,128)S(1)}, u32[]{:S(2)}, u32[]{:S(2)}) %collective-permute-start.6) | collective-permute-done | bytes 8224 | tf_op jit(solution)/shard_map/ppermute | solution.py:620
  41.5 2.9 %collective-permute-done.4.refs_15_ = f32[400,2048]{1,0:T(8,128)S(1)} collective-permute-done((f32[400,2048]{1,0:T(8,128)}, f32[400,2048]{1,0:T(8,128)S(1)}, u32[]{:S(2)}, u32[]{:S(2)}) %collective-permute-start.4) | collective-permute-done | bytes 3276832 | tf_op jit(solution)/shard_map/ppermute | solution.py:611
  44.4 10.9 %first_far.1 = (f32[400,2048]{1,0:T(8,128)S(1)}, f32[1,2048]{1,0:T(1,128)S(1)}, f32[32,400]{1,0:T(8,128)S(1)}, f32[408,1024]{1,0:T(8,128)S(1)}, f32[400,1024]{1,0:T(8,128)S(1)}, /*index=5*/f32[1,2048]{1,0:T(1,128)}) custom-call(f32[400,2048]{1,0:T(8,128)S(1)} %bitcast.11, f32[1,2048]{1,0:T(1,128)S(1)} %get-tuple-element.75.refs_1_, ...), custom_call_target="tpu_custom_call", output_to_operand_aliasing={{0}: (16, {})} | custom-call | flops 1000000 | bytes 100000 | tf_op jit(solution)/shard_map/first_far/pallas_call | solution.py:328
  55.3 1.4 %collective-permute-start.10 = (f32[408,1024]{1,0:T(8,128)S(1)}, f32[408,1024]{1,0:T(8,128)S(1)}, u32[]{:S(2)}, u32[]{:S(2)}) collective-permute-start(f32[408,1024]{1,0:T(8,128)S(1)} %get-tuple-element.96), channel_id=1, source_target_pairs={{0,2},{4,6},{8,10},{12,14},{16,18},{20,22},{24,26},{28,30},{1,3},{... | collective-permute-start | bytes 5013512 | tf_op jit(solution)/shard_map/ppermute | solution.py:624
  56.7 1.4 %collective-permute-start.11 = (f32[400,1024]{1,0:T(8,128)S(1)}, f32[400,1024]{1,0:T(8,128)S(1)}, u32[]{:S(2)}, u32[]{:S(2)}) collective-permute-start(f32[400,1024]{1,0:T(8,128)S(1)} %get-tuple-element.97), channel_id=1, source_target_pairs={{0,2},{4,6},{8,10},{12,14},{16,18},{20,22},{24,26},{28,30},{1,3},{... | collective-permute-start | bytes 4915208 | tf_op jit(solution)/shard_map/ppermute | solution.py:624
  58.1 1.3 %collective-permute-start.8 = (f32[400,512]{1,0:T(8,128)S(1)}, f32[400,512]{1,0:T(8,128)S(1)}, u32[]{:S(2)}, u32[]{:S(2)}) collective-permute-start(f32[400,512]{1,0:T(8,128)S(1)} %get-tuple-element.92), channel_id=1, source_target_pairs={{2,4},{6,8},{10,12},{14,16},{18,20},{22,24},{26,28},{30,0},{3,5},{... | collective-permute-start | bytes 2457608 | tf_op jit(solution)/shard_map/ppermute | solution.py:619
  59.4 1.3 %collective-permute-start.7 = (f32[400,256]{1,0:T(8,128)S(1)}, f32[400,256]{1,0:T(8,128)S(1)}, u32[]{:S(2)}, u32[]{:S(2)}) collective-permute-start(f32[400,256]{1,0:T(8,128)S(1)} %get-tuple-element.81), channel_id=1, source_target_pairs={{2,4},{6,8},{10,12},{14,16},{18,20},{22,24},{26,28},{30,0},{3,5},{... | collective-permute-start | bytes 1228808 | tf_op jit(solution)/shard_map/ppermute | solution.py:619
  60.7 3.7 %prepare1.1 = (f32[400,256]{1,0:T(8,128)S(1)}, f32[400,256]{1,0:T(8,128)S(1)}, bf16[400,256]{1,0:T(8,128)(2,1)S(1)}, bf16[256,400]{1,0:T(8,128)(2,1)S(1)}, bf16[...) custom-call(f32[400,2048]{1,0:T(8,128)S(1)} %get-tuple-element.79.le, ...), custom_call_target="tpu_custom_call" | custom-call | flops 1000000 | bytes 100000 | tf_op jit(solution)/shard_map/prepare1/pallas_call | solution.py:328
  64.4 0.0 collective-permute-done.11.refs_16_
  64.4 0.0 collective-permute-done.10.refs_15_
  64.5 1.0 %last_near.1 = (f32[400,2048]{1,0:T(8,128)}, f32[1,2048]{1,0:T(1,128)S(1)}, f32[32,400]{1,0:T(8,128)S(1)}, f32[400,2048]{1,0:T(8,128)}, f32[1,2048]{1,0:T(1,128)}) custom-call(f32[400,2048]{1,0:T(8,128)S(1)} %get-tuple-element.79.left.refs_0_, f32[1,2048]{1,0:T(1,128)S(1)} %get-tuple-element.80.refs_1_, f32[1,2048]{1,0:T(1,128)S(1)} %bitcast.13, ...), custom_call_target="tpu_custom_call" | custom-call | flops 1000000 | bytes 100000 | tf_op jit(solution)/shard_map/last_near/pallas_call | solution.py:328
  65.4 0.9 %collective-permute-done.9.refs_0_ = f32[400,1280]{1,0:T(8,128)S(1)} collective-permute-done((f32[400,1280]{1,0:T(8,128)S(1)}, f32[400,1280]{1,0:T(8,128)S(1)}, u32[]{:S(2)}, u32[]{:S(2)}) %collective-permute-start.9) | collective-permute-done | bytes 2048032 | tf_op jit(solution)/shard_map/ppermute | solution.py:619
  66.4 2.5 %last_piece0.1 = (f32[400,256]{1,0:T(8,128)S(1)}, f32[400,256]{1,0:T(8,128)S(1)}, f32[400,1280]{1,0:T(8,128)S(1)}) custom-call(f32[400,1280]{1,0:T(8,128)S(1)} %collective-permute-done.9.refs_0_, bf16[400,256]{1,0:T(8,128)(2,1)S(1)} %get-tuple-element.84.refs_6_.refs_1_.refs_3_, bf16[256,400]{1,0:T(8,128)(2,1)S(1)} %get-tuple-element.85.refs_7_.refs_2_.refs_4_, ...), custom_call_target="tpu_custom_call" | custom-call | flops 1000000 | bytes 100000 | tf_op jit(solution)/shard_map/last_piece0/pallas_call | solution.py:328
  68.9 2.1 %early_edges0.1 = (bf16[800,256]{1,0:T(8,128)(2,1)S(1)}, f32[256,400]{1,0:T(8,128)}) custom-call(f32[400,256]{1,0:T(8,128)S(1)} %get-tuple-element.82.refs_4_.refs_0_.refs_1_, f32[400,256]{1,0:T(8,128)S(1)} %get-tuple-element.83.refs_5_.refs_1_.refs_2_, f32[400,256]{1,0:T(8,128)S(1)} %get-tuple-element.99.refs_2_.refs_5_, ...), custom_call_target="tpu_custom_call" | custom-call | flops 1000000 | bytes 100000 | tf_op jit(solution)/shard_map/early_edges0/pallas_call | solution.py:328
  71.0 1.9 %early_right0.1 = (f32[400,2048]{1,0:T(8,128)}, f32[1,2048]{1,0:T(1,128)S(1)}) custom-call(f32[400,1280]{1,0:T(8,128)S(1)} %collective-permute-done.9.refs_0_, f32[1,2048]{1,0:T(1,128)S(1)} %collective-permute-done.6.refs_17_.refs_1_.refs_9_, f32[400,1280]{1,0:T(8,128)S(1)} %get-tuple-element.101.refs_2_, ...), custom_call_target="tpu_custom_call", output_to_operand_aliasing={{1}: (5, {}), {0}: (6, {})} | custom-call | flops 1000000 | bytes 100000 | tf_op jit(solution)/shard_map/early_right0/pallas_call | solution.py:328
  72.9 2.3 %collective-permute-done.8.refs_0_ = f32[400,512]{1,0:T(8,128)S(1)} collective-permute-done((f32[400,512]{1,0:T(8,128)S(1)}, f32[400,512]{1,0:T(8,128)S(1)}, u32[]{:S(2)}, u32[]{:S(2)}) %collective-permute-start.8) | collective-permute-done | bytes 819232 | tf_op jit(solution)/shard_map/ppermute | solution.py:619
  75.1 1.2 %last_piece1.1 = (f32[400,256]{1,0:T(8,128)S(1)}, f32[400,256]{1,0:T(8,128)S(1)}, f32[400,512]{1,0:T(8,128)S(1)}) custom-call(f32[400,512]{1,0:T(8,128)S(1)} %collective-permute-done.8.refs_0_, bf16[400,256]{1,0:T(8,128)(2,1)S(1)} %get-tuple-element.84.refs_6_.refs_1_.refs_3_, ...), custom_call_target="tpu_custom_call", output_to_operand_aliasing={{0}: (5, {}), {1}: (6, {})} | custom-call | flops 1000000 | bytes 100000 | tf_op jit(solution)/shard_map/last_piece1/pallas_call | solution.py:328
  76.4 1.3 %early_edges1.1 = (bf16[800,256]{1,0:T(8,128)(2,1)S(1)}, f32[256,400]{1,0:T(8,128)S(1)}) custom-call(f32[400,256]{1,0:T(8,128)S(1)} %get-tuple-element.82.refs_4_.refs_0_.refs_1_, f32[400,256]{1,0:T(8,128)S(1)} %get-tuple-element.83.refs_5_.refs_1_.refs_2_, f32[400,256]{1,0:T(8,128)S(1)} %get-tuple-element.105.refs_2_, ...), custom_call_target="tpu_custom_call" | custom-call | flops 1000000 | bytes 100000 | tf_op jit(solution)/shard_map/early_edges1/pallas_call | solution.py:328
  77.7 1.5 %early_right1.1 = (f32[400,2048]{1,0:T(8,128)}, f32[1,2048]{1,0:T(1,128)S(1)}) custom-call(f32[400,512]{1,0:T(8,128)S(1)} %collective-permute-done.8.refs_0_, f32[1,2048]{1,0:T(1,128)S(1)} %collective-permute-done.6.refs_17_.refs_1_.refs_9_, f32[400,512]{1,0:T(8,128)S(1)} %get-tuple-element.109.refs_2_, ...), custom_call_target="tpu_custom_call", output_to_operand_aliasing={{1}: (5, {}), {0}: (6, {})} | custom-call | flops 1000000 | bytes 100000 | tf_op jit(solution)/shard_map/early_right1/pallas_call | solution.py:328
  79.2 0.3 collective-permute-done.7.refs_0_.refs_8_
  79.5 2.3 %late_edges.1 = (f32[400,256]{1,0:T(8,128)S(1)}, bf16[800,256]{1,0:T(8,128)(2,1)S(1)}, bf16[800,256]{1,0:T(8,128)(2,1)S(1)}, f32[32,400]{1,0:T(8,128)S(1)}, bf16...) custom-call(f32[400,256]{1,0:T(8,128)S(1)} %collective-permute-done.7.refs_0_.refs_8_, ...), custom_call_target="tpu_custom_call", output_to_operand_aliasing={{3}: (14, {})} | custom-call | flops 1000000 | bytes 100000 | tf_op jit(solution)/shard_map/late_edges/pallas_call | solution.py:328
  81.8 0.9 %ahead_left.1 = (f32[400,768]{1,0:T(8,128)S(1)}, f32[32,400]{1,0:T(8,128)S(1)}) custom-call(f32[400,2048]{1,0:T(8,128)S(1)} %get-tuple-element.79.left.refs_0_, f32[1,2048]{1,0:T(1,128)S(1)} %get-tuple-element.80.refs_1_, bf16[800,256]{1,0:T(8,128)(2,1)S(1)} %get-tuple-element.113.refs_2_, ...), custom_call_target="tpu_custom_call", output_to_operand_aliasing={{1}: (7, {})} | custom-call | flops 1000000 | bytes 100000 | tf_op jit(solution)/shard_map/ahead_left/pallas_call | solution.py:328
  82.7 1.8 %collective-permute-start.12 = (f32[32,400]{1,0:T(8,128)S(1)}, f32[32,400]{1,0:T(8,128)S(1)}, u32[]{:S(2)}, u32[]{:S(2)}) collective-permute-start(f32[32,400]{1,0:T(8,128)S(1)} %get-tuple-element.124.rest_0_), channel_id=1, source_target_pairs={{0,1},{1,0},{2,3},{3,2},{4,5},{5,4},{6,7},{7,6},{8,9},{9,8},{10,11... | collective-permute-start | bytes 153608 | tf_op jit(solution)/shard_map/ppermute | solution.py:641
  84.5 0.0 copy-start.8
  84.6 2.4 %late_slabs.1 = (f32[400,2048]{1,0:T(8,128)}, f32[400,2048]{1,0:T(8,128)}) custom-call(f32[400,2048]{1,0:T(8,128)S(1)} %get-tuple-element.79.left.refs_0_, f32[1,2048]{1,0:T(1,128)S(1)} %get-tuple-element.80.refs_1_, bf16[800,256]{1,0:T(8,128)(2,1)S(1)} %get-tuple-element.113.refs_2_, ...), custom_call_target="tpu_custom_call", output_to_operand_aliasing={{0}: (13, {}), {1}: (14, {})} | custom-call | flops 1000000 | bytes 100000 | tf_op jit(solution)/shard_map/late_slabs/pallas_call | solution.py:328
  87.0 0.1 collective-permute-done.12.rest_1_
  87.1 0.0 copy-done.8
  87.1 0.7 relation_update.1
  (1 shorter events, 0.0 us)
Async XLA Ops:
  0.6 11.1 %copy-start.9 = (f32[2048]{0:T(1024)S(1)}, f32[2048]{0:T(1024)}, u32[]{:S(2)}) copy-start(f32[2048]{0:T(1024)} %param.14) | copy-start | bytes 24580
  0.6 11.2 %copy-start = (f32[2048,400]{0,1:T(8,128)S(1)}, f32[2048,400]{0,1:T(8,128)}, u32[]{:S(2)}) copy-start(f32[2048,400]{0,1:T(8,128)} %param.11) | copy-start | bytes 9830404
  0.7 11.2 %copy-start.1 = (f32[32,400]{1,0:T(8,128)S(1)}, f32[32,400]{1,0:T(8,128)}, u32[]{:S(2)}) copy-start(f32[32,400]{1,0:T(8,128)} %relations.5) | copy-start | bytes 153604
  0.7 11.2 %copy-start.2 = (s32[2,256]{1,0:T(2,128)S(1)}, s32[2,256]{1,0:T(2,128)}, u32[]{:S(2)}) copy-start(s32[2,256]{1,0:T(2,128)} %refs_10_.1) | copy-start | bytes 6148
  0.7 11.2 %copy-start.3 = (s32[2,1000]{1,0:T(2,128)S(1)}, s32[2,1000]{1,0:T(2,128)}, u32[]{:S(2)}) copy-start(s32[2,1000]{1,0:T(2,128)} %nsrc.3) | copy-start | bytes 24004
  0.7 11.2 %copy-start.4 = (s32[2,1000]{1,0:T(2,128)S(1)}, s32[2,1000]{1,0:T(2,128)}, u32[]{:S(2)}) copy-start(s32[2,1000]{1,0:T(2,128)} %ndst.3) | copy-start | bytes 24004
  0.7 11.2 %copy-start.6 = (s32[2,256]{1,0:T(2,128)S(1)}, s32[2,256]{1,0:T(2,128)}, u32[]{:S(2)}) copy-start(s32[2,256]{1,0:T(2,128)} %src.3) | copy-start | bytes 6148
  0.7 11.2 %copy-start.7 = (s32[2,256]{1,0:T(2,128)S(1)}, s32[2,256]{1,0:T(2,128)}, u32[]{:S(2)}) copy-start(s32[2,256]{1,0:T(2,128)} %rid.3) | copy-start | bytes 6148
  0.7 43.7 %collective-permute-start.4 = (f32[400,2048]{1,0:T(8,128)}, f32[400,2048]{1,0:T(8,128)S(1)}, u32[]{:S(2)}, u32[]{:S(2)}) collective-permute-start(f32[400,2048]{1,0:T(8,128)} %bitcast.18), channel_id=1, source_target_pairs={{2,4},{6,8},{10,12},{14,16},{18,20},{22,24},{26,28},{30,0},{3,5},{... | collective-permute-start | bytes 9830408 | tf_op jit(solution)/shard_map/ppermute | solution.py:611
  4.4 11.3 %copy-start.5 = (f32[2048]{0:T(1024)S(1)}, f32[2048]{0:T(1024)}, u32[]{:S(2)}) copy-start(f32[2048]{0:T(1024)} %param.12) | copy-start | bytes 24580
  4.4 11.3 %collective-permute-start.2 = (f32[400,1024]{1,0:T(8,128)S(1)}, f32[400,1024]{1,0:T(8,128)S(1)}, u32[]{:S(2)}, u32[]{:S(2)}) collective-permute-start(f32[400,1024]{1,0:T(8,128)S(1)} %get-tuple-element.125), channel_id=1, source_target_pairs={{0,2},{4,6},{8,10},{12,14},{16,18},{20,22},{24,26},{28,30},{1,3},{... | collective-permute-start | bytes 4915208 | tf_op jit(solution)/shard_map/ppermute | solution.py:612
  10.3 5.4 %collective-permute-start.1 = (f32[400,1024]{1,0:T(8,128)S(1)}, f32[400,1024]{1,0:T(8,128)S(1)}, u32[]{:S(2)}, u32[]{:S(2)}) collective-permute-start(f32[400,1024]{1,0:T(8,128)S(1)} %get-tuple-element.126), channel_id=1, source_target_pairs={{0,2},{4,6},{8,10},{12,14},{16,18},{20,22},{24,26},{28,30},{1,3},{... | collective-permute-start | bytes 4915208 | tf_op jit(solution)/shard_map/ppermute | solution.py:612
  11.8 4.0 %collective-permute-start = (f32[2048]{0:T(1024)S(1)}, f32[2048]{0:T(1024)S(1)}, u32[]{:S(2)}, u32[]{:S(2)}) collective-permute-start(f32[2048]{0:T(1024)S(1)} %copy-done.9), channel_id=1, source_target_pairs={{0,2},{4,6},{8,10},{12,14},{16,18},{20,22},{24,26},{28,30},{2,0},{... | collective-permute-start | bytes 24584 | tf_op jit(solution)/shard_map/ppermute | solution.py:613
  15.9 50.4 %collective-permute-start.9 = (f32[400,1280]{1,0:T(8,128)S(1)}, f32[400,1280]{1,0:T(8,128)S(1)}, u32[]{:S(2)}, u32[]{:S(2)}) collective-permute-start(f32[400,1280]{1,0:T(8,128)S(1)} %get-tuple-element.93), channel_id=1, source_target_pairs={{2,4},{6,8},{10,12},{14,16},{18,20},{22,24},{26,28},{30,0},{3,5},{... | collective-permute-start | bytes 6144008 | tf_op jit(solution)/shard_map/ppermute | solution.py:619
  17.2 15.9 %collective-permute-start.5 = (f32[1,2048]{1,0:T(1,128)S(1)}, f32[1,2048]{1,0:T(1,128)S(1)}, u32[]{:S(2)}, u32[]{:S(2)}) collective-permute-start(f32[1,2048]{1,0:T(1,128)S(1)} %get-tuple-element.78), channel_id=1, source_target_pairs={{2,0},{6,4},{10,8},{14,12},{18,16},{22,20},{26,24},{30,28},{3,1},{... | collective-permute-start | bytes 24584 | tf_op jit(solution)/shard_map/ppermute | solution.py:620
  18.5 18.0 %collective-permute-start.3 = (f32[2048]{0:T(1024)S(1)}, f32[2048]{0:T(1024)S(1)}, u32[]{:S(2)}, u32[]{:S(2)}) collective-permute-start(f32[2048]{0:T(1024)S(1)} %collective-permute-done), channel_id=1, source_target_pairs={{0,4},{4,8},{8,12},{12,16},{16,20},{20,24},{24,28},{28,0},{1,5},{5... | collective-permute-start | bytes 24584 | tf_op jit(solution)/shard_map/ppermute | solution.py:614
  33.1 8.4 %collective-permute-start.6 = (f32[1,2048]{1,0:T(1,128)S(1)}, f32[1,2048]{1,0:T(1,128)S(1)}, u32[]{:S(2)}, u32[]{:S(2)}) collective-permute-start(f32[1,2048]{1,0:T(1,128)S(1)} %collective-permute-done.5), channel_id=1, source_target_pairs={{0,4},{4,8},{8,12},{12,16},{16,20},{20,24},{24,28},{28,0},{1,5},{5... | collective-permute-start | bytes 24584 | tf_op jit(solution)/shard_map/ppermute | solution.py:620
  55.3 9.2 %collective-permute-start.10 = (f32[408,1024]{1,0:T(8,128)S(1)}, f32[408,1024]{1,0:T(8,128)S(1)}, u32[]{:S(2)}, u32[]{:S(2)}) collective-permute-start(f32[408,1024]{1,0:T(8,128)S(1)} %get-tuple-element.96), channel_id=1, source_target_pairs={{0,2},{4,6},{8,10},{12,14},{16,18},{20,22},{24,26},{28,30},{1,3},{... | collective-permute-start | bytes 5013512 | tf_op jit(solution)/shard_map/ppermute | solution.py:624
  56.7 7.7 %collective-permute-start.11 = (f32[400,1024]{1,0:T(8,128)S(1)}, f32[400,1024]{1,0:T(8,128)S(1)}, u32[]{:S(2)}, u32[]{:S(2)}) collective-permute-start(f32[400,1024]{1,0:T(8,128)S(1)} %get-tuple-element.97), channel_id=1, source_target_pairs={{0,2},{4,6},{8,10},{12,14},{16,18},{20,22},{24,26},{28,30},{1,3},{... | collective-permute-start | bytes 4915208 | tf_op jit(solution)/shard_map/ppermute | solution.py:624
  58.1 17.0 %collective-permute-start.8 = (f32[400,512]{1,0:T(8,128)S(1)}, f32[400,512]{1,0:T(8,128)S(1)}, u32[]{:S(2)}, u32[]{:S(2)}) collective-permute-start(f32[400,512]{1,0:T(8,128)S(1)} %get-tuple-element.92), channel_id=1, source_target_pairs={{2,4},{6,8},{10,12},{14,16},{18,20},{22,24},{26,28},{30,0},{3,5},{... | collective-permute-start | bytes 2457608 | tf_op jit(solution)/shard_map/ppermute | solution.py:619
  59.4 20.1 %collective-permute-start.7 = (f32[400,256]{1,0:T(8,128)S(1)}, f32[400,256]{1,0:T(8,128)S(1)}, u32[]{:S(2)}, u32[]{:S(2)}) collective-permute-start(f32[400,256]{1,0:T(8,128)S(1)} %get-tuple-element.81), channel_id=1, source_target_pairs={{2,4},{6,8},{10,12},{14,16},{18,20},{22,24},{26,28},{30,0},{3,5},{... | collective-permute-start | bytes 1228808 | tf_op jit(solution)/shard_map/ppermute | solution.py:619
  82.7 4.3 %collective-permute-start.12 = (f32[32,400]{1,0:T(8,128)S(1)}, f32[32,400]{1,0:T(8,128)S(1)}, u32[]{:S(2)}, u32[]{:S(2)}) collective-permute-start(f32[32,400]{1,0:T(8,128)S(1)} %get-tuple-element.124.rest_0_), channel_id=1, source_target_pairs={{0,1},{1,0},{2,3},{3,2},{4,5},{5,4},{6,7},{7,6},{8,9},{9,8},{10,11... | collective-permute-start | bytes 153608 | tf_op jit(solution)/shard_map/ppermute | solution.py:641
  84.5 2.5 %copy-start.8 = (f32[32]{0:T(128)S(1)}, f32[32]{0:T(128)}, u32[]{:S(2)}) copy-start(f32[32]{0:T(128)} %param.16) | copy-start | bytes 388

commit v8 on v3

--- a/solution.py
+++ b/solution.py
@@ -461,17 +461,17 @@
         table = jnp.concatenate([hits] * 3, axis=1)
         t_rows = held_rows[...] + mul(table, slab, NT)
         probe_rows[...] = half_product(weight_rows[...], t_rows)
-        source_scores(number, probe_rows, left16, count_l, gp, weights)
+        rgrad[...], more = negatives(parts[0], query[...], query_rows[...], times_at(count_r, 0, size, at), number)
         w, s = weight[...], source[...]
         t = t_rows.T
         probe[...] = (w * t).astype(BF16)
-        rgrad[...], more = negatives(parts[0], query[...], query_rows[...], times_at(count_r, 0, size, at), number)
         q = held_q[...] + more
+        coef = -jax.nn.sigmoid(-jnp.sum(s * w * t, axis=0, keepdims=True))
+        to_src[0:depth, :], to_src[depth:, :] = split(coef * w * t + q * w, 2)
+        known = coef * s * t + q * s
+        source_scores(number, probe_rows, left16, count_l, gp, weights)
         p = gp[...]
-        coef = -jax.nn.sigmoid(-jnp.sum(s * w * t, axis=0, keepdims=True))
-        g_weight = coef * s * t + q * s + p * t
-        rel_out[...] = rel_in[...] + sum(mul(kind[...], part, NT) for part in split(g_weight, 2))
-        to_src[0:depth, :], to_src[depth:, :] = split(coef * w * t + q * w, 2)
+        rel_out[...] = rel_in[...] + sum(mul(kind[...], part, NT) for part in split(known + p * t, 2))
         here = dst[step : step + 1, :] >= at
         to_dst[0:depth, :], to_dst[depth:, :] = split(jnp.where(here, coef * w * s + p * w, 0.0), 2)
 

time: 88.1 us -> 88.1 us (level)
  no operation moved by 1% of the time
where the time goes in v8:
time: 88.1 us; the launch traced here: 87.8 us
  Pallas kernels  36.4 us (41%)
  starting transfers between devices  25.6 us (29%)
  waiting for transfers between devices  22.5 us (26%)
  local copies, waits for them, and re-layouts  2.21 us (3%)
  between operations  1 us (1%)
    pallas_call x15, Pallas kernels, call(): pl.pallas_call(kernel, out_shape=tuple(shapes), in_specs=[large if i in i...  36.4 us
    ppermute x2, waiting for transfers between devices, local(): state = lax.ppermute(lax.ppermute(state, 'blk', back), 'blk', skip)  16.1 us
    ppermute x2, starting transfers between devices, local(): lax.ppermute(right[:, at:at + size], 'blk', inside)  7.28 us
    ppermute x2, starting transfers between devices, local(): state = lax.ppermute(lax.ppermute(state, 'blk', back), 'blk', skip)  4.74 us
    ppermute x3, starting transfers between devices, local(): far = [lax.ppermute(piece, 'blk', across) for piece in far]  3.88 us
    ppermute x1, starting transfers between devices, local(): state_far = lax.ppermute(state_near, 'blk', skip).reshape(1, rows)  3.46 us
    ppermute x3, waiting for transfers between devices, local(): far = [lax.ppermute(piece, 'blk', across) for piece in far]  3.42 us
    ppermute x1, waiting for transfers between devices, local(): right_far = lax.ppermute(right, 'blk', across)  2.87 us
  transfers between devices with their start and end apart: 13, of which 7 were waited for; matrix products, arithmetic and copies ran while one was open for 2% of the time, Pallas kernels for 37%

profile of v8, /device:TPU:0, one launch (start us, length us, event | category | flops | bytes accessed | tf_op | source)
XLA Modules:
  0.0 87.8 jit_solution(3262659548623770980)
XLA Ops:
  0.6 0.0 copy-start.9
  0.6 0.0 copy-start
  0.7 0.0 copy-start.1
  0.7 0.0 copy-start.2
  0.7 0.0 copy-start.3
  0.7 0.0 copy-start.4
  0.7 0.0 copy-start.6
  0.7 0.0 copy-start.7
  0.7 1.6 %collective-permute-start.4 = (f32[400,2048]{1,0:T(8,128)}, f32[400,2048]{1,0:T(8,128)S(1)}, u32[]{:S(2)}, u32[]{:S(2)}) collective-permute-start(f32[400,2048]{1,0:T(8,128)} %bitcast.18), channel_id=1, source_target_pairs={{2,4},{6,8},{10,12},{14,16},{18,20},{22,24},{26,28},{30,0},{3,5},{... | collective-permute-start | bytes 9830408 | tf_op jit(solution)/shard_map/ppermute | solution.py:611
  2.3 2.2 %fusion = (f32[400,1024]{1,0:T(8,128)S(1)}, f32[400,1024]{1,0:T(8,128)S(1)}) fusion(f32[400,2048]{1,0:T(8,128)} %bitcast.19), kind=kLoop, calls=%fused_computation | loop fusion | bytes 6553600 | tf_op jit(solution)/shard_map/slice | solution.py:612
  4.4 0.0 copy-start.5
  4.4 5.9 %collective-permute-start.2 = (f32[400,1024]{1,0:T(8,128)S(1)}, f32[400,1024]{1,0:T(8,128)S(1)}, u32[]{:S(2)}, u32[]{:S(2)}) collective-permute-start(f32[400,1024]{1,0:T(8,128)S(1)} %get-tuple-element.125), channel_id=1, source_target_pairs={{0,2},{4,6},{8,10},{12,14},{16,18},{20,22},{24,26},{28,30},{1,3},{... | collective-permute-start | bytes 4915208 | tf_op jit(solution)/shard_map/ppermute | solution.py:612
  10.3 1.4 %collective-permute-start.1 = (f32[400,1024]{1,0:T(8,128)S(1)}, f32[400,1024]{1,0:T(8,128)S(1)}, u32[]{:S(2)}, u32[]{:S(2)}) collective-permute-start(f32[400,1024]{1,0:T(8,128)S(1)} %get-tuple-element.126), channel_id=1, source_target_pairs={{0,2},{4,6},{8,10},{12,14},{16,18},{20,22},{24,26},{28,30},{1,3},{... | collective-permute-start | bytes 4915208 | tf_op jit(solution)/shard_map/ppermute | solution.py:612
  11.7 0.0 copy-done.9
  11.8 0.1 collective-permute-start
  11.8 0.0 copy-done
  11.8 0.0 copy-done.1
  11.9 0.0 copy-done.2
  11.9 0.0 copy-done.3
  11.9 0.0 copy-done.4
  11.9 0.0 copy-done.6
  11.9 0.0 copy-done.7
  11.9 3.7 %prepare0.1 = (f32[400,256]{1,0:T(8,128)S(1)}, f32[400,256]{1,0:T(8,128)S(1)}, bf16[400,256]{1,0:T(8,128)(2,1)S(1)}, bf16[256,400]{1,0:T(8,128)(2,1)S(1)}, bf16[...) custom-call(f32[400,2048]{1,0:T(8,128)S(1)} %bitcast.9, ...), custom_call_target="tpu_custom_call" | custom-call | flops 1000000 | bytes 100000 | tf_op jit(solution)/shard_map/prepare0/pallas_call | solution.py:328
  15.6 0.1 collective-permute-done
  15.7 0.0 collective-permute-done.2.refs_16_
  15.7 0.0 collective-permute-done.1.refs_15_
  15.7 0.0 copy-done.5
  15.7 0.2 first_near.1
  15.9 1.3 %collective-permute-start.9 = (f32[400,1280]{1,0:T(8,128)S(1)}, f32[400,1280]{1,0:T(8,128)S(1)}, u32[]{:S(2)}, u32[]{:S(2)}) collective-permute-start(f32[400,1280]{1,0:T(8,128)S(1)} %get-tuple-element.93), channel_id=1, source_target_pairs={{2,4},{6,8},{10,12},{14,16},{18,20},{22,24},{26,28},{30,0},{3,5},{... | collective-permute-start | bytes 6144008 | tf_op jit(solution)/shard_map/ppermute | solution.py:619
  17.2 1.3 %collective-permute-start.5 = (f32[1,2048]{1,0:T(1,128)S(1)}, f32[1,2048]{1,0:T(1,128)S(1)}, u32[]{:S(2)}, u32[]{:S(2)}) collective-permute-start(f32[1,2048]{1,0:T(1,128)S(1)} %get-tuple-element.78), channel_id=1, source_target_pairs={{2,0},{6,4},{10,8},{14,12},{18,16},{22,20},{26,24},{30,28},{3,1},{... | collective-permute-start | bytes 24584 | tf_op jit(solution)/shard_map/ppermute | solution.py:620
  18.5 3.5 %collective-permute-start.3 = (f32[2048]{0:T(1024)S(1)}, f32[2048]{0:T(1024)S(1)}, u32[]{:S(2)}, u32[]{:S(2)}) collective-permute-start(f32[2048]{0:T(1024)S(1)} %collective-permute-done), channel_id=1, source_target_pairs={{0,4},{4,8},{8,12},{12,16},{16,20},{20,24},{24,28},{28,0},{1,5},{5... | collective-permute-start | bytes 24584 | tf_op jit(solution)/shard_map/ppermute | solution.py:614
  22.0 11.2 %collective-permute-done.5 = f32[1,2048]{1,0:T(1,128)S(1)} collective-permute-done((f32[1,2048]{1,0:T(1,128)S(1)}, f32[1,2048]{1,0:T(1,128)S(1)}, u32[]{:S(2)}, u32[]{:S(2)}) %collective-permute-start.5) | collective-permute-done | bytes 8224 | tf_op jit(solution)/shard_map/ppermute | solution.py:620
  33.2 3.4 %collective-permute-start.6 = (f32[1,2048]{1,0:T(1,128)S(1)}, f32[1,2048]{1,0:T(1,128)S(1)}, u32[]{:S(2)}, u32[]{:S(2)}) collective-permute-start(f32[1,2048]{1,0:T(1,128)S(1)} %collective-permute-done.5), channel_id=1, source_target_pairs={{0,4},{4,8},{8,12},{12,16},{16,20},{20,24},{24,28},{28,0},{1,5},{5... | collective-permute-start | bytes 24584 | tf_op jit(solution)/shard_map/ppermute | solution.py:620
  36.6 0.0 collective-permute-done.3
  36.6 4.9 %collective-permute-done.6.refs_17_.refs_1_.refs_9_ = f32[1,2048]{1,0:T(1,128)S(1)} collective-permute-done((f32[1,2048]{1,0:T(1,128)S(1)}, f32[1,2048]{1,0:T(1,128)S(1)}, u32[]{:S(2)}, u32[]{:S(2)}) %collective-permute-start.6) | collective-permute-done | bytes 8224 | tf_op jit(solution)/shard_map/ppermute | solution.py:620
  41.5 2.9 %collective-permute-done.4.refs_15_ = f32[400,2048]{1,0:T(8,128)S(1)} collective-permute-done((f32[400,2048]{1,0:T(8,128)}, f32[400,2048]{1,0:T(8,128)S(1)}, u32[]{:S(2)}, u32[]{:S(2)}) %collective-permute-start.4) | collective-permute-done | bytes 3276832 | tf_op jit(solution)/shard_map/ppermute | solution.py:611
  44.4 10.9 %first_far.1 = (f32[400,2048]{1,0:T(8,128)S(1)}, f32[1,2048]{1,0:T(1,128)S(1)}, f32[32,400]{1,0:T(8,128)S(1)}, f32[408,1024]{1,0:T(8,128)S(1)}, f32[400,1024]{1,0:T(8,128)S(1)}, /*index=5*/f32[1,2048]{1,0:T(1,128)}) custom-call(f32[400,2048]{1,0:T(8,128)S(1)} %bitcast.11, f32[1,2048]{1,0:T(1,128)S(1)} %get-tuple-element.75.refs_1_, ...), custom_call_target="tpu_custom_call", output_to_operand_aliasing={{0}: (16, {})} | custom-call | flops 1000000 | bytes 100000 | tf_op jit(solution)/shard_map/first_far/pallas_call | solution.py:328
  55.3 1.4 %collective-permute-start.10 = (f32[408,1024]{1,0:T(8,128)S(1)}, f32[408,1024]{1,0:T(8,128)S(1)}, u32[]{:S(2)}, u32[]{:S(2)}) collective-permute-start(f32[408,1024]{1,0:T(8,128)S(1)} %get-tuple-element.96), channel_id=1, source_target_pairs={{0,2},{4,6},{8,10},{12,14},{16,18},{20,22},{24,26},{28,30},{1,3},{... | collective-permute-start | bytes 5013512 | tf_op jit(solution)/shard_map/ppermute | solution.py:624
  56.7 1.4 %collective-permute-start.11 = (f32[400,1024]{1,0:T(8,128)S(1)}, f32[400,1024]{1,0:T(8,128)S(1)}, u32[]{:S(2)}, u32[]{:S(2)}) collective-permute-start(f32[400,1024]{1,0:T(8,128)S(1)} %get-tuple-element.97), channel_id=1, source_target_pairs={{0,2},{4,6},{8,10},{12,14},{16,18},{20,22},{24,26},{28,30},{1,3},{... | collective-permute-start | bytes 4915208 | tf_op jit(solution)/shard_map/ppermute | solution.py:624
  58.1 1.3 %collective-permute-start.8 = (f32[400,512]{1,0:T(8,128)S(1)}, f32[400,512]{1,0:T(8,128)S(1)}, u32[]{:S(2)}, u32[]{:S(2)}) collective-permute-start(f32[400,512]{1,0:T(8,128)S(1)} %get-tuple-element.92), channel_id=1, source_target_pairs={{2,4},{6,8},{10,12},{14,16},{18,20},{22,24},{26,28},{30,0},{3,5},{... | collective-permute-start | bytes 2457608 | tf_op jit(solution)/shard_map/ppermute | solution.py:619
  59.4 1.3 %collective-permute-start.7 = (f32[400,256]{1,0:T(8,128)S(1)}, f32[400,256]{1,0:T(8,128)S(1)}, u32[]{:S(2)}, u32[]{:S(2)}) collective-permute-start(f32[400,256]{1,0:T(8,128)S(1)} %get-tuple-element.81), channel_id=1, source_target_pairs={{2,4},{6,8},{10,12},{14,16},{18,20},{22,24},{26,28},{30,0},{3,5},{... | collective-permute-start | bytes 1228808 | tf_op jit(solution)/shard_map/ppermute | solution.py:619
  60.7 3.7 %prepare1.1 = (f32[400,256]{1,0:T(8,128)S(1)}, f32[400,256]{1,0:T(8,128)S(1)}, bf16[400,256]{1,0:T(8,128)(2,1)S(1)}, bf16[256,400]{1,0:T(8,128)(2,1)S(1)}, bf16[...) custom-call(f32[400,2048]{1,0:T(8,128)S(1)} %get-tuple-element.79.le, ...), custom_call_target="tpu_custom_call" | custom-call | flops 1000000 | bytes 100000 | tf_op jit(solution)/shard_map/prepare1/pallas_call | solution.py:328
  64.5 0.0 collective-permute-done.11.refs_16_
  64.5 0.0 collective-permute-done.10.refs_15_
  64.5 1.0 %last_near.1 = (f32[400,2048]{1,0:T(8,128)}, f32[1,2048]{1,0:T(1,128)S(1)}, f32[32,400]{1,0:T(8,128)S(1)}, f32[400,2048]{1,0:T(8,128)}, f32[1,2048]{1,0:T(1,128)}) custom-call(f32[400,2048]{1,0:T(8,128)S(1)} %get-tuple-element.79.left.refs_0_, f32[1,2048]{1,0:T(1,128)S(1)} %get-tuple-element.80.refs_1_, f32[1,2048]{1,0:T(1,128)S(1)} %bitcast.13, ...), custom_call_target="tpu_custom_call" | custom-call | flops 1000000 | bytes 100000 | tf_op jit(solution)/shard_map/last_near/pallas_call | solution.py:328
  65.5 0.9 collective-permute-done.9.refs_0_
  66.4 2.5 %last_piece0.1 = (f32[400,256]{1,0:T(8,128)S(1)}, f32[400,256]{1,0:T(8,128)S(1)}, f32[400,1280]{1,0:T(8,128)S(1)}) custom-call(f32[400,1280]{1,0:T(8,128)S(1)} %collective-permute-done.9.refs_0_, bf16[400,256]{1,0:T(8,128)(2,1)S(1)} %get-tuple-element.84.refs_6_.refs_1_.refs_3_, bf16[256,400]{1,0:T(8,128)(2,1)S(1)} %get-tuple-element.85.refs_7_.refs_2_.refs_4_, ...), custom_call_target="tpu_custom_call" | custom-call | flops 1000000 | bytes 100000 | tf_op jit(solution)/shard_map/last_piece0/pallas_call | solution.py:328
  68.9 2.1 %early_edges0.1 = (bf16[800,256]{1,0:T(8,128)(2,1)S(1)}, f32[256,400]{1,0:T(8,128)}) custom-call(f32[400,256]{1,0:T(8,128)S(1)} %get-tuple-element.82.refs_4_.refs_0_.refs_1_, f32[400,256]{1,0:T(8,128)S(1)} %get-tuple-element.83.refs_5_.refs_1_.refs_2_, f32[400,256]{1,0:T(8,128)S(1)} %get-tuple-element.99.refs_2_.refs_5_, ...), custom_call_target="tpu_custom_call" | custom-call | flops 1000000 | bytes 100000 | tf_op jit(solution)/shard_map/early_edges0/pallas_call | solution.py:328
  71.0 1.9 %early_right0.1 = (f32[400,2048]{1,0:T(8,128)}, f32[1,2048]{1,0:T(1,128)S(1)}) custom-call(f32[400,1280]{1,0:T(8,128)S(1)} %collective-permute-done.9.refs_0_, f32[1,2048]{1,0:T(1,128)S(1)} %collective-permute-done.6.refs_17_.refs_1_.refs_9_, f32[400,1280]{1,0:T(8,128)S(1)} %get-tuple-element.101.refs_2_, ...), custom_call_target="tpu_custom_call", output_to_operand_aliasing={{1}: (5, {}), {0}: (6, {})} | custom-call | flops 1000000 | bytes 100000 | tf_op jit(solution)/shard_map/early_right0/pallas_call | solution.py:328
  72.9 2.3 %collective-permute-done.8.refs_0_ = f32[400,512]{1,0:T(8,128)S(1)} collective-permute-done((f32[400,512]{1,0:T(8,128)S(1)}, f32[400,512]{1,0:T(8,128)S(1)}, u32[]{:S(2)}, u32[]{:S(2)}) %collective-permute-start.8) | collective-permute-done | bytes 819232 | tf_op jit(solution)/shard_map/ppermute | solution.py:619
  75.1 1.2 %last_piece1.1 = (f32[400,256]{1,0:T(8,128)S(1)}, f32[400,256]{1,0:T(8,128)S(1)}, f32[400,512]{1,0:T(8,128)S(1)}) custom-call(f32[400,512]{1,0:T(8,128)S(1)} %collective-permute-done.8.refs_0_, bf16[400,256]{1,0:T(8,128)(2,1)S(1)} %get-tuple-element.84.refs_6_.refs_1_.refs_3_, ...), custom_call_target="tpu_custom_call", output_to_operand_aliasing={{0}: (5, {}), {1}: (6, {})} | custom-call | flops 1000000 | bytes 100000 | tf_op jit(solution)/shard_map/last_piece1/pallas_call | solution.py:328
  76.4 1.3 %early_edges1.1 = (bf16[800,256]{1,0:T(8,128)(2,1)S(1)}, f32[256,400]{1,0:T(8,128)S(1)}) custom-call(f32[400,256]{1,0:T(8,128)S(1)} %get-tuple-element.82.refs_4_.refs_0_.refs_1_, f32[400,256]{1,0:T(8,128)S(1)} %get-tuple-element.83.refs_5_.refs_1_.refs_2_, f32[400,256]{1,0:T(8,128)S(1)} %get-tuple-element.105.refs_2_, ...), custom_call_target="tpu_custom_call" | custom-call | flops 1000000 | bytes 100000 | tf_op jit(solution)/shard_map/early_edges1/pallas_call | solution.py:328
  77.7 1.5 %early_right1.1 = (f32[400,2048]{1,0:T(8,128)}, f32[1,2048]{1,0:T(1,128)S(1)}) custom-call(f32[400,512]{1,0:T(8,128)S(1)} %collective-permute-done.8.refs_0_, f32[1,2048]{1,0:T(1,128)S(1)} %collective-permute-done.6.refs_17_.refs_1_.refs_9_, f32[400,512]{1,0:T(8,128)S(1)} %get-tuple-element.109.refs_2_, ...), custom_call_target="tpu_custom_call", output_to_operand_aliasing={{1}: (5, {}), {0}: (6, {})} | custom-call | flops 1000000 | bytes 100000 | tf_op jit(solution)/shard_map/early_right1/pallas_call | solution.py:328
  79.2 0.3 collective-permute-done.7.refs_0_.refs_8_
  79.5 2.3 %late_edges.1 = (f32[400,256]{1,0:T(8,128)S(1)}, bf16[800,256]{1,0:T(8,128)(2,1)S(1)}, bf16[800,256]{1,0:T(8,128)(2,1)S(1)}, f32[32,400]{1,0:T(8,128)S(1)}, bf16...) custom-call(f32[400,256]{1,0:T(8,128)S(1)} %collective-permute-done.7.refs_0_.refs_8_, ...), custom_call_target="tpu_custom_call", output_to_operand_aliasing={{3}: (14, {})} | custom-call | flops 1000000 | bytes 100000 | tf_op jit(solution)/shard_map/late_edges/pallas_call | solution.py:328
  81.8 0.9 %ahead_left.1 = (f32[400,768]{1,0:T(8,128)S(1)}, f32[32,400]{1,0:T(8,128)S(1)}) custom-call(f32[400,2048]{1,0:T(8,128)S(1)} %get-tuple-element.79.left.refs_0_, f32[1,2048]{1,0:T(1,128)S(1)} %get-tuple-element.80.refs_1_, bf16[800,256]{1,0:T(8,128)(2,1)S(1)} %get-tuple-element.113.refs_2_, ...), custom_call_target="tpu_custom_call", output_to_operand_aliasing={{1}: (7, {})} | custom-call | flops 1000000 | bytes 100000 | tf_op jit(solution)/shard_map/ahead_left/pallas_call | solution.py:328
  82.7 1.8 %collective-permute-start.12 = (f32[32,400]{1,0:T(8,128)S(1)}, f32[32,400]{1,0:T(8,128)S(1)}, u32[]{:S(2)}, u32[]{:S(2)}) collective-permute-start(f32[32,400]{1,0:T(8,128)S(1)} %get-tuple-element.124.rest_0_), channel_id=1, source_target_pairs={{0,1},{1,0},{2,3},{3,2},{4,5},{5,4},{6,7},{7,6},{8,9},{9,8},{10,11... | collective-permute-start | bytes 153608 | tf_op jit(solution)/shard_map/ppermute | solution.py:641
  84.5 0.0 copy-start.8
  84.5 2.4 %late_slabs.1 = (f32[400,2048]{1,0:T(8,128)}, f32[400,2048]{1,0:T(8,128)}) custom-call(f32[400,2048]{1,0:T(8,128)S(1)} %get-tuple-element.79.left.refs_0_, f32[1,2048]{1,0:T(1,128)S(1)} %get-tuple-element.80.refs_1_, bf16[800,256]{1,0:T(8,128)(2,1)S(1)} %get-tuple-element.113.refs_2_, ...), custom_call_target="tpu_custom_call", output_to_operand_aliasing={{0}: (13, {}), {1}: (14, {})} | custom-call | flops 1000000 | bytes 100000 | tf_op jit(solution)/shard_map/late_slabs/pallas_call | solution.py:328
  87.0 0.0 collective-permute-done.12.rest_1_
  87.0 0.0 copy-done.8
  87.0 0.7 relation_update.1
  (1 shorter events, 0.0 us)
Async XLA Ops:
  0.6 11.1 %copy-start.9 = (f32[2048]{0:T(1024)S(1)}, f32[2048]{0:T(1024)}, u32[]{:S(2)}) copy-start(f32[2048]{0:T(1024)} %param.14) | copy-start | bytes 24580
  0.6 11.2 %copy-start = (f32[2048,400]{0,1:T(8,128)S(1)}, f32[2048,400]{0,1:T(8,128)}, u32[]{:S(2)}) copy-start(f32[2048,400]{0,1:T(8,128)} %param.11) | copy-start | bytes 9830404
  0.7 11.2 %copy-start.1 = (f32[32,400]{1,0:T(8,128)S(1)}, f32[32,400]{1,0:T(8,128)}, u32[]{:S(2)}) copy-start(f32[32,400]{1,0:T(8,128)} %relations.5) | copy-start | bytes 153604
  0.7 11.2 %copy-start.2 = (s32[2,256]{1,0:T(2,128)S(1)}, s32[2,256]{1,0:T(2,128)}, u32[]{:S(2)}) copy-start(s32[2,256]{1,0:T(2,128)} %refs_10_.1) | copy-start | bytes 6148
  0.7 11.2 %copy-start.3 = (s32[2,1000]{1,0:T(2,128)S(1)}, s32[2,1000]{1,0:T(2,128)}, u32[]{:S(2)}) copy-start(s32[2,1000]{1,0:T(2,128)} %nsrc.3) | copy-start | bytes 24004
  0.7 11.2 %copy-start.4 = (s32[2,1000]{1,0:T(2,128)S(1)}, s32[2,1000]{1,0:T(2,128)}, u32[]{:S(2)}) copy-start(s32[2,1000]{1,0:T(2,128)} %ndst.3) | copy-start | bytes 24004
  0.7 11.2 %copy-start.6 = (s32[2,256]{1,0:T(2,128)S(1)}, s32[2,256]{1,0:T(2,128)}, u32[]{:S(2)}) copy-start(s32[2,256]{1,0:T(2,128)} %src.3) | copy-start | bytes 6148
  0.7 11.2 %copy-start.7 = (s32[2,256]{1,0:T(2,128)S(1)}, s32[2,256]{1,0:T(2,128)}, u32[]{:S(2)}) copy-start(s32[2,256]{1,0:T(2,128)} %rid.3) | copy-start | bytes 6148
  0.7 43.7 %collective-permute-start.4 = (f32[400,2048]{1,0:T(8,128)}, f32[400,2048]{1,0:T(8,128)S(1)}, u32[]{:S(2)}, u32[]{:S(2)}) collective-permute-start(f32[400,2048]{1,0:T(8,128)} %bitcast.18), channel_id=1, source_target_pairs={{2,4},{6,8},{10,12},{14,16},{18,20},{22,24},{26,28},{30,0},{3,5},{... | collective-permute-start | bytes 9830408 | tf_op jit(solution)/shard_map/ppermute | solution.py:611
  4.4 11.3 %copy-start.5 = (f32[2048]{0:T(1024)S(1)}, f32[2048]{0:T(1024)}, u32[]{:S(2)}) copy-start(f32[2048]{0:T(1024)} %param.12) | copy-start | bytes 24580
  4.4 11.3 %collective-permute-start.2 = (f32[400,1024]{1,0:T(8,128)S(1)}, f32[400,1024]{1,0:T(8,128)S(1)}, u32[]{:S(2)}, u32[]{:S(2)}) collective-permute-start(f32[400,1024]{1,0:T(8,128)S(1)} %get-tuple-element.125), channel_id=1, source_target_pairs={{0,2},{4,6},{8,10},{12,14},{16,18},{20,22},{24,26},{28,30},{1,3},{... | collective-permute-start | bytes 4915208 | tf_op jit(solution)/shard_map/ppermute | solution.py:612
  10.3 5.4 %collective-permute-start.1 = (f32[400,1024]{1,0:T(8,128)S(1)}, f32[400,1024]{1,0:T(8,128)S(1)}, u32[]{:S(2)}, u32[]{:S(2)}) collective-permute-start(f32[400,1024]{1,0:T(8,128)S(1)} %get-tuple-element.126), channel_id=1, source_target_pairs={{0,2},{4,6},{8,10},{12,14},{16,18},{20,22},{24,26},{28,30},{1,3},{... | collective-permute-start | bytes 4915208 | tf_op jit(solution)/shard_map/ppermute | solution.py:612
  11.8 4.0 %collective-permute-start = (f32[2048]{0:T(1024)S(1)}, f32[2048]{0:T(1024)S(1)}, u32[]{:S(2)}, u32[]{:S(2)}) collective-permute-start(f32[2048]{0:T(1024)S(1)} %copy-done.9), channel_id=1, source_target_pairs={{0,2},{4,6},{8,10},{12,14},{16,18},{20,22},{24,26},{28,30},{2,0},{... | collective-permute-start | bytes 24584 | tf_op jit(solution)/shard_map/ppermute | solution.py:613
  15.9 50.4 %collective-permute-start.9 = (f32[400,1280]{1,0:T(8,128)S(1)}, f32[400,1280]{1,0:T(8,128)S(1)}, u32[]{:S(2)}, u32[]{:S(2)}) collective-permute-start(f32[400,1280]{1,0:T(8,128)S(1)} %get-tuple-element.93), channel_id=1, source_target_pairs={{2,4},{6,8},{10,12},{14,16},{18,20},{22,24},{26,28},{30,0},{3,5},{... | collective-permute-start | bytes 6144008 | tf_op jit(solution)/shard_map/ppermute | solution.py:619
  17.2 15.9 %collective-permute-start.5 = (f32[1,2048]{1,0:T(1,128)S(1)}, f32[1,2048]{1,0:T(1,128)S(1)}, u32[]{:S(2)}, u32[]{:S(2)}) collective-permute-start(f32[1,2048]{1,0:T(1,128)S(1)} %get-tuple-element.78), channel_id=1, source_target_pairs={{2,0},{6,4},{10,8},{14,12},{18,16},{22,20},{26,24},{30,28},{3,1},{... | collective-permute-start | bytes 24584 | tf_op jit(solution)/shard_map/ppermute | solution.py:620
  18.5 18.1 %collective-permute-start.3 = (f32[2048]{0:T(1024)S(1)}, f32[2048]{0:T(1024)S(1)}, u32[]{:S(2)}, u32[]{:S(2)}) collective-permute-start(f32[2048]{0:T(1024)S(1)} %collective-permute-done), channel_id=1, source_target_pairs={{0,4},{4,8},{8,12},{12,16},{16,20},{20,24},{24,28},{28,0},{1,5},{5... | collective-permute-start | bytes 24584 | tf_op jit(solution)/shard_map/ppermute | solution.py:614
  33.2 8.4 %collective-permute-start.6 = (f32[1,2048]{1,0:T(1,128)S(1)}, f32[1,2048]{1,0:T(1,128)S(1)}, u32[]{:S(2)}, u32[]{:S(2)}) collective-permute-start(f32[1,2048]{1,0:T(1,128)S(1)} %collective-permute-done.5), channel_id=1, source_target_pairs={{0,4},{4,8},{8,12},{12,16},{16,20},{20,24},{24,28},{28,0},{1,5},{5... | collective-permute-start | bytes 24584 | tf_op jit(solution)/shard_map/ppermute | solution.py:620
  55.3 9.2 %collective-permute-start.10 = (f32[408,1024]{1,0:T(8,128)S(1)}, f32[408,1024]{1,0:T(8,128)S(1)}, u32[]{:S(2)}, u32[]{:S(2)}) collective-permute-start(f32[408,1024]{1,0:T(8,128)S(1)} %get-tuple-element.96), channel_id=1, source_target_pairs={{0,2},{4,6},{8,10},{12,14},{16,18},{20,22},{24,26},{28,30},{1,3},{... | collective-permute-start | bytes 5013512 | tf_op jit(solution)/shard_map/ppermute | solution.py:624
  56.7 7.7 %collective-permute-start.11 = (f32[400,1024]{1,0:T(8,128)S(1)}, f32[400,1024]{1,0:T(8,128)S(1)}, u32[]{:S(2)}, u32[]{:S(2)}) collective-permute-start(f32[400,1024]{1,0:T(8,128)S(1)} %get-tuple-element.97), channel_id=1, source_target_pairs={{0,2},{4,6},{8,10},{12,14},{16,18},{20,22},{24,26},{28,30},{1,3},{... | collective-permute-start | bytes 4915208 | tf_op jit(solution)/shard_map/ppermute | solution.py:624
  58.1 17.0 %collective-permute-start.8 = (f32[400,512]{1,0:T(8,128)S(1)}, f32[400,512]{1,0:T(8,128)S(1)}, u32[]{:S(2)}, u32[]{:S(2)}) collective-permute-start(f32[400,512]{1,0:T(8,128)S(1)} %get-tuple-element.92), channel_id=1, source_target_pairs={{2,4},{6,8},{10,12},{14,16},{18,20},{22,24},{26,28},{30,0},{3,5},{... | collective-permute-start | bytes 2457608 | tf_op jit(solution)/shard_map/ppermute | solution.py:619
  59.4 20.1 %collective-permute-start.7 = (f32[400,256]{1,0:T(8,128)S(1)}, f32[400,256]{1,0:T(8,128)S(1)}, u32[]{:S(2)}, u32[]{:S(2)}) collective-permute-start(f32[400,256]{1,0:T(8,128)S(1)} %get-tuple-element.81), channel_id=1, source_target_pairs={{2,4},{6,8},{10,12},{14,16},{18,20},{22,24},{26,28},{30,0},{3,5},{... | collective-permute-start | bytes 1228808 | tf_op jit(solution)/shard_map/ppermute | solution.py:619
  82.7 4.3 %collective-permute-start.12 = (f32[32,400]{1,0:T(8,128)S(1)}, f32[32,400]{1,0:T(8,128)S(1)}, u32[]{:S(2)}, u32[]{:S(2)}) collective-permute-start(f32[32,400]{1,0:T(8,128)S(1)} %get-tuple-element.124.rest_0_), channel_id=1, source_target_pairs={{0,1},{1,0},{2,3},{3,2},{4,5},{5,4},{6,7},{7,6},{8,9},{9,8},{10,11... | collective-permute-start | bytes 153608 | tf_op jit(solution)/shard_map/ppermute | solution.py:641
  84.5 2.5 %copy-start.8 = (f32[32]{0:T(128)S(1)}, f32[32]{0:T(128)}, u32[]{:S(2)}) copy-start(f32[32]{0:T(128)} %param.16) | copy-start | bytes 388

commit v9 on v3

--- a/solution.py
+++ b/solution.py
@@ -495,7 +495,7 @@
 
 
 def ahead_rows(rows):
-    return rows // 8 * 3
+    return rows // 4
 
 
 def first_along_rel():

time: 88.1 us -> 88.4 us (level)
  no operation moved by 1% of the time
where the time goes in v9:
time: 88.4 us; the launch traced here: 88 us
  Pallas kernels  36.5 us (41%)
  starting transfers between devices  25.8 us (29%)
  waiting for transfers between devices  22.5 us (25%)
  local copies, waits for them, and re-layouts  2.21 us (2%)
  between operations  1.02 us (1%)
    pallas_call x15, Pallas kernels, call(): pl.pallas_call(kernel, out_shape=tuple(shapes), in_specs=[large if i in i...  36.5 us
    ppermute x2, waiting for transfers between devices, local(): state = lax.ppermute(lax.ppermute(state, 'blk', back), 'blk', skip)  16.1 us
    ppermute x2, starting transfers between devices, local(): lax.ppermute(right[:, at:at + size], 'blk', inside)  7.28 us
    ppermute x2, starting transfers between devices, local(): state = lax.ppermute(lax.ppermute(state, 'blk', back), 'blk', skip)  4.74 us
    ppermute x3, starting transfers between devices, local(): far = [lax.ppermute(piece, 'blk', across) for piece in far]  3.88 us
    ppermute x1, starting transfers between devices, local(): state_far = lax.ppermute(state_near, 'blk', skip).reshape(1, rows)  3.46 us
    ppermute x3, waiting for transfers between devices, local(): far = [lax.ppermute(piece, 'blk', across) for piece in far]  3.42 us
    ppermute x1, waiting for transfers between devices, local(): right_far = lax.ppermute(right, 'blk', across)  2.87 us
  transfers between devices with their start and end apart: 13, of which 7 were waited for; matrix products, arithmetic and copies ran while one was open for 2% of the time, Pallas kernels for 37%

profile of v9, /device:TPU:0, one launch (start us, length us, event | category | flops | bytes accessed | tf_op | source)
XLA Modules:
  0.0 88.0 jit_solution(4148957112127346782)
XLA Ops:
  0.6 0.0 copy-start.9
  0.6 0.0 copy-start
  0.7 0.0 copy-start.1
  0.7 0.0 copy-start.2
  0.7 0.0 copy-start.3
  0.7 0.0 copy-start.4
  0.7 0.0 copy-start.6
  0.7 0.0 copy-start.7
  0.7 1.6 %collective-permute-start.4 = (f32[400,2048]{1,0:T(8,128)}, f32[400,2048]{1,0:T(8,128)S(1)}, u32[]{:S(2)}, u32[]{:S(2)}) collective-permute-start(f32[400,2048]{1,0:T(8,128)} %bitcast.18), channel_id=1, source_target_pairs={{2,4},{6,8},{10,12},{14,16},{18,20},{22,24},{26,28},{30,0},{3,5},{... | collective-permute-start | bytes 9830408 | tf_op jit(solution)/shard_map/ppermute | solution.py:611
  2.3 2.2 %fusion = (f32[400,1024]{1,0:T(8,128)S(1)}, f32[400,1024]{1,0:T(8,128)S(1)}) fusion(f32[400,2048]{1,0:T(8,128)} %bitcast.19), kind=kLoop, calls=%fused_computation | loop fusion | bytes 6553600 | tf_op jit(solution)/shard_map/slice | solution.py:612
  4.4 0.0 copy-start.5
  4.4 5.9 %collective-permute-start.2 = (f32[400,1024]{1,0:T(8,128)S(1)}, f32[400,1024]{1,0:T(8,128)S(1)}, u32[]{:S(2)}, u32[]{:S(2)}) collective-permute-start(f32[400,1024]{1,0:T(8,128)S(1)} %get-tuple-element.125), channel_id=1, source_target_pairs={{0,2},{4,6},{8,10},{12,14},{16,18},{20,22},{24,26},{28,30},{1,3},{... | collective-permute-start | bytes 4915208 | tf_op jit(solution)/shard_map/ppermute | solution.py:612
  10.3 1.4 %collective-permute-start.1 = (f32[400,1024]{1,0:T(8,128)S(1)}, f32[400,1024]{1,0:T(8,128)S(1)}, u32[]{:S(2)}, u32[]{:S(2)}) collective-permute-start(f32[400,1024]{1,0:T(8,128)S(1)} %get-tuple-element.126), channel_id=1, source_target_pairs={{0,2},{4,6},{8,10},{12,14},{16,18},{20,22},{24,26},{28,30},{1,3},{... | collective-permute-start | bytes 4915208 | tf_op jit(solution)/shard_map/ppermute | solution.py:612
  11.7 0.0 copy-done.9
  11.8 0.1 collective-permute-start
  11.8 0.0 copy-done
  11.8 0.0 copy-done.1
  11.9 0.0 copy-done.2
  11.9 0.0 copy-done.3
  11.9 0.0 copy-done.4
  11.9 0.0 copy-done.6
  11.9 0.0 copy-done.7
  11.9 3.7 %prepare0.1 = (f32[400,256]{1,0:T(8,128)S(1)}, f32[400,256]{1,0:T(8,128)S(1)}, bf16[400,256]{1,0:T(8,128)(2,1)S(1)}, bf16[256,400]{1,0:T(8,128)(2,1)S(1)}, bf16[...) custom-call(f32[400,2048]{1,0:T(8,128)S(1)} %bitcast.9, ...), custom_call_target="tpu_custom_call" | custom-call | flops 1000000 | bytes 100000 | tf_op jit(solution)/shard_map/prepare0/pallas_call | solution.py:328
  15.6 0.1 collective-permute-done
  15.7 0.0 collective-permute-done.2.refs_16_
  15.7 0.0 collective-permute-done.1.refs_15_
  15.7 0.0 copy-done.5
  15.7 0.2 first_near.1
  15.9 1.3 %collective-permute-start.9 = (f32[400,1280]{1,0:T(8,128)S(1)}, f32[400,1280]{1,0:T(8,128)S(1)}, u32[]{:S(2)}, u32[]{:S(2)}) collective-permute-start(f32[400,1280]{1,0:T(8,128)S(1)} %get-tuple-element.93), channel_id=1, source_target_pairs={{2,4},{6,8},{10,12},{14,16},{18,20},{22,24},{26,28},{30,0},{3,5},{... | collective-permute-start | bytes 6144008 | tf_op jit(solution)/shard_map/ppermute | solution.py:619
  17.2 1.3 %collective-permute-start.5 = (f32[1,2048]{1,0:T(1,128)S(1)}, f32[1,2048]{1,0:T(1,128)S(1)}, u32[]{:S(2)}, u32[]{:S(2)}) collective-permute-start(f32[1,2048]{1,0:T(1,128)S(1)} %get-tuple-element.78), channel_id=1, source_target_pairs={{2,0},{6,4},{10,8},{14,12},{18,16},{22,20},{26,24},{30,28},{3,1},{... | collective-permute-start | bytes 24584 | tf_op jit(solution)/shard_map/ppermute | solution.py:620
  18.5 3.5 %collective-permute-start.3 = (f32[2048]{0:T(1024)S(1)}, f32[2048]{0:T(1024)S(1)}, u32[]{:S(2)}, u32[]{:S(2)}) collective-permute-start(f32[2048]{0:T(1024)S(1)} %collective-permute-done), channel_id=1, source_target_pairs={{0,4},{4,8},{8,12},{12,16},{16,20},{20,24},{24,28},{28,0},{1,5},{5... | collective-permute-start | bytes 24584 | tf_op jit(solution)/shard_map/ppermute | solution.py:614
  22.0 11.2 %collective-permute-done.5 = f32[1,2048]{1,0:T(1,128)S(1)} collective-permute-done((f32[1,2048]{1,0:T(1,128)S(1)}, f32[1,2048]{1,0:T(1,128)S(1)}, u32[]{:S(2)}, u32[]{:S(2)}) %collective-permute-start.5) | collective-permute-done | bytes 8224 | tf_op jit(solution)/shard_map/ppermute | solution.py:620
  33.2 3.4 %collective-permute-start.6 = (f32[1,2048]{1,0:T(1,128)S(1)}, f32[1,2048]{1,0:T(1,128)S(1)}, u32[]{:S(2)}, u32[]{:S(2)}) collective-permute-start(f32[1,2048]{1,0:T(1,128)S(1)} %collective-permute-done.5), channel_id=1, source_target_pairs={{0,4},{4,8},{8,12},{12,16},{16,20},{20,24},{24,28},{28,0},{1,5},{5... | collective-permute-start | bytes 24584 | tf_op jit(solution)/shard_map/ppermute | solution.py:620
  36.6 0.0 collective-permute-done.3
  36.6 4.9 %collective-permute-done.6.refs_17_.refs_1_.refs_9_ = f32[1,2048]{1,0:T(1,128)S(1)} collective-permute-done((f32[1,2048]{1,0:T(1,128)S(1)}, f32[1,2048]{1,0:T(1,128)S(1)}, u32[]{:S(2)}, u32[]{:S(2)}) %collective-permute-start.6) | collective-permute-done | bytes 8224 | tf_op jit(solution)/shard_map/ppermute | solution.py:620
  41.5 2.9 %collective-permute-done.4.refs_15_ = f32[400,2048]{1,0:T(8,128)S(1)} collective-permute-done((f32[400,2048]{1,0:T(8,128)}, f32[400,2048]{1,0:T(8,128)S(1)}, u32[]{:S(2)}, u32[]{:S(2)}) %collective-permute-start.4) | collective-permute-done | bytes 3276832 | tf_op jit(solution)/shard_map/ppermute | solution.py:611
  44.4 10.9 %first_far.1 = (f32[400,2048]{1,0:T(8,128)S(1)}, f32[1,2048]{1,0:T(1,128)S(1)}, f32[32,400]{1,0:T(8,128)S(1)}, f32[408,1024]{1,0:T(8,128)S(1)}, f32[400,1024]{1,0:T(8,128)S(1)}, /*index=5*/f32[1,2048]{1,0:T(1,128)}) custom-call(f32[400,2048]{1,0:T(8,128)S(1)} %bitcast.11, f32[1,2048]{1,0:T(1,128)S(1)} %get-tuple-element.75.refs_1_, ...), custom_call_target="tpu_custom_call", output_to_operand_aliasing={{0}: (16, {})} | custom-call | flops 1000000 | bytes 100000 | tf_op jit(solution)/shard_map/first_far/pallas_call | solution.py:328
  55.3 1.4 %collective-permute-start.10 = (f32[408,1024]{1,0:T(8,128)S(1)}, f32[408,1024]{1,0:T(8,128)S(1)}, u32[]{:S(2)}, u32[]{:S(2)}) collective-permute-start(f32[408,1024]{1,0:T(8,128)S(1)} %get-tuple-element.96), channel_id=1, source_target_pairs={{0,2},{4,6},{8,10},{12,14},{16,18},{20,22},{24,26},{28,30},{1,3},{... | collective-permute-start | bytes 5013512 | tf_op jit(solution)/shard_map/ppermute | solution.py:624
  56.7 1.4 %collective-permute-start.11 = (f32[400,1024]{1,0:T(8,128)S(1)}, f32[400,1024]{1,0:T(8,128)S(1)}, u32[]{:S(2)}, u32[]{:S(2)}) collective-permute-start(f32[400,1024]{1,0:T(8,128)S(1)} %get-tuple-element.97), channel_id=1, source_target_pairs={{0,2},{4,6},{8,10},{12,14},{16,18},{20,22},{24,26},{28,30},{1,3},{... | collective-permute-start | bytes 4915208 | tf_op jit(solution)/shard_map/ppermute | solution.py:624
  58.1 1.3 %collective-permute-start.8 = (f32[400,512]{1,0:T(8,128)S(1)}, f32[400,512]{1,0:T(8,128)S(1)}, u32[]{:S(2)}, u32[]{:S(2)}) collective-permute-start(f32[400,512]{1,0:T(8,128)S(1)} %get-tuple-element.92), channel_id=1, source_target_pairs={{2,4},{6,8},{10,12},{14,16},{18,20},{22,24},{26,28},{30,0},{3,5},{... | collective-permute-start | bytes 2457608 | tf_op jit(solution)/shard_map/ppermute | solution.py:619
  59.4 1.3 %collective-permute-start.7 = (f32[400,256]{1,0:T(8,128)S(1)}, f32[400,256]{1,0:T(8,128)S(1)}, u32[]{:S(2)}, u32[]{:S(2)}) collective-permute-start(f32[400,256]{1,0:T(8,128)S(1)} %get-tuple-element.81), channel_id=1, source_target_pairs={{2,4},{6,8},{10,12},{14,16},{18,20},{22,24},{26,28},{30,0},{3,5},{... | collective-permute-start | bytes 1228808 | tf_op jit(solution)/shard_map/ppermute | solution.py:619
  60.7 3.7 %prepare1.1 = (f32[400,256]{1,0:T(8,128)S(1)}, f32[400,256]{1,0:T(8,128)S(1)}, bf16[400,256]{1,0:T(8,128)(2,1)S(1)}, bf16[256,400]{1,0:T(8,128)(2,1)S(1)}, bf16[...) custom-call(f32[400,2048]{1,0:T(8,128)S(1)} %get-tuple-element.79.le, ...), custom_call_target="tpu_custom_call" | custom-call | flops 1000000 | bytes 100000 | tf_op jit(solution)/shard_map/prepare1/pallas_call | solution.py:328
  64.5 0.0 collective-permute-done.11.refs_16_
  64.5 0.0 collective-permute-done.10.refs_15_
  64.5 1.0 %last_near.1 = (f32[400,2048]{1,0:T(8,128)}, f32[1,2048]{1,0:T(1,128)S(1)}, f32[32,400]{1,0:T(8,128)S(1)}, f32[400,2048]{1,0:T(8,128)}, f32[1,2048]{1,0:T(1,128)}) custom-call(f32[400,2048]{1,0:T(8,128)S(1)} %get-tuple-element.79.left.refs_0_, f32[1,2048]{1,0:T(1,128)S(1)} %get-tuple-element.80.refs_1_, f32[1,2048]{1,0:T(1,128)S(1)} %bitcast.13, ...), custom_call_target="tpu_custom_call" | custom-call | flops 1000000 | bytes 100000 | tf_op jit(solution)/shard_map/last_near/pallas_call | solution.py:328
  65.5 0.9 collective-permute-done.9.refs_0_
  66.4 2.5 %last_piece0.1 = (f32[400,256]{1,0:T(8,128)S(1)}, f32[400,256]{1,0:T(8,128)S(1)}, f32[400,1280]{1,0:T(8,128)S(1)}) custom-call(f32[400,1280]{1,0:T(8,128)S(1)} %collective-permute-done.9.refs_0_, bf16[400,256]{1,0:T(8,128)(2,1)S(1)} %get-tuple-element.84.refs_6_.refs_1_.refs_3_, bf16[256,400]{1,0:T(8,128)(2,1)S(1)} %get-tuple-element.85.refs_7_.refs_2_.refs_4_, ...), custom_call_target="tpu_custom_call" | custom-call | flops 1000000 | bytes 100000 | tf_op jit(solution)/shard_map/last_piece0/pallas_call | solution.py:328
  68.9 2.1 %early_edges0.1 = (bf16[800,256]{1,0:T(8,128)(2,1)S(1)}, f32[256,400]{1,0:T(8,128)}) custom-call(f32[400,256]{1,0:T(8,128)S(1)} %get-tuple-element.82.refs_4_.refs_0_.refs_1_, f32[400,256]{1,0:T(8,128)S(1)} %get-tuple-element.83.refs_5_.refs_1_.refs_2_, f32[400,256]{1,0:T(8,128)S(1)} %get-tuple-element.99.refs_2_.refs_5_, ...), custom_call_target="tpu_custom_call" | custom-call | flops 1000000 | bytes 100000 | tf_op jit(solution)/shard_map/early_edges0/pallas_call | solution.py:328
  71.0 1.9 %early_right0.1 = (f32[400,2048]{1,0:T(8,128)}, f32[1,2048]{1,0:T(1,128)S(1)}) custom-call(f32[400,1280]{1,0:T(8,128)S(1)} %collective-permute-done.9.refs_0_, f32[1,2048]{1,0:T(1,128)S(1)} %collective-permute-done.6.refs_17_.refs_1_.refs_9_, f32[400,1280]{1,0:T(8,128)S(1)} %get-tuple-element.101.refs_2_, ...), custom_call_target="tpu_custom_call", output_to_operand_aliasing={{1}: (5, {}), {0}: (6, {})} | custom-call | flops 1000000 | bytes 100000 | tf_op jit(solution)/shard_map/early_right0/pallas_call | solution.py:328
  72.9 2.3 %collective-permute-done.8.refs_0_ = f32[400,512]{1,0:T(8,128)S(1)} collective-permute-done((f32[400,512]{1,0:T(8,128)S(1)}, f32[400,512]{1,0:T(8,128)S(1)}, u32[]{:S(2)}, u32[]{:S(2)}) %collective-permute-start.8) | collective-permute-done | bytes 819232 | tf_op jit(solution)/shard_map/ppermute | solution.py:619
  75.1 1.2 %last_piece1.1 = (f32[400,256]{1,0:T(8,128)S(1)}, f32[400,256]{1,0:T(8,128)S(1)}, f32[400,512]{1,0:T(8,128)S(1)}) custom-call(f32[400,512]{1,0:T(8,128)S(1)} %collective-permute-done.8.refs_0_, bf16[400,256]{1,0:T(8,128)(2,1)S(1)} %get-tuple-element.84.refs_6_.refs_1_.refs_3_, ...), custom_call_target="tpu_custom_call", output_to_operand_aliasing={{0}: (5, {}), {1}: (6, {})} | custom-call | flops 1000000 | bytes 100000 | tf_op jit(solution)/shard_map/last_piece1/pallas_call | solution.py:328
  76.4 1.3 %early_edges1.1 = (bf16[800,256]{1,0:T(8,128)(2,1)S(1)}, f32[256,400]{1,0:T(8,128)S(1)}) custom-call(f32[400,256]{1,0:T(8,128)S(1)} %get-tuple-element.82.refs_4_.refs_0_.refs_1_, f32[400,256]{1,0:T(8,128)S(1)} %get-tuple-element.83.refs_5_.refs_1_.refs_2_, f32[400,256]{1,0:T(8,128)S(1)} %get-tuple-element.105.refs_2_, ...), custom_call_target="tpu_custom_call" | custom-call | flops 1000000 | bytes 100000 | tf_op jit(solution)/shard_map/early_edges1/pallas_call | solution.py:328
  77.7 1.5 %early_right1.1 = (f32[400,2048]{1,0:T(8,128)}, f32[1,2048]{1,0:T(1,128)S(1)}) custom-call(f32[400,512]{1,0:T(8,128)S(1)} %collective-permute-done.8.refs_0_, f32[1,2048]{1,0:T(1,128)S(1)} %collective-permute-done.6.refs_17_.refs_1_.refs_9_, f32[400,512]{1,0:T(8,128)S(1)} %get-tuple-element.109.refs_2_, ...), custom_call_target="tpu_custom_call", output_to_operand_aliasing={{1}: (5, {}), {0}: (6, {})} | custom-call | flops 1000000 | bytes 100000 | tf_op jit(solution)/shard_map/early_right1/pallas_call | solution.py:328
  79.2 0.3 collective-permute-done.7.refs_0_.refs_8_
  79.5 2.3 %late_edges.1 = (f32[400,256]{1,0:T(8,128)S(1)}, bf16[800,256]{1,0:T(8,128)(2,1)S(1)}, bf16[800,256]{1,0:T(8,128)(2,1)S(1)}, f32[32,400]{1,0:T(8,128)S(1)}, bf16...) custom-call(f32[400,256]{1,0:T(8,128)S(1)} %collective-permute-done.7.refs_0_.refs_8_, ...), custom_call_target="tpu_custom_call", output_to_operand_aliasing={{3}: (14, {})} | custom-call | flops 1000000 | bytes 100000 | tf_op jit(solution)/shard_map/late_edges/pallas_call | solution.py:328
  81.8 0.7 ahead_left.1
  82.5 2.0 %collective-permute-start.12 = (f32[32,400]{1,0:T(8,128)S(1)}, f32[32,400]{1,0:T(8,128)S(1)}, u32[]{:S(2)}, u32[]{:S(2)}) collective-permute-start(f32[32,400]{1,0:T(8,128)S(1)} %get-tuple-element.124.rest_0_), channel_id=1, source_target_pairs={{0,1},{1,0},{2,3},{3,2},{4,5},{5,4},{6,7},{7,6},{8,9},{9,8},{10,11... | collective-permute-start | bytes 153608 | tf_op jit(solution)/shard_map/ppermute | solution.py:641
  84.5 0.0 copy-start.8
  84.5 2.8 %late_slabs.1 = (f32[400,2048]{1,0:T(8,128)}, f32[400,2048]{1,0:T(8,128)}) custom-call(f32[400,2048]{1,0:T(8,128)S(1)} %get-tuple-element.79.left.refs_0_, f32[1,2048]{1,0:T(1,128)S(1)} %get-tuple-element.80.refs_1_, bf16[800,256]{1,0:T(8,128)(2,1)S(1)} %get-tuple-element.113.refs_2_, ...), custom_call_target="tpu_custom_call", output_to_operand_aliasing={{0}: (13, {}), {1}: (14, {})} | custom-call | flops 1000000 | bytes 100000 | tf_op jit(solution)/shard_map/late_slabs/pallas_call | solution.py:328
  87.3 0.0 collective-permute-done.12.rest_1_
  87.3 0.0 copy-done.8
  87.3 0.7 relation_update.1
  (1 shorter events, 0.0 us)
Async XLA Ops:
  0.6 11.1 %copy-start.9 = (f32[2048]{0:T(1024)S(1)}, f32[2048]{0:T(1024)}, u32[]{:S(2)}) copy-start(f32[2048]{0:T(1024)} %param.14) | copy-start | bytes 24580
  0.6 11.2 %copy-start = (f32[2048,400]{0,1:T(8,128)S(1)}, f32[2048,400]{0,1:T(8,128)}, u32[]{:S(2)}) copy-start(f32[2048,400]{0,1:T(8,128)} %param.11) | copy-start | bytes 9830404
  0.7 11.2 %copy-start.1 = (f32[32,400]{1,0:T(8,128)S(1)}, f32[32,400]{1,0:T(8,128)}, u32[]{:S(2)}) copy-start(f32[32,400]{1,0:T(8,128)} %relations.5) | copy-start | bytes 153604
  0.7 11.2 %copy-start.2 = (s32[2,256]{1,0:T(2,128)S(1)}, s32[2,256]{1,0:T(2,128)}, u32[]{:S(2)}) copy-start(s32[2,256]{1,0:T(2,128)} %refs_10_.1) | copy-start | bytes 6148
  0.7 11.2 %copy-start.3 = (s32[2,1000]{1,0:T(2,128)S(1)}, s32[2,1000]{1,0:T(2,128)}, u32[]{:S(2)}) copy-start(s32[2,1000]{1,0:T(2,128)} %nsrc.3) | copy-start | bytes 24004
  0.7 11.2 %copy-start.4 = (s32[2,1000]{1,0:T(2,128)S(1)}, s32[2,1000]{1,0:T(2,128)}, u32[]{:S(2)}) copy-start(s32[2,1000]{1,0:T(2,128)} %ndst.3) | copy-start | bytes 24004
  0.7 11.2 %copy-start.6 = (s32[2,256]{1,0:T(2,128)S(1)}, s32[2,256]{1,0:T(2,128)}, u32[]{:S(2)}) copy-start(s32[2,256]{1,0:T(2,128)} %src.3) | copy-start | bytes 6148
  0.7 11.2 %copy-start.7 = (s32[2,256]{1,0:T(2,128)S(1)}, s32[2,256]{1,0:T(2,128)}, u32[]{:S(2)}) copy-start(s32[2,256]{1,0:T(2,128)} %rid.3) | copy-start | bytes 6148
  0.7 43.7 %collective-permute-start.4 = (f32[400,2048]{1,0:T(8,128)}, f32[400,2048]{1,0:T(8,128)S(1)}, u32[]{:S(2)}, u32[]{:S(2)}) collective-permute-start(f32[400,2048]{1,0:T(8,128)} %bitcast.18), channel_id=1, source_target_pairs={{2,4},{6,8},{10,12},{14,16},{18,20},{22,24},{26,28},{30,0},{3,5},{... | collective-permute-start | bytes 9830408 | tf_op jit(solution)/shard_map/ppermute | solution.py:611
  4.4 11.3 %copy-start.5 = (f32[2048]{0:T(1024)S(1)}, f32[2048]{0:T(1024)}, u32[]{:S(2)}) copy-start(f32[2048]{0:T(1024)} %param.12) | copy-start | bytes 24580
  4.4 11.3 %collective-permute-start.2 = (f32[400,1024]{1,0:T(8,128)S(1)}, f32[400,1024]{1,0:T(8,128)S(1)}, u32[]{:S(2)}, u32[]{:S(2)}) collective-permute-start(f32[400,1024]{1,0:T(8,128)S(1)} %get-tuple-element.125), channel_id=1, source_target_pairs={{0,2},{4,6},{8,10},{12,14},{16,18},{20,22},{24,26},{28,30},{1,3},{... | collective-permute-start | bytes 4915208 | tf_op jit(solution)/shard_map/ppermute | solution.py:612
  10.3 5.4 %collective-permute-start.1 = (f32[400,1024]{1,0:T(8,128)S(1)}, f32[400,1024]{1,0:T(8,128)S(1)}, u32[]{:S(2)}, u32[]{:S(2)}) collective-permute-start(f32[400,1024]{1,0:T(8,128)S(1)} %get-tuple-element.126), channel_id=1, source_target_pairs={{0,2},{4,6},{8,10},{12,14},{16,18},{20,22},{24,26},{28,30},{1,3},{... | collective-permute-start | bytes 4915208 | tf_op jit(solution)/shard_map/ppermute | solution.py:612
  11.8 4.0 %collective-permute-start = (f32[2048]{0:T(1024)S(1)}, f32[2048]{0:T(1024)S(1)}, u32[]{:S(2)}, u32[]{:S(2)}) collective-permute-start(f32[2048]{0:T(1024)S(1)} %copy-done.9), channel_id=1, source_target_pairs={{0,2},{4,6},{8,10},{12,14},{16,18},{20,22},{24,26},{28,30},{2,0},{... | collective-permute-start | bytes 24584 | tf_op jit(solution)/shard_map/ppermute | solution.py:613
  15.9 50.4 %collective-permute-start.9 = (f32[400,1280]{1,0:T(8,128)S(1)}, f32[400,1280]{1,0:T(8,128)S(1)}, u32[]{:S(2)}, u32[]{:S(2)}) collective-permute-start(f32[400,1280]{1,0:T(8,128)S(1)} %get-tuple-element.93), channel_id=1, source_target_pairs={{2,4},{6,8},{10,12},{14,16},{18,20},{22,24},{26,28},{30,0},{3,5},{... | collective-permute-start | bytes 6144008 | tf_op jit(solution)/shard_map/ppermute | solution.py:619
  17.2 15.9 %collective-permute-start.5 = (f32[1,2048]{1,0:T(1,128)S(1)}, f32[1,2048]{1,0:T(1,128)S(1)}, u32[]{:S(2)}, u32[]{:S(2)}) collective-permute-start(f32[1,2048]{1,0:T(1,128)S(1)} %get-tuple-element.78), channel_id=1, source_target_pairs={{2,0},{6,4},{10,8},{14,12},{18,16},{22,20},{26,24},{30,28},{3,1},{... | collective-permute-start | bytes 24584 | tf_op jit(solution)/shard_map/ppermute | solution.py:620
  18.5 18.1 %collective-permute-start.3 = (f32[2048]{0:T(1024)S(1)}, f32[2048]{0:T(1024)S(1)}, u32[]{:S(2)}, u32[]{:S(2)}) collective-permute-start(f32[2048]{0:T(1024)S(1)} %collective-permute-done), channel_id=1, source_target_pairs={{0,4},{4,8},{8,12},{12,16},{16,20},{20,24},{24,28},{28,0},{1,5},{5... | collective-permute-start | bytes 24584 | tf_op jit(solution)/shard_map/ppermute | solution.py:614
  33.2 8.4 %collective-permute-start.6 = (f32[1,2048]{1,0:T(1,128)S(1)}, f32[1,2048]{1,0:T(1,128)S(1)}, u32[]{:S(2)}, u32[]{:S(2)}) collective-permute-start(f32[1,2048]{1,0:T(1,128)S(1)} %collective-permute-done.5), channel_id=1, source_target_pairs={{0,4},{4,8},{8,12},{12,16},{16,20},{20,24},{24,28},{28,0},{1,5},{5... | collective-permute-start | bytes 24584 | tf_op jit(solution)/shard_map/ppermute | solution.py:620
  55.3 9.2 %collective-permute-start.10 = (f32[408,1024]{1,0:T(8,128)S(1)}, f32[408,1024]{1,0:T(8,128)S(1)}, u32[]{:S(2)}, u32[]{:S(2)}) collective-permute-start(f32[408,1024]{1,0:T(8,128)S(1)} %get-tuple-element.96), channel_id=1, source_target_pairs={{0,2},{4,6},{8,10},{12,14},{16,18},{20,22},{24,26},{28,30},{1,3},{... | collective-permute-start | bytes 5013512 | tf_op jit(solution)/shard_map/ppermute | solution.py:624
  56.7 7.7 %collective-permute-start.11 = (f32[400,1024]{1,0:T(8,128)S(1)}, f32[400,1024]{1,0:T(8,128)S(1)}, u32[]{:S(2)}, u32[]{:S(2)}) collective-permute-start(f32[400,1024]{1,0:T(8,128)S(1)} %get-tuple-element.97), channel_id=1, source_target_pairs={{0,2},{4,6},{8,10},{12,14},{16,18},{20,22},{24,26},{28,30},{1,3},{... | collective-permute-start | bytes 4915208 | tf_op jit(solution)/shard_map/ppermute | solution.py:624
  58.1 17.0 %collective-permute-start.8 = (f32[400,512]{1,0:T(8,128)S(1)}, f32[400,512]{1,0:T(8,128)S(1)}, u32[]{:S(2)}, u32[]{:S(2)}) collective-permute-start(f32[400,512]{1,0:T(8,128)S(1)} %get-tuple-element.92), channel_id=1, source_target_pairs={{2,4},{6,8},{10,12},{14,16},{18,20},{22,24},{26,28},{30,0},{3,5},{... | collective-permute-start | bytes 2457608 | tf_op jit(solution)/shard_map/ppermute | solution.py:619
  59.4 20.1 %collective-permute-start.7 = (f32[400,256]{1,0:T(8,128)S(1)}, f32[400,256]{1,0:T(8,128)S(1)}, u32[]{:S(2)}, u32[]{:S(2)}) collective-permute-start(f32[400,256]{1,0:T(8,128)S(1)} %get-tuple-element.81), channel_id=1, source_target_pairs={{2,4},{6,8},{10,12},{14,16},{18,20},{22,24},{26,28},{30,0},{3,5},{... | collective-permute-start | bytes 1228808 | tf_op jit(solution)/shard_map/ppermute | solution.py:619
  82.5 4.8 %collective-permute-start.12 = (f32[32,400]{1,0:T(8,128)S(1)}, f32[32,400]{1,0:T(8,128)S(1)}, u32[]{:S(2)}, u32[]{:S(2)}) collective-permute-start(f32[32,400]{1,0:T(8,128)S(1)} %get-tuple-element.124.rest_0_), channel_id=1, source_target_pairs={{0,1},{1,0},{2,3},{3,2},{4,5},{5,4},{6,7},{7,6},{8,9},{9,8},{10,11... | collective-permute-start | bytes 153608 | tf_op jit(solution)/shard_map/ppermute | solution.py:641
  84.5 2.8 %copy-start.8 = (f32[32]{0:T(128)S(1)}, f32[32]{0:T(128)}, u32[]{:S(2)}) copy-start(f32[32]{0:T(128)} %param.16) | copy-start | bytes 388
